TPU v7x, 256 devices: a whole 4x4x8 slice. The times are simulated.
256 devices in a mesh: dp: 16 (over y_lo, x, core), ctx: 16 (over y_hi, z).
Axes of the slice: x: 4, y: 4 (y_hi: 2, y_lo: 2; y = y_hi * 2 + y_lo), z: 8, core: 2. Of those that a mesh axis runs over, the one named last changes fastest.
Arguments:
- query: bfloat16 [16, 2048, 1024], P('dp', 'ctx'), may hold values from -5 to 5
- key: bfloat16 [16, 2048, 128], P('dp', 'ctx'), may hold values from -5 to 5
- value: bfloat16 [16, 2048, 128], P('dp', 'ctx'), may hold values from -6 to 6
- output: bfloat16 [16, 2048, 1024], P('dp', 'ctx'), may hold values from -6 to 6
- output_cotangent: bfloat16 [16, 2048, 1024], P('dp', 'ctx'), may hold values from -6 to 6
- inputs: bfloat16 [32768, 8192], P(('dp', 'ctx')), may hold values from -0.125 to 0.125
- doc_lengths: int32 [16, 8], P('dp'), may hold values from 1 to 1024, 2048 in all within a row
- block_order: int32 [32], replicated, may hold values from 0 to 31, each once
Outputs:
- d_query: bfloat16 [16, 2048, 1024], P('dp', 'ctx')
- d_key: bfloat16 [16, 2048, 128], P('dp', 'ctx')
- value_gradient: bfloat16 [16, 2048, 128], P('dp', 'ctx')
- value_weight_gradient: float32 [8192, 128], P(('dp', 'ctx'))
Inputs may be any that keep to these rules, and one draw needn't show every extreme that they name: `doc_lengths`: row s lists in order the lengths of the 8 documents packed into sequence s; they add up to 2048 and the longest has exactly 1024 tokens. Storage block c of every sequence (storage rows c * 64 onward) holds the sequence's block block_order[c] of 64 tokens; each number appears once.
All inputs are finite; a program needn't handle non-finite values.
Results may differ from a plain program's by a relative error of at most 0.015.
Values may be sent and summed in bfloat16 or wider, within the bound.
No kernel may reach another device: no remote copies, remote signals or barrier semaphores. Data moves between devices by JAX's collectives and lax.ppermute only.
A program may use at most 64 MiB of HBM per device.

v0:
```python
import jax
import jax.numpy as jnp
from jax import lax
from jax.sharding import PartitionSpec as P

HEAD_SIZE = 128
KEY_VALUE_HEADS = 1
QUERY_HEADS = 8


score_with_mask = -1e30


def over_blocks(running, members, first_row, step_fn):
    piece_rows = members[0].shape[0]
    block_span = min(512, piece_rows)
    for block_start in range(0, piece_rows, block_span):
        span_rows = min(block_span, piece_rows - block_start)
        running = step_fn(
            running,
            tuple((member[block_start : block_start + span_rows] for member in members)),
            first_row + block_start,
        )
    return running


def local(query, key, value, output, output_cotangent, inputs, doc_lengths, block_order):
    total_row_count = query.shape[1]
    query_group_width = QUERY_HEADS // KEY_VALUE_HEADS
    score_scale = HEAD_SIZE ** (-0.5)
    block_rows = total_row_count // 2
    key_value_width = KEY_VALUE_HEADS * HEAD_SIZE
    seq_length = total_row_count * lax.axis_size("ctx")
    doc_ends = jnp.cumsum(doc_lengths[0])

    def locate(first_row, count_rows):
        storage = first_row + jnp.arange(count_rows, dtype=jnp.int32)
        position = block_order[storage // block_rows] * block_rows + storage % block_rows
        segment = jnp.sum((position[:, None] >= doc_ends[None, :]).astype(jnp.int32), axis=1)
        return (position, segment)

    query_pos, query_seg = locate(lax.axis_index("ctx") * total_row_count, total_row_count)
    query_rows = query[0].reshape(total_row_count, KEY_VALUE_HEADS, query_group_width, HEAD_SIZE)
    output_gradients = output_cotangent[0].reshape(
        total_row_count, KEY_VALUE_HEADS, query_group_width, HEAD_SIZE
    )
    forward_result = output[0].reshape(
        total_row_count, KEY_VALUE_HEADS, query_group_width, HEAD_SIZE
    )
    delta = jnp.sum(
        output_gradients.astype(jnp.float32) * forward_result.astype(jnp.float32), axis=3
    ).transpose(1, 2, 0)

    def allowed_pairs(first_row, count_rows):
        key_pos, key_seg = locate(first_row, count_rows)
        return (query_seg[:, None] == key_seg[None, :]) & (key_pos[None, :] <= query_pos[:, None])

    def masked_scores(key_block, allowed):
        scores = (
            jnp.einsum("qhgd,khd->hgqk", query_rows, key_block, preferred_element_type=jnp.float32)
            * score_scale
        )
        return jnp.where(allowed[None, None], scores, score_with_mask)

    def stats_block(running, blocks, first_row):
        key_block = blocks[0]
        allowed = allowed_pairs(first_row, key_block.shape[0])
        top_old, total_old = running
        scores = masked_scores(key_block, allowed)
        top_new = jnp.maximum(top_old, jnp.max(scores, axis=3))
        total_new = total_old * jnp.exp(top_old - top_new) + jnp.sum(
            jnp.exp(scores - top_new[..., None]), axis=3
        )
        return (top_new, total_new)

    def grad_block(running, blocks, first_row):
        key_block, value_block = blocks
        span_rows = key_block.shape[0]
        allowed = allowed_pairs(first_row, span_rows)
        probs = jnp.where(
            allowed[None, None],
            jnp.exp(masked_scores(key_block, allowed) - log_total[..., None]),
            0.0,
        )
        probs_low = probs.astype(jnp.bfloat16)
        dprobs = jnp.einsum(
            "qhgd,khd->hgqk", output_gradients, value_block, preferred_element_type=jnp.float32
        )
        dscores = (probs * (dprobs - delta[..., None])).astype(jnp.bfloat16)
        query_add = jnp.einsum(
            "hgqk,khd->qhgd", dscores, key_block, preferred_element_type=jnp.float32
        )
        key_add = (
            jnp.einsum("hgqk,qhgd->khd", dscores, query_rows, preferred_element_type=jnp.float32)
            * score_scale
        )
        value_add = jnp.einsum(
            "hgqk,qhgd->khd", probs_low, output_gradients, preferred_element_type=jnp.float32
        )
        query_add, key_add, value_add = (query_add, key_add, value_add)
        query_acc, key_acc, value_acc = running
        key_acc = lax.dynamic_update_slice_in_dim(
            key_acc, key_add.reshape(span_rows, key_value_width), first_row, 0
        )
        value_acc = lax.dynamic_update_slice_in_dim(
            value_acc, value_add.reshape(span_rows, key_value_width), first_row, 0
        )
        return (query_acc + query_add, key_acc, value_acc)

    empty_stats = (
        jnp.full(
            (KEY_VALUE_HEADS, query_group_width, total_row_count), score_with_mask, jnp.float32
        ),
        jnp.zeros((KEY_VALUE_HEADS, query_group_width, total_row_count), jnp.float32),
    )
    empty_grads = (
        jnp.zeros((total_row_count, KEY_VALUE_HEADS, query_group_width, HEAD_SIZE), jnp.float32),
        jnp.zeros((seq_length, key_value_width), jnp.float32),
        jnp.zeros((seq_length, key_value_width), jnp.float32),
    )
    top_score, total_sum = over_blocks(
        empty_stats,
        (
            lax.all_gather(key, "ctx", axis=1, tiled=True)[0].reshape(
                -1, KEY_VALUE_HEADS, HEAD_SIZE
            ),
        ),
        jnp.int32(0),
        stats_block,
    )
    log_total = top_score + jnp.log(total_sum)
    grads = over_blocks(
        empty_grads,
        (
            lax.all_gather(key, "ctx", axis=1, tiled=True)[0].reshape(
                -1, KEY_VALUE_HEADS, HEAD_SIZE
            ),
            lax.all_gather(value, "ctx", axis=1, tiled=True)[0].reshape(
                -1, KEY_VALUE_HEADS, HEAD_SIZE
            ),
        ),
        jnp.int32(0),
        grad_block,
    )
    query_acc, key_acc, value_acc = grads
    d_query = (
        (query_acc * score_scale)
        .astype(jnp.bfloat16)
        .reshape(1, total_row_count, QUERY_HEADS * HEAD_SIZE)
    )
    key_sum, value_sum = (
        lax.psum_scatter(
            key_acc.astype(jnp.bfloat16), "ctx", scatter_dimension=0, tiled=True
        ).astype(jnp.float32),
        lax.psum_scatter(
            value_acc.astype(jnp.bfloat16), "ctx", scatter_dimension=0, tiled=True
        ).astype(jnp.float32),
    )
    d_key = key_sum.astype(jnp.bfloat16).reshape(1, total_row_count, key_value_width)
    value_gradient = value_sum.astype(jnp.bfloat16).reshape(1, total_row_count, key_value_width)
    value_local = value_gradient[0]
    weight_grad = lax.psum_scatter(
        lax.dot_general(
            inputs, value_local, (((0,), (0,)), ((), ())), preferred_element_type=jnp.float32
        ),
        ("dp", "ctx"),
        scatter_dimension=0,
        tiled=True,
    )
    return (d_query, d_key, value_gradient, weight_grad)


def solution(mesh):
    in_specs = (
        P("dp", "ctx", None),
        P("dp", "ctx", None),
        P("dp", "ctx", None),
        P("dp", "ctx", None),
        P("dp", "ctx", None),
        P(("dp", "ctx"), None),
        P("dp", None),
        P(),
    )
    out_specs = (
        P("dp", "ctx", None),
        P("dp", "ctx", None),
        P("dp", "ctx", None),
        P(("dp", "ctx"), None),
    )
    return jax.shard_map(local, mesh=mesh, in_specs=in_specs, out_specs=out_specs, check_vma=False)
```

profile of v0, /device:TPU:32, one launch (start us, length us, event | category | flops | bytes accessed | tf_op | source)
XLA Modules:
  0.0 1816.5 jit_solution(18429122147290802749)
XLA Ops:
  11.2 1.8 fusion.86
  13.0 4.3 compare_select_fusion.4
  17.3 4.4 compare_select_fusion.16
  21.7 2.1 fusion.85
  23.8 1.6 gather_fusion
  25.4 1.0 copy.132
  26.4 1.0 copy.133
  27.4 42.6 %all_gather.7 = bf16[1,2048,128]{2,1,0:T(8,128)(2,1)S(1)} all-gather(bf16[1,128,128]{2,1,0:T(8,128)(2,1)} %param.9), channel_id=1, replica_groups=mesh['dp'=16,'ctx'=16] {'ctx'}, dimensions={1}, use_global_device_ids=true | all-gather | bytes 557056 | tf_op jit(solution)/shard_map/all_gather | solution.py:135
  70.3 16.4 fusion.67
  86.7 16.4 fusion.69
  103.1 15.7 fusion.71
  118.8 15.7 fusion.65
  141.1 0.8 copy-done.19
  142.0 43.8 %all_gather.8 = bf16[1,2048,128]{2,1,0:T(8,128)(2,1)S(1)} all-gather(bf16[1,128,128]{2,1,0:T(8,128)(2,1)} %param.10), channel_id=1, replica_groups=mesh['dp'=16,'ctx'=16] {'ctx'}, dimensions={1}, use_global_device_ids=true | all-gather | bytes 557056 | tf_op jit(solution)/shard_map/all_gather | solution.py:138
  185.8 1.2 multiply_bitcast_fusion
  187.0 0.9 copy.134
  187.9 1.2 reduce_sum.117
  189.3 2.4 fusion.12
  191.8 2.1 fusion.13
  195.2 0.9 dynamic_update_slice.24
  196.1 1.1 fusion.26
  197.1 1.1 fusion.24
  198.9 1.0 copy-done.10
  199.9 1.1 fusion.22
  201.0 136.2 %reduce-scatter.8.cloned.1.call-done = bf16[128,128]{1,0:T(8,128)(2,1)} async-done(((bf16[2048,128]{1,0:T(8,128)(2,1)}), bf16[128,128]{1,0:T(8,128)(2,1)}) %reduce-scatter.8.cloned.1.call-update) | async-done | bytes 32784 | tf_op jit(solution)/shard_map/reduce_scatter | solution.py:155
  337.3 3.5 convolution_bitcast_fusion
  340.7 5.6 copy.130
  346.3 1.7 fusion.48
  348.0 1.3 convolution_add_fusion.2
  350.1 0.9 copy.116
  351.0 186.6 %reduce-scatter.6.cloned.1.call-done = bf16[128,128]{1,0:T(8,128)(2,1)} async-done(((bf16[2048,128]{1,0:T(8,128)(2,1)}), bf16[128,128]{1,0:T(8,128)(2,1)}) %reduce-scatter.6.cloned.1.call-update) | async-done | bytes 32784 | tf_op jit(solution)/shard_map/reduce_scatter | solution.py:152
  537.5 1272.5 %reduce-scatter.10.cloned.1.call-done = f32[32,128]{1,0:T(8,128)} async-done(((f32[8192,128]{1,0:T(8,128)}), f32[32,128]{1,0:T(8,128)}) %reduce-scatter.10.cloned.1.call-update) | async-done | bytes 16400
  (130 shorter events, 13.6 us)
Async XLA Ops:
  7.2 330.1 %copy-start = (bf16[128,8192]{1,0:T(8,128)(2,1)S(1)}, bf16[128,8192]{1,0:T(8,128)(2,1)}, u32[]{:S(2)}) copy-start(bf16[128,8192]{1,0:T(8,128)(2,1)} %param.13) | copy-start | bytes 6291460
  7.2 62.9 %copy-start.23 = (s32[1,8]{1,0:T(1,128)S(1)}, s32[1,8]{1,0:T(1,128)}, u32[]{:S(2)}) copy-start(s32[1,8]{1,0:T(1,128)} %param.14) | copy-start | bytes 100
  7.2 330.1 %reduce-scatter.8.cloned.1.call-start = ((), (), s32[]{:S(2)}) async-start(), calls=%async_computation.4 | async-start | bytes 557056 | tf_op jit(solution)/shard_map/reduce_scatter | solution.py:155
  27.4 161.8 %copy-start.12 = (bf16[16,8,8,128]{3,2,1,0:T(8,128)(2,1)}, bf16[16,8,8,128]{3,2,1,0:T(8,128)(2,1)S(1)}, u32[]{:S(2)}) copy-start(bf16[16,8,8,128]{3,2,1,0:T(8,128)(2,1)S(1)} %copy.133) | copy-start | bytes 786436
  70.0 66.7 %copy-start.14 = (bf16[1,2048,128]{2,1,0:T(8,128)(2,1)}, bf16[1,2048,128]{2,1,0:T(8,128)(2,1)S(1)}, u32[]{:S(2)}) copy-start(bf16[1,2048,128]{2,1,0:T(8,128)(2,1)S(1)} %all_gather.7) | copy-start | bytes 1572868
  135.3 3.1 copy-start.22
  135.3 4.2 copy-start.21
  135.8 4.8 copy-start.1
  136.3 3.8 copy-start.3
  136.7 2.8 copy-start.5
  137.2 1.8 copy-start.7
  140.6 45.2 %copy-start.20 = (bf16[1,128,1024]{2,1,0:T(8,128)(2,1)S(1)}, bf16[1,128,1024]{2,1,0:T(8,128)(2,1)}, u32[]{:S(2)}) copy-start(bf16[1,128,1024]{2,1,0:T(8,128)(2,1)} %param.12) | copy-start | bytes 786436
  141.1 0.8 copy-start.19
  142.0 395.6 %reduce-scatter.6.cloned.1.call-start = ((), (), s32[]{:S(2)}) async-start(), calls=%async_computation.3 | async-start | bytes 557056 | tf_op jit(solution)/shard_map/reduce_scatter | solution.py:152
  185.8 3.4 copy-start.17
  189.3 2.5 copy-start.6
  191.7 3.0 copy-start.16
  191.7 2.2 copy-start.4
  191.7 2.2 copy-start.13
  191.7 2.3 copy-start.18
  194.7 3.5 copy-start.8
  195.2 3.0 copy-start.2
  198.9 1.0 copy-start.10
  201.0 1609.0 %reduce-scatter.10.cloned.1.call-start = ((), (), s32[]{:S(2)}) async-start(), calls=%async_computation.5 | async-start | bytes 4210688
  346.3 3.1 copy-start.9
  346.3 3.1 copy-start.15
  348.0 1.7 copy-start.11
Sparse Core Ops, SparseCore 0:
  142.1 195.1 reduce-scatter.7
  342.1 195.3 reduce-scatter.5
  540.6 1269.3 reduce-scatter.9
where the time goes:
time: 1820 us
  waiting for transfers between devices  1600 us (88%)
  blocking collectives  86.4 us (5%)
  other arithmetic  81.5 us (4%)
  matrix products  20.5 us (1%)
  local copies, waits for them, and re-layouts  18.4 us (1%)
    unnamed x4, waiting for transfers between devices  1270 us
    reduce_scatter x1, waiting for transfers between devices, local(): lax.psum_scatter(key_acc.astype(jnp.bfloat16), 'ctx', scatter_dimension=0...  187 us
    reduce_scatter x1, waiting for transfers between devices, local(): lax.psum_scatter(value_acc.astype(jnp.bfloat16), 'ctx', scatter_dimension...  136 us
    add x5, other arithmetic, locate(): block_order[storage // block_rows] * block_rows + storage % block_rows  64.1 us
    all_gather x1, blocking collectives, local(): lax.all_gather(value, 'ctx', axis=1, tiled=True)[0]  43.8 us
    all_gather x1, blocking collectives, local(): lax.all_gather(key, 'ctx', axis=1, tiled=True)[0]  42.6 us
  transfers between devices with their start and end apart: 3, of which 3 were waited for; matrix products, arithmetic and copies ran while one was open for 2% of the time, Pallas kernels for 0%

commit v1 on v0

v1 whole, which is shorter than its diff:
```python
import functools
import math

import jax
import jax.numpy as jnp
from jax import lax
from jax.experimental import pallas as pl
from jax.experimental.pallas import tpu as pltpu
from jax.sharding import Mesh, PartitionSpec as P

HEAD_SIZE = 128
QUERY_HEADS = 8
BLOCK = 64
BLOCKS = 32
NDOC = 8
ROWS = 128
KEYS = 2048
N_CTX = 16
CHUNK = 256
PAIR = 2 * HEAD_SIZE
PAIRS = QUERY_HEADS // 2
SCALE = HEAD_SIZE**-0.5
SCALE_LOG2 = SCALE * math.log2(math.e)
MASKED = -1e30
VMEM_LIMIT = 48 * 1024 * 1024
NT = (((1,), (1,)), ((), ()))

CTX = ("yhi", "z")
NEAR = ("x", "core")
FAR = ("ylo", "yhi", "z")


def two_heads(block):
    return jnp.concatenate([block[:, :HEAD_SIZE], block[:, HEAD_SIZE:]], axis=0)


def fold_rows(tile, op):
    return op(tile.reshape(tile.shape[0] // 8, 8, tile.shape[1]), axis=0)


def write_bias(scalars, bias):
    lane = lax.broadcasted_iota(jnp.int32, (1, ROWS), 1)
    me = scalars[BLOCKS + NDOC]
    first, second = scalars[2 * me] * BLOCK, scalars[2 * me + 1] * BLOCK
    high = jnp.where(lane < BLOCK, first + lane, second + lane - BLOCK)
    low = jnp.zeros_like(high)
    end = scalars[BLOCKS]
    for doc in range(1, NDOC):
        low = jnp.where(high >= end, end, low)
        end = end + scalars[BLOCKS + doc]
    low = jnp.where(high >= end, end, low)
    row = lax.broadcasted_iota(jnp.int32, (BLOCK, ROWS), 0)

    def one_block(block, carry):
        position = scalars[block] * BLOCK + row
        allowed = (position <= high) & (position >= low)
        start = pl.multiple_of(block * BLOCK, BLOCK)
        bias[pl.ds(start, BLOCK), :] = jnp.where(allowed, 0.0, MASKED)
        return carry

    lax.fori_loop(0, BLOCKS, one_block, 0)


def probs_kernel(scalars, query, cotangent, kv, probs, value_part, bias, scores, value_acc):
    step = pl.program_id(0)

    @pl.when(step == 0)
    def _():
        write_bias(scalars, bias)
        value_acc[...] = jnp.zeros_like(value_acc)

    queries = two_heads(query[...])
    gradients = two_heads(cotangent[...])

    def rows_of(chunk):
        return pl.ds(pl.multiple_of(chunk * CHUNK, CHUNK), CHUNK)

    def score(chunk, top):
        rows = rows_of(chunk)
        raw = lax.dot_general(
            kv[rows, :HEAD_SIZE], queries, NT, preferred_element_type=jnp.float32
        )
        add = bias[rows, :]
        tile = raw * SCALE_LOG2 + jnp.concatenate([add, add], axis=1)
        scores[rows, :] = tile
        return jnp.maximum(top, fold_rows(tile, jnp.max))

    top = lax.fori_loop(0, KEYS // CHUNK, score, jnp.full((8, PAIR), MASKED, jnp.float32))
    top = jnp.max(top, axis=0, keepdims=True)

    def weigh(chunk, total):
        rows = rows_of(chunk)
        tile = jnp.exp2(scores[rows, :] - top)
        scores[rows, :] = tile
        return total + fold_rows(tile, jnp.sum)

    total = lax.fori_loop(0, KEYS // CHUNK, weigh, jnp.zeros((8, PAIR), jnp.float32))
    share = 1.0 / jnp.sum(total, axis=0, keepdims=True)

    def finish(chunk, carry):
        rows = rows_of(chunk)
        low = (scores[rows, :] * share).astype(jnp.bfloat16)
        probs[rows, :] = low
        value_acc[rows, :] += jnp.dot(low, gradients, preferred_element_type=jnp.float32)
        return carry

    lax.fori_loop(0, KEYS // CHUNK, finish, 0)

    @pl.when(step == PAIRS - 1)
    def _():
        value_part[...] = value_acc[...].astype(jnp.bfloat16)


def grads_kernel(
    query, output, cotangent, kv, probs, query_grad, key_part, key_turned, key_acc, query_acc
):
    step = pl.program_id(0)

    @pl.when(step == 0)
    def _():
        key_turned[...] = kv[:, :HEAD_SIZE].T
        key_acc[...] = jnp.zeros_like(key_acc)

    queries = two_heads(query[...])
    gradients = two_heads(cotangent[...])
    product = gradients.astype(jnp.float32) * two_heads(output[...]).astype(jnp.float32)
    delta = jnp.concatenate(
        [
            jnp.sum(product[:ROWS].T, axis=0, keepdims=True),
            jnp.sum(product[ROWS:].T, axis=0, keepdims=True),
        ],
        axis=1,
    )
    query_acc[...] = jnp.zeros_like(query_acc)
    for chunk in range(KEYS // CHUNK):
        rows = pl.ds(chunk * CHUNK, CHUNK)
        dprobs = lax.dot_general(
            kv[rows, HEAD_SIZE:], gradients, NT, preferred_element_type=jnp.float32
        )
        dscores = (probs[rows, :].astype(jnp.float32) * (dprobs - delta)).astype(jnp.bfloat16)
        key_acc[rows, :] += jnp.dot(dscores, queries, preferred_element_type=jnp.float32)
        query_acc[...] += jnp.dot(
            key_turned[:, rows], dscores, preferred_element_type=jnp.float32
        )
    turned = query_acc[...] * SCALE
    query_grad[:, :HEAD_SIZE] = turned[:, :ROWS].T.astype(jnp.bfloat16)
    query_grad[:, HEAD_SIZE:] = turned[:, ROWS:].T.astype(jnp.bfloat16)

    @pl.when(step == PAIRS - 1)
    def _():
        key_part[...] = (key_acc[...] * SCALE).astype(jnp.bfloat16)


def pair_block(step):
    return (0, step)


def whole(step):
    return (0, 0)


def attention_probs(scalars, query, cotangent, kv):
    return pl.pallas_call(
        probs_kernel,
        grid=(PAIRS,),
        in_specs=[
            pl.BlockSpec(memory_space=pltpu.SMEM),
            pl.BlockSpec((ROWS, PAIR), pair_block),
            pl.BlockSpec((ROWS, PAIR), pair_block),
            pl.BlockSpec((KEYS, 2 * HEAD_SIZE), whole),
        ],
        out_specs=[
            pl.BlockSpec((KEYS, PAIR), pair_block),
            pl.BlockSpec((KEYS, HEAD_SIZE), whole),
        ],
        out_shape=[
            jax.ShapeDtypeStruct((KEYS, QUERY_HEADS * ROWS), jnp.bfloat16),
            jax.ShapeDtypeStruct((KEYS, HEAD_SIZE), jnp.bfloat16),
        ],
        scratch_shapes=[
            pltpu.VMEM((KEYS, ROWS), jnp.float32),
            pltpu.VMEM((KEYS, PAIR), jnp.float32),
            pltpu.VMEM((KEYS, HEAD_SIZE), jnp.float32),
        ],
        compiler_params=pltpu.CompilerParams(vmem_limit_bytes=VMEM_LIMIT),
        name="probs_and_value_part",
    )(scalars, query, cotangent, kv)


def attention_grads(query, output, cotangent, kv, probs):
    return pl.pallas_call(
        grads_kernel,
        grid=(PAIRS,),
        in_specs=[
            pl.BlockSpec((ROWS, PAIR), pair_block),
            pl.BlockSpec((ROWS, PAIR), pair_block),
            pl.BlockSpec((ROWS, PAIR), pair_block),
            pl.BlockSpec((KEYS, 2 * HEAD_SIZE), whole),
            pl.BlockSpec((KEYS, PAIR), pair_block),
        ],
        out_specs=[
            pl.BlockSpec((ROWS, PAIR), pair_block),
            pl.BlockSpec((KEYS, HEAD_SIZE), whole),
        ],
        out_shape=[
            jax.ShapeDtypeStruct((ROWS, QUERY_HEADS * HEAD_SIZE), jnp.bfloat16),
            jax.ShapeDtypeStruct((KEYS, HEAD_SIZE), jnp.bfloat16),
        ],
        scratch_shapes=[
            pltpu.VMEM((HEAD_SIZE, KEYS), jnp.bfloat16),
            pltpu.VMEM((KEYS, HEAD_SIZE), jnp.float32),
            pltpu.VMEM((HEAD_SIZE, PAIR), jnp.float32),
        ],
        compiler_params=pltpu.CompilerParams(vmem_limit_bytes=VMEM_LIMIT),
        name="query_and_key_part",
    )(query, output, cotangent, kv, probs)


def exchange(blocks, axes):
    return lax.all_to_all(blocks, axes, 0, 0, tiled=False)


def gather(block, axes, count):
    return exchange(jnp.broadcast_to(block[None], (count,) + block.shape), axes)


def summed(blocks):
    return jnp.sum(blocks.astype(jnp.float32), axis=0)


def local(query, key, value, output, output_cotangent, inputs, doc_lengths, block_order):
    scalars = jnp.concatenate(
        [block_order, doc_lengths[0], lax.axis_index(CTX).astype(jnp.int32)[None]]
    )
    near_count, far_count = lax.axis_size(NEAR), lax.axis_size(FAR)
    low_count = lax.axis_size("ylo")
    columns = inputs.shape[1]
    kv = gather(jnp.concatenate([key[0], value[0]], axis=1), CTX, N_CTX).reshape(KEYS, -1)

    by_column_owner = inputs.reshape(ROWS, low_count, near_count, -1).transpose(2, 0, 1, 3)
    near_inputs = exchange(
        by_column_owner.reshape(near_count, ROWS, columns // near_count), NEAR
    ).reshape(near_count * ROWS, columns // near_count)

    probs, value_part = attention_probs(scalars, query[0], output_cotangent[0], kv)
    value_blocks = exchange(value_part.reshape(N_CTX, ROWS, HEAD_SIZE), CTX)
    query_grad, key_part = attention_grads(
        query[0], output[0], output_cotangent[0], kv, probs
    )
    value_grad = summed(value_blocks).astype(jnp.bfloat16)
    key_blocks = exchange(key_part.reshape(N_CTX, ROWS, HEAD_SIZE), CTX)
    key_grad = summed(key_blocks).astype(jnp.bfloat16)

    near_values = gather(value_grad, NEAR, near_count).reshape(-1, HEAD_SIZE)
    weight_part = lax.dot_general(
        near_inputs,
        near_values,
        (((0,), (0,)), ((), ())),
        preferred_element_type=jnp.float32,
    ).astype(jnp.bfloat16)
    weight_grad = summed(exchange(weight_part.reshape(far_count, -1, HEAD_SIZE), FAR))
    return query_grad[None], key_grad[None], value_grad[None], weight_grad


def solution(mesh):
    fine = Mesh(
        mesh.devices.reshape(2, 4, 2, 2, 8), ("ylo", "x", "core", "yhi", "z")
    )
    dp = ("ylo", "x", "core")
    tokens = P(dp, CTX, None)
    flat = P(dp + CTX, None)
    return jax.shard_map(
        local,
        mesh=fine,
        in_specs=(tokens,) * 5 + (flat, P(dp, None), P()),
        out_specs=(tokens, tokens, tokens, flat),
        check_vma=False,
    )
```

time: 1820 us -> 165 us (0.09)
  waiting for transfers between devices: 1600 us -> 86.4 us
  blocking collectives: 86.4 us -> 0 us
  other arithmetic: 81.5 us -> 2.34 us
  starting transfers between devices: 0.12 us -> 36 us
  Pallas kernels: 0 us -> 23.4 us
  matrix products: 20.5 us -> 2.03 us
    unnamed x4 -> x0, waiting for transfers between devices: 1270 us -> none
    reduce_scatter x2 -> x0, waiting for transfers between devices: 323 us -> none  [the longest x1 187 us: local(): lax.psum_scatter(key_acc.astype(jnp.bfloat16), 'ctx', scatter_dimension=0...]
    all_gather x2 -> x0, blocking collectives: 86.4 us -> none  [the longest x1 43.8 us: local(): lax.all_gather(value, 'ctx', axis=1, tiled=True)[0]]
    all_to_all x0 -> x6, waiting for transfers between devices: none -> 86.4 us  [exchange(): return lax.all_to_all(blocks, axes, 0, 0, tiled=False)]
    add x6 -> x0, other arithmetic: 64.2 us -> none  [the longest x5 64.1 us: locate(): block_order[storage // block_rows] * block_rows + storage % block_rows]
    all_to_all x0 -> x6, starting transfers between devices: none -> 36 us  [exchange(): return lax.all_to_all(blocks, axes, 0, 0, tiled=False)]
    pallas_call x0 -> x2, Pallas kernels: none -> 23.4 us  [the longest x1 15.8 us: attention_probs(): pl.pallas_call(probs_kernel, grid=(PAIRS,), in_specs=[pl.BlockSpec(memory...]
    dot_general x21 -> x1, matrix products: 20.5 us -> 2.03 us  [local(): lax.dot_general(near_inputs, near_values, (((0,), (0,)), ((), ())), prefe...]
  transfers between devices with their start and end apart: 3 -> 6, of which waited for: 3 -> 5; matrix products, arithmetic and copies ran while one was open for 2% -> 8% of each run, Pallas kernels for 0% -> 5%
where the time goes in v1:
time: 165 us; the launch traced here: 164 us
  waiting for transfers between devices  86.4 us (52%)
  starting transfers between devices  36 us (22%)
  Pallas kernels  23.4 us (14%)
  local copies, waits for them, and re-layouts  12.7 us (8%)
  other arithmetic  2.34 us (1%)
  matrix products  2.03 us (1%)
    all_to_all x6, waiting for transfers between devices, exchange(): return lax.all_to_all(blocks, axes, 0, 0, tiled=False)  86.4 us
    all_to_all x6, starting transfers between devices, exchange(): return lax.all_to_all(blocks, axes, 0, 0, tiled=False)  36 us
    pallas_call x1, Pallas kernels, attention_probs(): pl.pallas_call(probs_kernel, grid=(PAIRS,), in_specs=[pl.BlockSpec(memory...  15.8 us
    pallas_call x1, Pallas kernels, attention_grads(): pl.pallas_call(grads_kernel, grid=(PAIRS,), in_specs=[pl.BlockSpec((ROWS,...  7.54 us
    reshape x1, local copies, waits for them, and re-layouts, local(): by_column_owner.reshape(near_count, ROWS, columns // near_count)  4.5 us
  transfers between devices with their start and end apart: 6, of which 5 were waited for; matrix products, arithmetic and copies ran while one was open for 8% of the time, Pallas kernels for 5%

profile of v1, /device:TPU:32, one launch (start us, length us, event | category | flops | bytes accessed | tf_op | source)
XLA Modules:
  0.0 163.6 jit_solution(4962825897179340233)
XLA Ops:
  0.6 0.0 copy-start.4
  0.7 0.8 pad_maximum_fusion
  1.5 1.1 broadcast_in_dim.24
  2.6 11.2 %all-to-all-start = ((bf16[16,128,256]{2,1,0:T(8,128)(2,1)}), bf16[16,128,256]{2,1,0:T(8,128)(2,1)S(1)}, u32[]{:S(2)}, u32[]{:S(2)}) async-start(bf16[16,128,256]{2,1,0:T(8,128)(2,1)} %broadcast_in_dim.24), calls=%async_computation | async-start | bytes 2097152 | tf_op jit(solution)/shard_map/all_to_all | solution.py:220
  13.8 0.1 pad_add_fusion.scalars
  13.9 27.7 %all-to-all-done = bf16[16,128,256]{2,1,0:T(8,128)(2,1)S(1)} async-done(((bf16[16,128,256]{2,1,0:T(8,128)(2,1)}), bf16[16,128,256]{2,1,0:T(8,128)(2,1)S(1)}, u32[]{:S(2)}, u32[]{:S(2)}) %all-to-all-start) | async-done | bytes 1048608 | tf_op jit(solution)/shard_map/all_to_all | solution.py:220
  41.6 0.0 copy-done
  41.6 15.8 %probs_and_value_part.1 = (bf16[2048,1024]{1,0:T(8,128)(2,1)}, bf16[2048,128]{1,0:T(8,128)(2,1)}) custom-call(s32[41]{0:T(128)S(1)} %pad_add_fusion.scalars, bf16[128,1024]{1,0:T(8,128)(2,1)S(1)} %bitcast.32, bf16[128,1024]{1,0:T(8,128)(2,1)S(1)} %bitcast.34, bf16[2048,256]{1,0:T(8,128)(2,1)S(1)} %bitcast.30), custom_call_target="tpu_custom_call" | custom-call | tf_op jit(solution)/shard_map/probs_and_value_part/pallas_call | solution.py:163
  57.4 5.2 %all-to-all-start.2 = ((bf16[16,128,128]{2,1,0:T(8,128)(2,1)}), bf16[16,128,128]{2,1,0:T(8,128)(2,1)S(1)}, u32[]{:S(2)}, u32[]{:S(2)}) async-start(bf16[16,128,128]{2,1,0:T(8,128)(2,1)} %bitcast.11), calls=%async_computation.2 | async-start | bytes 1048576 | tf_op jit(solution)/shard_map/all_to_all | solution.py:220
  62.6 2.4 %copy.17 = bf16[16,8,16,512]{3,2,1,0:T(8,128)(2,1)S(1)} copy(bf16[16,8,16,512]{3,1,2,0:T(8,128)(2,1)} %bitcast.39) | data formatting | bytes 4194304
  65.1 2.9 %copy.19 = bf16[128,2,8,512]{3,1,0,2:T(2,128)(2,1)} copy(bf16[128,2,8,512]{3,2,1,0:T(8,128)(2,1)S(1)} %bitcast.38) | data formatting | bytes 4194304 | tf_op jit(solution)/shard_map/reshape | solution.py:240
  68.0 4.5 %reshape.34 = bf16[8,128,1024]{2,1,0:T(8,128)(2,1)} reshape(bf16[8,128,2,512]{3,2,1,0:T(2,128)(2,1)} %bitcast.37) | data formatting | bytes 4194304 | tf_op jit(solution)/shard_map/reshape | solution.py:242
  72.5 6.5 %all-to-all-done.2 = bf16[16,128,128]{2,1,0:T(8,128)(2,1)S(1)} async-done(((bf16[16,128,128]{2,1,0:T(8,128)(2,1)}), bf16[16,128,128]{2,1,0:T(8,128)(2,1)S(1)}, u32[]{:S(2)}, u32[]{:S(2)}) %all-to-all-start.2) | async-done | bytes 524320 | tf_op jit(solution)/shard_map/all_to_all | solution.py:220
  79.0 4.4 %all-to-all-start.4 = ((bf16[8,128,1024]{2,1,0:T(8,128)(2,1)}), bf16[8,128,1024]{2,1,0:T(8,128)(2,1)}, u32[]{:S(2)}, u32[]{:S(2)}) async-start(bf16[8,128,1024]{2,1,0:T(8,128)(2,1)} %reshape.34), calls=%async_computation.4 | async-start | bytes 4194304 | tf_op jit(solution)/shard_map/all_to_all | solution.py:220
  83.4 0.1 reduce_sum.34
  83.5 0.0 copy-start.3
  83.5 0.1 copy.14
  83.6 27.0 %all-to-all-done.4 = bf16[8,128,1024]{2,1,0:T(8,128)(2,1)} async-done(((bf16[8,128,1024]{2,1,0:T(8,128)(2,1)}), bf16[8,128,1024]{2,1,0:T(8,128)(2,1)}, u32[]{:S(2)}, u32[]{:S(2)}) %all-to-all-start.4) | async-done | bytes 2097184 | tf_op jit(solution)/shard_map/all_to_all | solution.py:220
  110.7 0.7 broadcast_in_dim.29
  111.4 3.4 %all-to-all-start.3 = ((bf16[8,128,128]{1,2,0:T(8,128)(2,1)}), bf16[8,128,128]{1,2,0:T(8,128)(2,1)S(1)}, u32[]{:S(2)}, u32[]{:S(2)}) async-start(bf16[8,128,128]{1,2,0:T(8,128)(2,1)} %broadcast_in_dim.29), calls=%async_computation.3 | async-start | bytes 524288 | tf_op jit(solution)/shard_map/all_to_all | solution.py:220
  114.8 0.0 copy-done.2
  114.8 7.5 %query_and_key_part.1 = (bf16[128,1024]{1,0:T(8,128)(2,1)}, bf16[2048,128]{1,0:T(8,128)(2,1)}) custom-call(bf16[128,1024]{1,0:T(8,128)(2,1)S(1)} %bitcast.33, bf16[128,1024]{1,0:T(8,128)(2,1)S(1)} %bitcast.36, bf16[128,1024]{1,0:T(8,128)(2,1)S(1)} %bitcast.35, bf16[2048,256]{1,0:T(8,128)(2,1)S(1)} %bitcast.31, bf16[2048,1024]{1,0:T(8,128)(2,1)} %get-tuple-element.8.probs), custom_call_target="tpu_custom_call" | custom-call | tf_op jit(solution)/shard_map/query_and_key_part/pallas_call | solution.py:191
  122.4 0.0 copy-done.3
  122.4 0.0 all-to-all-done.3
  122.4 5.6 %all-to-all-start.1 = ((bf16[16,128,128]{2,1,0:T(8,128)(2,1)}), bf16[16,128,128]{2,1,0:T(8,128)(2,1)S(1)}, u32[]{:S(2)}, u32[]{:S(2)}) async-start(bf16[16,128,128]{2,1,0:T(8,128)(2,1)} %bitcast.9), calls=%async_computation.1 | async-start | bytes 1048576 | tf_op jit(solution)/shard_map/all_to_all | solution.py:220
  127.9 2.0 %fusion.1 = bf16[1024,128]{0,1:T(8,128)(2,1)S(1)} fusion(bf16[8,128,128]{1,2,0:T(8,128)(2,1)S(1)} %all-to-all-done.3, bf16[8,128,1024]{2,1,0:T(8,128)(2,1)} %all-to-all-done.4), kind=kOutput, calls=%fused_computation.3 | convolution fusion | flops 268566528 | bytes 2621440 | tf_op jit(solution)/shard_map/dot_general | solution.py:255
  130.0 0.8 copy.16
  130.8 13.3 %all-to-all-done.1 = bf16[16,128,128]{2,1,0:T(8,128)(2,1)S(1)} async-done(((bf16[16,128,128]{2,1,0:T(8,128)(2,1)}), bf16[16,128,128]{2,1,0:T(8,128)(2,1)S(1)}, u32[]{:S(2)}, u32[]{:S(2)}) %all-to-all-start.1) | async-done | bytes 524320 | tf_op jit(solution)/shard_map/all_to_all | solution.py:220
  144.1 6.2 %all-to-all-start.5 = ((bf16[32,32,128]{2,1,0:T(8,128)(2,1)}), bf16[32,32,128]{2,1,0:T(8,128)(2,1)S(1)}, u32[]{:S(2)}, u32[]{:S(2)}) async-start(bf16[32,32,128]{2,1,0:T(8,128)(2,1)} %bitcast.16), calls=%async_computation.5 | async-start | bytes 524288 | tf_op jit(solution)/shard_map/all_to_all | solution.py:220
  150.4 0.7 reduce_sum.33
  151.1 11.8 %all-to-all-done.5 = bf16[32,32,128]{2,1,0:T(8,128)(2,1)S(1)} async-done(((bf16[32,32,128]{2,1,0:T(8,128)(2,1)}), bf16[32,32,128]{2,1,0:T(8,128)(2,1)S(1)}, u32[]{:S(2)}, u32[]{:S(2)}) %all-to-all-start.5) | async-done | bytes 262176 | tf_op jit(solution)/shard_map/all_to_all | solution.py:220
  162.9 0.7 convert_reduce_fusion
  (7 shorter events, 0.0 us)
Async XLA Ops:
  0.6 13.2 %copy-start.4 = (s32[1,8]{1,0:T(1,128)S(1)}, s32[1,8]{1,0:T(1,128)}, u32[]{:S(2)}) copy-start(s32[1,8]{1,0:T(1,128)} %param.14) | copy-start | bytes 100
  0.6 13.2 %copy-start.5 = (s32[32]{0:T(128)S(1)}, s32[32]{0:T(128)}, u32[]{:S(2)}) copy-start(s32[32]{0:T(128)} %param.15) | copy-start | bytes 388
  0.7 40.9 %copy-start = (bf16[1,128,1024]{2,1,0:T(8,128)(2,1)S(1)}, bf16[1,128,1024]{2,1,0:T(8,128)(2,1)}, u32[]{:S(2)}) copy-start(bf16[1,128,1024]{2,1,0:T(8,128)(2,1)} %param.8) | copy-start | bytes 786436
  0.7 40.9 %copy-start.1 = (bf16[1,128,1024]{2,1,0:T(8,128)(2,1)S(1)}, bf16[1,128,1024]{2,1,0:T(8,128)(2,1)}, u32[]{:S(2)}) copy-start(bf16[1,128,1024]{2,1,0:T(8,128)(2,1)} %param.12) | copy-start | bytes 786436
  2.6 39.0 %all-to-all-start = ((bf16[16,128,256]{2,1,0:T(8,128)(2,1)}), bf16[16,128,256]{2,1,0:T(8,128)(2,1)S(1)}, u32[]{:S(2)}, u32[]{:S(2)}) async-start(bf16[16,128,256]{2,1,0:T(8,128)(2,1)} %broadcast_in_dim.24), calls=%async_computation | async-start | bytes 2097152 | tf_op jit(solution)/shard_map/all_to_all | solution.py:220
  57.4 21.6 %all-to-all-start.2 = ((bf16[16,128,128]{2,1,0:T(8,128)(2,1)}), bf16[16,128,128]{2,1,0:T(8,128)(2,1)S(1)}, u32[]{:S(2)}, u32[]{:S(2)}) async-start(bf16[16,128,128]{2,1,0:T(8,128)(2,1)} %bitcast.11), calls=%async_computation.2 | async-start | bytes 1048576 | tf_op jit(solution)/shard_map/all_to_all | solution.py:220
  72.5 42.3 %copy-start.2 = (bf16[1,128,1024]{2,1,0:T(8,128)(2,1)S(1)}, bf16[1,128,1024]{2,1,0:T(8,128)(2,1)}, u32[]{:S(2)}) copy-start(bf16[1,128,1024]{2,1,0:T(8,128)(2,1)} %param.11) | copy-start | bytes 786436
  79.0 31.6 %all-to-all-start.4 = ((bf16[8,128,1024]{2,1,0:T(8,128)(2,1)}), bf16[8,128,1024]{2,1,0:T(8,128)(2,1)}, u32[]{:S(2)}, u32[]{:S(2)}) async-start(bf16[8,128,1024]{2,1,0:T(8,128)(2,1)} %reshape.34), calls=%async_computation.4 | async-start | bytes 4194304 | tf_op jit(solution)/shard_map/all_to_all | solution.py:220
  83.5 38.9 %copy-start.3 = (bf16[128,128]{1,0:T(8,128)(2,1)}, bf16[128,128]{1,0:T(8,128)(2,1)S(1)}, u32[]{:S(2)}) copy-start(bf16[128,128]{1,0:T(8,128)(2,1)S(1)} %reduce_sum.34) | copy-start | bytes 98308
  111.4 11.0 %all-to-all-start.3 = ((bf16[8,128,128]{1,2,0:T(8,128)(2,1)}), bf16[8,128,128]{1,2,0:T(8,128)(2,1)S(1)}, u32[]{:S(2)}, u32[]{:S(2)}) async-start(bf16[8,128,128]{1,2,0:T(8,128)(2,1)} %broadcast_in_dim.29), calls=%async_computation.3 | async-start | bytes 524288 | tf_op jit(solution)/shard_map/all_to_all | solution.py:220
  122.4 21.7 %all-to-all-start.1 = ((bf16[16,128,128]{2,1,0:T(8,128)(2,1)}), bf16[16,128,128]{2,1,0:T(8,128)(2,1)S(1)}, u32[]{:S(2)}, u32[]{:S(2)}) async-start(bf16[16,128,128]{2,1,0:T(8,128)(2,1)} %bitcast.9), calls=%async_computation.1 | async-start | bytes 1048576 | tf_op jit(solution)/shard_map/all_to_all | solution.py:220
  144.1 18.8 %all-to-all-start.5 = ((bf16[32,32,128]{2,1,0:T(8,128)(2,1)}), bf16[32,32,128]{2,1,0:T(8,128)(2,1)S(1)}, u32[]{:S(2)}, u32[]{:S(2)}) async-start(bf16[32,32,128]{2,1,0:T(8,128)(2,1)} %bitcast.16), calls=%async_computation.5 | async-start | bytes 524288 | tf_op jit(solution)/shard_map/all_to_all | solution.py:220

commit v2 on v1

v2 whole, which is shorter than its diff:
```python
import math

import jax
import jax.numpy as jnp
from jax import lax
from jax.experimental import pallas as pl
from jax.experimental.pallas import tpu as pltpu
from jax.sharding import Mesh, PartitionSpec as P

HEAD_SIZE = 128
QUERY_HEADS = 8
BLOCK = 64
BLOCKS = 32
NDOC = 8
ROWS = 128
KEYS = 2048
N_CTX = 16
CHUNK = 256
MOST = 1024
SPAN_BLOCKS = MOST // BLOCK + 1
SPAN = SPAN_BLOCKS * BLOCK
GROUP = 4
GROUPS = QUERY_HEADS // GROUP
LANES = GROUP * BLOCK
SCALE = HEAD_SIZE**-0.5
SCALE_LOG2 = SCALE * math.log2(math.e)
MASKED = -1e30
VMEM_LIMIT = 16 * 1024 * 1024
NT = (((1,), (1,)), ((), ()))

CTX = ("yhi", "z")
NEAR = ("x", "core")
FAR = ("ylo", "yhi", "z")


def chunks():
    return [(start, min(CHUNK, SPAN - start)) for start in range(0, SPAN, CHUNK)]


def fold_rows(tile, op):
    return op(tile.reshape(tile.shape[0] // 8, 8, tile.shape[1]), axis=0)


def heads_of(array, half, group):
    rows = slice(half * BLOCK, (half + 1) * BLOCK)
    first = group * GROUP
    return jnp.concatenate(
        [
            array[rows, (first + head) * HEAD_SIZE : (first + head + 1) * HEAD_SIZE]
            for head in range(GROUP)
        ],
        axis=0,
    )


def invert_order(scalars, slots):
    for slot in range(BLOCKS):
        slots[scalars[slot]] = slot


def span_of(scalars, half):
    own = scalars[2 * scalars[BLOCKS + NDOC] + half]
    start, end = jnp.int32(0), jnp.int32(0)
    for doc in range(NDOC):
        end = end + scalars[BLOCKS + doc]
        start = jnp.where(own * BLOCK >= end, end, start)
    return own, start // BLOCK


def slot_of(slots, first, step):
    return slots[jnp.minimum(first + step, BLOCKS - 1)]


def slot_rows(slots, first, step):
    return pl.ds(pl.multiple_of(slot_of(slots, first, step) * BLOCK, BLOCK), BLOCK)


def block_of(kv, part, slots, first, step):
    slot = slot_of(slots, first, step)
    rows = pl.ds(pl.multiple_of((slot % 2) * BLOCK, BLOCK), BLOCK)
    return kv[slot // 2, part, rows, :]


def write_bias(scalars, own, first, bias):
    lane = lax.broadcasted_iota(jnp.int32, (1, HEAD_SIZE), 1)
    high = own * BLOCK + lane % BLOCK
    low, end = jnp.zeros_like(high), jnp.int32(0)
    for doc in range(NDOC):
        end = end + scalars[BLOCKS + doc]
        low = jnp.where(high >= end, end, low)
    for start, size in chunks():
        row = lax.broadcasted_iota(jnp.int32, (size, HEAD_SIZE), 0)
        position = first * BLOCK + start + row
        allowed = (position <= high) & (position >= low)
        bias[start : start + size, :] = jnp.where(allowed, 0.0, MASKED)


def probs_kernel(
    scalars,
    query,
    cotangent,
    kv,
    probs,
    share_out,
    value_part,
    slots,
    keys,
    bias,
    scores,
    parts,
    low_parts,
    done,
):
    invert_order(scalars, slots)
    parts[...] = jnp.zeros_like(parts)
    for half in range(2):
        own, first = span_of(scalars, half)
        for step in range(SPAN_BLOCKS):
            keys[step * BLOCK : (step + 1) * BLOCK, :] = block_of(kv, 0, slots, first, step)
        write_bias(scalars, own, first, bias)
        for group in range(GROUPS):
            tile_index = half * GROUPS + group
            queries = heads_of(query, half, group)
            top = jnp.full((8, LANES), MASKED, jnp.float32)
            for start, size in chunks():
                rows = slice(start, start + size)
                raw = lax.dot_general(
                    keys[rows, :], queries, NT, preferred_element_type=jnp.float32
                )
                add = bias[rows, :]
                tile = raw * SCALE_LOG2 + jnp.concatenate([add, add], axis=1)
                scores[rows, :] = tile
                top = jnp.maximum(top, fold_rows(tile, jnp.max))
            top = jnp.max(top, axis=0, keepdims=True)
            total = jnp.zeros((8, LANES), jnp.float32)
            for start, size in chunks():
                rows = slice(start, start + size)
                tile = jnp.exp2(scores[rows, :] - top)
                probs[tile_index, rows, :] = tile.astype(jnp.bfloat16)
                total = total + fold_rows(tile, jnp.sum)
            share = 1.0 / jnp.sum(total, axis=0, keepdims=True)
            share_out[tile_index] = jnp.broadcast_to(share, (8, LANES))
        gradients = []
        for group in range(GROUPS):
            share = share_out[half * GROUPS + group][:1]
            by_row = jnp.broadcast_to(share, (HEAD_SIZE, LANES)).T
            gradients.append(
                (heads_of(cotangent, half, group).astype(jnp.float32) * by_row).astype(
                    jnp.bfloat16
                )
            )
        for start, size in chunks():
            rows = slice(start, start + size)
            add = sum(
                jnp.dot(
                    probs[half * GROUPS + group, rows, :],
                    gradients[group],
                    preferred_element_type=jnp.float32,
                )
                for group in range(GROUPS)
            )
            for step in range(size // BLOCK):
                target = slot_rows(slots, first, start // BLOCK + step)
                parts[target, :] += add[step * BLOCK : (step + 1) * BLOCK]
    low_parts[...] = parts[...].astype(jnp.bfloat16)
    copy = pltpu.make_async_copy(low_parts, value_part, done)
    copy.start()
    copy.wait()


def grads_kernel(
    scalars,
    query,
    output,
    cotangent,
    kv,
    probs,
    share_in,
    query_grad,
    key_sent,
    key_kept,
    slots,
    keys,
    values,
    key_turned,
    parts,
):
    invert_order(scalars, slots)
    parts[...] = jnp.zeros_like(parts)
    for half in range(2):
        _, first = span_of(scalars, half)
        for step in range(SPAN_BLOCKS):
            rows = slice(step * BLOCK, (step + 1) * BLOCK)
            keys[rows, :] = block_of(kv, 0, slots, first, step)
            values[rows, :] = block_of(kv, 1, slots, first, step)
        key_turned[...] = keys[...].T
        queries, gradients, deltas, shares, turned = [], [], [], [], []
        for group in range(GROUPS):
            queries.append(heads_of(query, half, group))
            gradients.append(heads_of(cotangent, half, group))
            product = gradients[group].astype(jnp.float32) * heads_of(output, half, group).astype(
                jnp.float32
            )
            deltas.append(jnp.sum(product.T, axis=0, keepdims=True))
            shares.append(share_in[half * GROUPS + group][:1])
            turned.append(jnp.zeros((HEAD_SIZE, LANES), jnp.float32))
        for start, size in chunks():
            rows = slice(start, start + size)
            add = 0.0
            for group in range(GROUPS):
                dprobs = lax.dot_general(
                    values[rows, :],
                    gradients[group],
                    NT,
                    preferred_element_type=jnp.float32,
                )
                weight = probs[half * GROUPS + group, rows, :].astype(jnp.float32) * shares[group]
                dscores = (weight * (dprobs - deltas[group])).astype(jnp.bfloat16)
                add = add + jnp.dot(dscores, queries[group], preferred_element_type=jnp.float32)
                turned[group] = turned[group] + jnp.dot(
                    key_turned[:, rows], dscores, preferred_element_type=jnp.float32
                )
            for step in range(size // BLOCK):
                target = slot_rows(slots, first, start // BLOCK + step)
                parts[target, :] += add[step * BLOCK : (step + 1) * BLOCK]
        for group in range(GROUPS):
            by_row = (turned[group] * SCALE).T.astype(jnp.bfloat16)
            for head in range(GROUP):
                column = (group * GROUP + head) * HEAD_SIZE
                query_grad[
                    half * BLOCK : (half + 1) * BLOCK, column : column + HEAD_SIZE
                ] = by_row[head * BLOCK : (head + 1) * BLOCK]
    me = scalars[BLOCKS + NDOC]
    for slot, relative in enumerate((0, 4, 2, 6, 1, 5, 3, 7)):
        for half, part in enumerate((key_kept, key_sent)):
            start = pl.multiple_of((me ^ (half * 8 + relative)) * ROWS, ROWS)
            part[slot] = (parts[pl.ds(start, ROWS), :] * SCALE).astype(part.dtype)


def attention_probs(scalars, query, cotangent, kv):
    return pl.pallas_call(
        probs_kernel,
        in_specs=[pl.BlockSpec(memory_space=pltpu.SMEM)]
        + [pl.BlockSpec(memory_space=pltpu.VMEM)] * 3,
        out_specs=[pl.BlockSpec(memory_space=pltpu.VMEM)] * 2
        + [pl.BlockSpec(memory_space=pltpu.HBM)],
        out_shape=[
            jax.ShapeDtypeStruct((2 * GROUPS, SPAN, LANES), jnp.bfloat16),
            jax.ShapeDtypeStruct((2 * GROUPS, 8, LANES), jnp.float32),
            jax.ShapeDtypeStruct((KEYS, HEAD_SIZE), jnp.bfloat16),
        ],
        scratch_shapes=[
            pltpu.SMEM((BLOCKS,), jnp.int32),
            pltpu.VMEM((SPAN, HEAD_SIZE), jnp.bfloat16),
            pltpu.VMEM((SPAN, HEAD_SIZE), jnp.float32),
            pltpu.VMEM((SPAN, LANES), jnp.float32),
            pltpu.VMEM((KEYS, HEAD_SIZE), jnp.float32),
            pltpu.VMEM((KEYS, HEAD_SIZE), jnp.bfloat16),
            pltpu.SemaphoreType.DMA,
        ],
        compiler_params=pltpu.CompilerParams(vmem_limit_bytes=VMEM_LIMIT),
        name="probs_and_value_part",
    )(scalars, query, cotangent, kv)


def attention_grads(scalars, query, output, cotangent, kv, probs, share):
    return pl.pallas_call(
        grads_kernel,
        in_specs=[pl.BlockSpec(memory_space=pltpu.SMEM)]
        + [pl.BlockSpec(memory_space=pltpu.VMEM)] * 6,
        out_specs=[pl.BlockSpec(memory_space=pltpu.VMEM)] * 3,
        out_shape=[
            jax.ShapeDtypeStruct((ROWS, QUERY_HEADS * HEAD_SIZE), jnp.bfloat16),
            jax.ShapeDtypeStruct((8, ROWS, HEAD_SIZE), jnp.bfloat16),
            jax.ShapeDtypeStruct((8, ROWS, HEAD_SIZE), jnp.float32),
        ],
        scratch_shapes=[
            pltpu.SMEM((BLOCKS,), jnp.int32),
            pltpu.VMEM((SPAN, HEAD_SIZE), jnp.bfloat16),
            pltpu.VMEM((SPAN, HEAD_SIZE), jnp.bfloat16),
            pltpu.VMEM((HEAD_SIZE, SPAN), jnp.bfloat16),
            pltpu.VMEM((KEYS, HEAD_SIZE), jnp.float32),
        ],
        compiler_params=pltpu.CompilerParams(vmem_limit_bytes=VMEM_LIMIT),
        name="query_and_key_part",
    )(scalars, query, output, cotangent, kv, probs, share)


def split_kernel(place, *refs):
    piece, parts = refs[0], refs[1:]
    step = pl.program_id(0)
    for relative in range(4):

        @pl.when(step // 4 == relative)
        def _(relative=relative):
            parts[relative][0] = piece[...]


def split_inputs(place, inputs):
    width = 512

    def source(step, place):
        relative, core, low = step // 4, (step // 2) % 2, step % 2
        near = (place[0] ^ relative) * 2 + (place[1] ^ core)
        return (0, low * 8 + near)

    def target(relative):
        def index(step, place):
            local_step = jnp.clip(step - 4 * relative, 0, 3)
            return (local_step // 2, 0, local_step % 2)

        return index

    return pl.pallas_call(
        split_kernel,
        grid_spec=pltpu.PrefetchScalarGridSpec(
            num_scalar_prefetch=1,
            grid=(16,),
            in_specs=[pl.BlockSpec((ROWS, width), source)],
            out_specs=[pl.BlockSpec((1, ROWS, width), target(r)) for r in range(4)],
        ),
        out_shape=[jax.ShapeDtypeStruct((2, ROWS, 2 * width), jnp.bfloat16)] * 4,
        name="split_inputs",
    )(place, inputs)


def stack_kernel(zero, one, two, three, after, stacked):
    for relative, piece in enumerate((zero, one, two, three)):
        stacked[relative] = piece[1]


def stack_partner(pieces, after):
    return pl.pallas_call(
        stack_kernel,
        in_specs=[pl.BlockSpec(memory_space=pltpu.VMEM)] * 4
        + [pl.BlockSpec(memory_space=pl.ANY)],
        out_specs=pl.BlockSpec(memory_space=pltpu.VMEM),
        out_shape=jax.ShapeDtypeStruct((4,) + pieces[0].shape[1:], jnp.bfloat16),
        compiler_params=pltpu.CompilerParams(vmem_limit_bytes=VMEM_LIMIT),
        name="stack_partner",
    )(*pieces, after)


def fold(kept, received, next_kept, next_sent):
    total = kept[...] + received[...].astype(jnp.float32)
    count = next_kept.shape[0]
    next_kept[...] = total[:count]
    next_sent[...] = total[count:].astype(jnp.bfloat16)


def halves_of(kept):
    half = (kept.shape[0] // 2,) + kept.shape[1:]
    return [
        jax.ShapeDtypeStruct(half, jnp.float32),
        jax.ShapeDtypeStruct(half, jnp.bfloat16),
    ]


def spread_kernel(blocks, kept, received, value_grad, spread, next_kept, next_sent):
    total = blocks[0].astype(jnp.float32)
    for block in range(1, blocks.shape[0]):
        total = total + blocks[block].astype(jnp.float32)
    low = total.astype(jnp.bfloat16)
    value_grad[...] = low
    for copy in range(spread.shape[0]):
        spread[copy] = low
    fold(kept, received, next_kept, next_sent)


def sum_and_spread(blocks, count, kept, received):
    shape = blocks.shape[1:]
    return pl.pallas_call(
        spread_kernel,
        in_specs=[pl.BlockSpec(memory_space=pltpu.VMEM)] * 3,
        out_specs=[pl.BlockSpec(memory_space=pltpu.VMEM)] * 4,
        out_shape=[
            jax.ShapeDtypeStruct(shape, jnp.bfloat16),
            jax.ShapeDtypeStruct((count,) + shape, jnp.bfloat16),
        ]
        + halves_of(kept),
        compiler_params=pltpu.CompilerParams(vmem_limit_bytes=VMEM_LIMIT),
        name="sum_and_spread",
    )(blocks, kept, received)


def join_kernel(key, value, joined, pair, done):
    pair[0] = key[...]
    pair[1] = value[...]
    copies = [
        pltpu.make_async_copy(pair, joined.at[copy], done.at[copy])
        for copy in range(joined.shape[0])
    ]
    for copy in copies:
        copy.start()
    for copy in copies:
        copy.wait()


def join_keys_values(key, value):
    return pl.pallas_call(
        join_kernel,
        in_specs=[pl.BlockSpec(memory_space=pltpu.VMEM)] * 2,
        out_specs=pl.BlockSpec(memory_space=pltpu.HBM),
        out_shape=jax.ShapeDtypeStruct((N_CTX, 2, ROWS, HEAD_SIZE), jnp.bfloat16),
        scratch_shapes=[
            pltpu.VMEM((2, ROWS, HEAD_SIZE), jnp.bfloat16),
            pltpu.SemaphoreType.DMA((N_CTX,)),
        ],
        name="join_keys_values",
    )(key, value)


def weight_kernel(
    place,
    values,
    own,
    one,
    two,
    three,
    partner,
    kept,
    received,
    weight_part,
    next_kept,
    next_sent,
):
    x, core = place[0], place[1]
    total = jnp.zeros((HEAD_SIZE, weight_part.shape[0]), jnp.float32)
    for relative, mine in enumerate((own, one, two, three)):
        near = (x ^ relative) * 2
        lhs = jnp.concatenate([values[near + core].T, values[near + (1 - core)].T], axis=1)
        rhs = jnp.concatenate([mine[0], partner[relative]], axis=0)
        total = total + jnp.dot(lhs, rhs, preferred_element_type=jnp.float32)
    for block in range(weight_part.shape[0] // HEAD_SIZE):
        columns = pl.ds(block * HEAD_SIZE, HEAD_SIZE)
        weight_part[columns, :] = total[:, block * HEAD_SIZE : (block + 1) * HEAD_SIZE].T.astype(
            jnp.bfloat16
        )
    fold(kept, received, next_kept, next_sent)


def weight_product(place, values, pieces, partner, kept, received):
    return pl.pallas_call(
        weight_kernel,
        in_specs=[pl.BlockSpec(memory_space=pltpu.SMEM)]
        + [pl.BlockSpec(memory_space=pltpu.VMEM)] * 8,
        out_specs=[pl.BlockSpec(memory_space=pltpu.VMEM)] * 3,
        out_shape=[jax.ShapeDtypeStruct((pieces[0].shape[2], HEAD_SIZE), jnp.bfloat16)]
        + halves_of(kept),
        compiler_params=pltpu.CompilerParams(vmem_limit_bytes=VMEM_LIMIT),
        name="weight_product",
    )(place, values, *pieces, partner, kept, received)


def exchange(blocks, axes):
    return lax.all_to_all(blocks, axes, 0, 0, tiled=False)


def summed(blocks):
    return jnp.sum(blocks.astype(jnp.float32), axis=0)


def swapped(block, axis, shift):
    count = lax.axis_size(axis)
    return lax.ppermute(block, axis, [(i, i ^ shift) for i in range(count)])


def local(query, key, value, output, output_cotangent, inputs, doc_lengths, block_order):
    scalars = jnp.concatenate(
        [block_order, doc_lengths[0], lax.axis_index(CTX).astype(jnp.int32)[None]]
    )
    place = jnp.stack([lax.axis_index("x"), lax.axis_index("core")]).astype(jnp.int32)
    near_count, far_count = lax.axis_size(NEAR), lax.axis_size(FAR)
    kv = exchange(join_keys_values(key[0], value[0]), CTX)

    parts = split_inputs(place, inputs)
    pieces = [parts[0]] + [swapped(parts[r], "x", r) for r in range(1, 4)]
    probs, share, value_part = attention_probs(scalars, query[0], output_cotangent[0], kv)
    value_blocks = exchange(value_part.reshape(N_CTX, ROWS, HEAD_SIZE), CTX)
    query_grad, key_sent, key_kept = attention_grads(
        scalars, query[0], output[0], output_cotangent[0], kv, probs, share
    )
    partner = swapped(stack_partner(pieces, query_grad), "core", 1)
    value_grad, spread, key_kept, key_sent = sum_and_spread(
        value_blocks, near_count, key_kept, swapped(key_sent, "yhi", 1)
    )
    near_values = exchange(spread, NEAR)
    weight_part, key_kept, key_sent = weight_product(
        place, near_values, pieces, partner, key_kept, swapped(key_sent, "z", 1)
    )
    weight_blocks = exchange(weight_part.reshape(far_count, -1, HEAD_SIZE), FAR)
    key_sum = key_kept + swapped(key_sent, "z", 2).astype(jnp.float32)
    received = swapped(key_sum[1:].astype(jnp.bfloat16), "z", 4)
    key_grad = (key_sum[:1] + received.astype(jnp.float32)).astype(jnp.bfloat16)
    weight_grad = summed(weight_blocks)
    return query_grad[None], key_grad, value_grad[None], weight_grad


def solution(mesh):
    fine = Mesh(
        mesh.devices.reshape(2, 4, 2, 2, 8), ("ylo", "x", "core", "yhi", "z")
    )
    dp = ("ylo", "x", "core")
    tokens = P(dp, CTX, None)
    flat = P(dp + CTX, None)
    return jax.shard_map(
        local,
        mesh=fine,
        in_specs=(tokens,) * 5 + (flat, P(dp, None), P()),
        out_specs=(tokens, tokens, tokens, flat),
        check_vma=False,
    )
```

time: 165 us -> 115 us (0.70)
  waiting for transfers between devices: 86.4 us -> 34.1 us
  starting transfers between devices: 36 us -> 43.4 us
  local copies, waits for them, and re-layouts: 12.7 us -> 7.28 us
  Pallas kernels: 23.4 us -> 25.9 us
  matrix products: 2.03 us -> 0 us
    all_to_all x6 -> x4, waiting for transfers between devices: 86.4 us -> 14.3 us  [exchange(): return lax.all_to_all(blocks, axes, 0, 0, tiled=False)]
    ppermute x0 -> x8, waiting for transfers between devices: none -> 19.7 us  [swapped(): return lax.ppermute(block, axis, [(i, i ^ shift) for i in range(count)])]
    ppermute x0 -> x8, starting transfers between devices: none -> 15 us  [swapped(): return lax.ppermute(block, axis, [(i, i ^ shift) for i in range(count)])]
    all_to_all x6 -> x4, starting transfers between devices: 36 us -> 28.4 us  [exchange(): return lax.all_to_all(blocks, axes, 0, 0, tiled=False)]
    reshape x2 -> x0, local copies, waits for them, and re-layouts: 7.45 us -> none  [the longest x1 4.5 us: local(): by_column_owner.reshape(near_count, ROWS, columns // near_count)]
    unnamed x13 -> x30, local copies, waits for them, and re-layouts: 2.45 us -> 7.27 us
    pallas_call x2 -> x7, Pallas kernels: 23.4 us -> 25.9 us  [the longest x1 10.4 us: split_inputs(): pl.pallas_call(split_kernel, grid_spec=pltpu.PrefetchScalarGridSpec(num_s...]
    dot_general x1 -> x0, matrix products: 2.03 us -> none  [local(): lax.dot_general(near_inputs, near_values, (((0,), (0,)), ((), ())), prefe...]
  transfers between devices with their start and end apart: 6 -> 12, of which waited for: 5 -> 6; matrix products, arithmetic and copies ran while one was open for 8% -> 1% of each run, Pallas kernels for 5% -> 19%
where the time goes in v2:
time: 115 us; the launch traced here: 114 us
  starting transfers between devices  43.4 us (38%)
  waiting for transfers between devices  34.1 us (30%)
  Pallas kernels  25.9 us (23%)
  local copies, waits for them, and re-layouts  7.28 us (6%)
  other arithmetic  2.01 us (2%)
    all_to_all x4, starting transfers between devices, exchange(): return lax.all_to_all(blocks, axes, 0, 0, tiled=False)  28.4 us
    ppermute x8, waiting for transfers between devices, swapped(): return lax.ppermute(block, axis, [(i, i ^ shift) for i in range(count)])  19.7 us
    ppermute x8, starting transfers between devices, swapped(): return lax.ppermute(block, axis, [(i, i ^ shift) for i in range(count)])  15 us
    all_to_all x4, waiting for transfers between devices, exchange(): return lax.all_to_all(blocks, axes, 0, 0, tiled=False)  14.3 us
    pallas_call x1, Pallas kernels, split_inputs(): pl.pallas_call(split_kernel, grid_spec=pltpu.PrefetchScalarGridSpec(num_s...  10.4 us
    unnamed x30, local copies, waits for them, and re-layouts  7.27 us
    pallas_call x1, Pallas kernels, attention_grads(): pl.pallas_call(grads_kernel, in_specs=[pl.BlockSpec(memory_space=pltpu.SM...  4.25 us
    pallas_call x1, Pallas kernels, attention_probs(): pl.pallas_call(probs_kernel, in_specs=[pl.BlockSpec(memory_space=pltpu.SM...  3.39 us
  transfers between devices with their start and end apart: 12, of which 6 were waited for; matrix products, arithmetic and copies ran while one was open for 1% of the time, Pallas kernels for 19%

profile of v2, /device:TPU:32, one launch (start us, length us, event | category | flops | bytes accessed | tf_op | source)
XLA Modules:
  0.0 113.5 jit_solution(5016041416329663747)
XLA Ops:
  0.6 1.9 %join_keys_values.1 = bf16[16,2,128,128]{3,2,1,0:T(8,128)(2,1)} custom-call(bf16[128,128]{1,0:T(8,128)(2,1)} %bitcast.20, bf16[128,128]{1,0:T(8,128)(2,1)} %bitcast.21), custom_call_target="tpu_custom_call" | custom-call | tf_op jit(solution)/shard_map/join_keys_values/pallas_call | solution.py:400
  2.6 11.4 %all-to-all-start = ((bf16[16,2,128,128]{3,2,1,0:T(8,128)(2,1)}), bf16[16,2,128,128]{3,2,1,0:T(8,128)(2,1)S(1)}, u32[]{:S(2)}, u32[]{:S(2)}) async-start(bf16[16,2,128,128]{3,2,1,0:T(8,128)(2,1)} %join_keys_values.1), calls=%async_computation | async-start | bytes 2097152 | tf_op jit(solution)/shard_map/all_to_all | solution.py:456
  13.9 0.6 pad_add_fusion.1.place
  14.6 10.4 %split_inputs.1 = (bf16[2,128,1024]{2,1,0:T(8,128)(2,1)}, bf16[2,128,1024]{2,1,0:T(8,128)(2,1)}, bf16[2,128,1024]{2,1,0:T(8,128)(2,1)}, bf16[2,128,1024]{2,1,0:T(8,128)(2,1)}) custom-call(s32[2]{0:T(128)} %pad_add_fusion.1.place, bf16[128,8192]{1,0:T(8,128)(2,1)} %refs_0_.1), custom_call_target="tpu_custom_call" | custom-call | tf_op jit(solution)/shard_map/split_inputs/pallas_call | solution.py:314
  25.0 1.5 %collective-permute-start.1 = (bf16[2,128,1024]{2,1,0:T(8,128)(2,1)}, bf16[2,128,1024]{2,1,0:T(8,128)(2,1)}, u32[]{:S(2)}, u32[]{:S(2)}) collective-permute-start(bf16[2,128,1024]{2,1,0:T(8,128)(2,1)} %get-tuple-element.29), channel_id=1, source_target_pairs={{0,32},{32,0},{64,96},{96,64},{1,33},{33,1},{65,97},{97,65},{2,34}... | collective-permute-start | bytes 1572872 | tf_op jit(solution)/shard_map/ppermute | solution.py:465
  26.5 2.7 %collective-permute-start.2 = (bf16[2,128,1024]{2,1,0:T(8,128)(2,1)}, bf16[2,128,1024]{2,1,0:T(8,128)(2,1)}, u32[]{:S(2)}, u32[]{:S(2)}) collective-permute-start(bf16[2,128,1024]{2,1,0:T(8,128)(2,1)} %get-tuple-element.30), channel_id=1, source_target_pairs={{0,64},{32,96},{64,0},{96,32},{1,65},{33,97},{65,1},{97,33},{2,66}... | collective-permute-start | bytes 1572872 | tf_op jit(solution)/shard_map/ppermute | solution.py:465
  29.8 11.9 %all-to-all-done.kv = bf16[16,2,128,128]{3,2,1,0:T(8,128)(2,1)S(1)} async-done(((bf16[16,2,128,128]{3,2,1,0:T(8,128)(2,1)}), bf16[16,2,128,128]{3,2,1,0:T(8,128)(2,1)S(1)}, u32[]{:S(2)}, u32[]{:S(2)}) %all-to-all-start) | async-done | bytes 1048608 | tf_op jit(solution)/shard_map/all_to_all | solution.py:456
  41.7 0.9 copy-done.3
  42.6 3.4 %probs_and_value_part.1 = (bf16[4,1088,256]{2,1,0:T(8,128)(2,1)S(1)}, f32[4,8,256]{2,1,0:T(8,128)S(1)}, bf16[2048,128]{1,0:T(8,128)(2,1)S(1)}) custom-call(s32[41]{0:T(128)S(1)} %pad_add_fusion.scalars, bf16[128,1024]{1,0:T(8,128)(2,1)S(1)} %bitcast.13, bf16[128,1024]{1,0:T(8,128)(2,1)S(1)} %bitcast.15, bf16[16,2,128,128]{3,2,1,0:T(8,128)(2,1)S(1)} %all-to-all-done.kv), custom_call_target="tpu_custom_call" | custom-call | tf_op jit(solution)/shard_map/probs_and_value_part/pallas_call | solution.py:241
  46.1 0.8 copy-done.7
  47.5 5.2 %all-to-all-start.1 = ((bf16[16,128,128]{2,1,0:T(8,128)(2,1)}), bf16[16,128,128]{2,1,0:T(8,128)(2,1)}, u32[]{:S(2)}, u32[]{:S(2)}) async-start(bf16[16,128,128]{2,1,0:T(8,128)(2,1)} %bitcast.17), calls=%async_computation.1 | async-start | bytes 1048576 | tf_op jit(solution)/shard_map/all_to_all | solution.py:456
  52.7 1.0 copy-done.4
  53.7 0.9 copy-done.8
  54.7 0.8 copy-done.11
  55.4 4.2 %query_and_key_part.1 = (bf16[128,1024]{1,0:T(8,128)(2,1)}, bf16[8,128,128]{2,1,0:T(8,128)(2,1)S(1)}, f32[8,128,128]{2,1,0:T(8,128)S(1)}) custom-call(s32[41]{0:T(128)S(1)} %pad_add_fusion.scalars, bf16[128,1024]{1,0:T(8,128)(2,1)S(1)} %bitcast.14, bf16[128,1024]{1,0:T(8,128)(2,1)S(1)} %bitcast.18, bf16[128,1024]{1,0:T(8,128)(2,1)S(1)} %bitcast.16, ...), custom_call_target="tpu_custom_call" | custom-call | tf_op jit(solution)/shard_map/query_and_key_part/pallas_call | solution.py:267
  59.7 1.1 copy-done.9
  60.8 1.5 %stack_partner.1 = bf16[4,128,1024]{2,1,0:T(8,128)(2,1)S(1)} custom-call(bf16[2,128,1024]{2,1,0:T(8,128)(2,1)S(1)} %copy-done, bf16[2,128,1024]{2,1,0:T(8,128)(2,1)} %collective-permute-done.1.one, bf16[2,128,1024]{2,1,0:T(8,128)(2,1)} %collective-permute-done.2.two, bf16[2,128,1024]{2,1,0:T(8,128)(2,1)} %collective-permute-done.3.three, ...), custom_call_target="tpu_custom_call" | custom-call | tf_op jit(solution)/shard_map/stack_partner/pallas_call | solution.py:333
  62.4 3.1 %collective-permute-start = (bf16[8,128,128]{2,1,0:T(8,128)(2,1)S(1)}, bf16[8,128,128]{2,1,0:T(8,128)(2,1)S(1)}, u32[]{:S(2)}, u32[]{:S(2)}) collective-permute-start(bf16[8,128,128]{2,1,0:T(8,128)(2,1)S(1)} %get-tuple-element.26), channel_id=1, source_target_pairs={{0,8},{8,0},{1,9},{9,1},{2,10},{10,2},{3,11},{11,3},{4,12},{12,4},... | collective-permute-start | bytes 786440 | tf_op jit(solution)/shard_map/ppermute | solution.py:465
  65.5 7.9 %collective-permute-done.received = bf16[8,128,128]{2,1,0:T(8,128)(2,1)S(1)} collective-permute-done((bf16[8,128,128]{2,1,0:T(8,128)(2,1)S(1)}, bf16[8,128,128]{2,1,0:T(8,128)(2,1)S(1)}, u32[]{:S(2)}, u32[]{:S(2)}) %collective-permute-start) | collective-permute-done | bytes 262176 | tf_op jit(solution)/shard_map/ppermute | solution.py:465
  73.4 1.0 copy-done.6
  74.5 1.9 %sum_and_spread.1 = (bf16[128,128]{1,0:T(8,128)(2,1)}, bf16[8,128,128]{2,1,0:T(8,128)(2,1)}, f32[4,128,128]{2,1,0:T(8,128)S(1)}, bf16[4,128,128]{2,1,0:T(8,128)(2,1)S(1)}) custom-call(bf16[16,128,128]{2,1,0:T(8,128)(2,1)} %all-to-all-done.1.blocks, f32[8,128,128]{2,1,0:T(8,128)S(1)} %copy-done.6, bf16[8,128,128]{2,1,0:T(8,128)(2,1)S(1)} %collective-permute-done.received), custom_call_target="tpu_custom_call" | custom-call | tf_op jit(solution)/shard_map/sum_and_spread/pallas_call | solution.py:372
  76.3 4.3 %all-to-all-start.2 = ((bf16[8,128,128]{2,1,0:T(8,128)(2,1)}), bf16[8,128,128]{2,1,0:T(8,128)(2,1)S(1)}, u32[]{:S(2)}, u32[]{:S(2)}) async-start(bf16[8,128,128]{2,1,0:T(8,128)(2,1)} %get-tuple-element.27), calls=%async_computation.2 | async-start | bytes 524288 | tf_op jit(solution)/shard_map/all_to_all | solution.py:456
  81.2 5.3 %collective-permute-done.5.received = bf16[4,128,128]{2,1,0:T(8,128)(2,1)S(1)} collective-permute-done((bf16[4,128,128]{2,1,0:T(8,128)(2,1)S(1)}, bf16[4,128,128]{2,1,0:T(8,128)(2,1)S(1)}, u32[]{:S(2)}, u32[]{:S(2)}) %collective-permute-start.5) | collective-permute-done | bytes 131104 | tf_op jit(solution)/shard_map/ppermute | solution.py:465
  86.5 1.6 %all-to-all-done.2.values = bf16[8,128,128]{2,1,0:T(8,128)(2,1)S(1)} async-done(((bf16[8,128,128]{2,1,0:T(8,128)(2,1)}), bf16[8,128,128]{2,1,0:T(8,128)(2,1)S(1)}, u32[]{:S(2)}, u32[]{:S(2)}) %all-to-all-start.2) | async-done | bytes 262176 | tf_op jit(solution)/shard_map/all_to_all | solution.py:456
  88.2 2.6 %weight_product.1 = (bf16[1024,128]{1,0:T(8,128)(2,1)}, f32[2,128,128]{2,1,0:T(8,128)S(1)}, bf16[2,128,128]{2,1,0:T(8,128)(2,1)S(1)}) custom-call(s32[2]{0:T(128)S(1)} %copy-done.12, bf16[8,128,128]{2,1,0:T(8,128)(2,1)S(1)} %all-to-all-done.2.values, bf16[2,128,1024]{2,1,0:T(8,128)(2,1)S(1)} %copy-done.1, bf16[2,128,1024]{2,1,0:T(8,128)(2,1)} %collective-permute-done.1.one, ...), custom_call_target="tpu_custom_call" | custom-call | tf_op jit(solution)/shard_map/weight_product/pallas_call | solution.py:443
  90.8 2.0 %collective-permute-start.6 = (bf16[2,128,128]{2,1,0:T(8,128)(2,1)S(1)}, bf16[2,128,128]{2,1,0:T(8,128)(2,1)S(1)}, u32[]{:S(2)}, u32[]{:S(2)}) collective-permute-start(bf16[2,128,128]{2,1,0:T(8,128)(2,1)S(1)} %get-tuple-element.35), channel_id=1, source_target_pairs={{0,2},{1,3},{2,0},{3,1},{4,6},{5,7},{6,4},{7,5},{8,10},{9,11},{10,... | collective-permute-start | bytes 196616 | tf_op jit(solution)/shard_map/ppermute | solution.py:465
  92.8 7.5 %all-to-all-start.3 = ((bf16[32,32,128]{2,1,0:T(8,128)(2,1)}), bf16[32,32,128]{2,1,0:T(8,128)(2,1)S(1)}, u32[]{:S(2)}, u32[]{:S(2)}) async-start(bf16[32,32,128]{2,1,0:T(8,128)(2,1)} %bitcast.12), calls=%async_computation.3 | async-start | bytes 524288 | tf_op jit(solution)/shard_map/all_to_all | solution.py:456
  100.4 4.6 %collective-permute-start.7 = (bf16[1,128,128]{2,1,0:T(8,128)(2,1)S(1)}, bf16[1,128,128]{2,1,0:T(8,128)(2,1)S(1)}, u32[]{:S(2)}, u32[]{:S(2)}) collective-permute-start(bf16[1,128,128]{2,1,0:T(8,128)(2,1)S(1)} %slice.15), channel_id=1, source_target_pairs={{0,4},{1,5},{2,6},{3,7},{4,0},{5,1},{6,2},{7,3},{8,12},{9,13},{10,... | collective-permute-start | bytes 98312 | tf_op jit(solution)/shard_map/ppermute | solution.py:465
  105.0 6.5 %collective-permute-done.7 = bf16[1,128,128]{2,1,0:T(8,128)(2,1)S(1)} collective-permute-done((bf16[1,128,128]{2,1,0:T(8,128)(2,1)S(1)}, bf16[1,128,128]{2,1,0:T(8,128)(2,1)S(1)}, u32[]{:S(2)}, u32[]{:S(2)}) %collective-permute-start.7) | collective-permute-done | bytes 32800 | tf_op jit(solution)/shard_map/ppermute | solution.py:465
  111.4 0.6 fusion
  112.1 0.8 all-to-all-done.3
  112.9 0.7 convert_reduce_fusion
  (35 shorter events, 1.9 us)
Async XLA Ops:
  2.5 27.2 %copy-start.13 = (s32[1,8]{1,0:T(1,128)S(1)}, s32[1,8]{1,0:T(1,128)}, u32[]{:S(2)}) copy-start(s32[1,8]{1,0:T(1,128)} %param.14) | copy-start | bytes 100
  2.5 27.2 %copy-start.14 = (s32[32]{0:T(128)S(1)}, s32[32]{0:T(128)}, u32[]{:S(2)}) copy-start(s32[32]{0:T(128)} %param.15) | copy-start | bytes 388
  2.6 39.1 %copy-start.2 = (bf16[1,128,1024]{2,1,0:T(8,128)(2,1)S(1)}, bf16[1,128,1024]{2,1,0:T(8,128)(2,1)}, u32[]{:S(2)}) copy-start(bf16[1,128,1024]{2,1,0:T(8,128)(2,1)} %param.8) | copy-start | bytes 786436
  2.6 39.1 %all-to-all-start = ((bf16[16,2,128,128]{3,2,1,0:T(8,128)(2,1)}), bf16[16,2,128,128]{3,2,1,0:T(8,128)(2,1)S(1)}, u32[]{:S(2)}, u32[]{:S(2)}) async-start(bf16[16,2,128,128]{3,2,1,0:T(8,128)(2,1)} %join_keys_values.1), calls=%async_computation | async-start | bytes 2097152 | tf_op jit(solution)/shard_map/all_to_all | solution.py:456
  25.0 34.7 %collective-permute-start.1 = (bf16[2,128,1024]{2,1,0:T(8,128)(2,1)}, bf16[2,128,1024]{2,1,0:T(8,128)(2,1)}, u32[]{:S(2)}, u32[]{:S(2)}) collective-permute-start(bf16[2,128,1024]{2,1,0:T(8,128)(2,1)} %get-tuple-element.29), channel_id=1, source_target_pairs={{0,32},{32,0},{64,96},{96,64},{1,33},{33,1},{65,97},{97,65},{2,34}... | collective-permute-start | bytes 1572872 | tf_op jit(solution)/shard_map/ppermute | solution.py:465
  26.5 33.2 %collective-permute-start.2 = (bf16[2,128,1024]{2,1,0:T(8,128)(2,1)}, bf16[2,128,1024]{2,1,0:T(8,128)(2,1)}, u32[]{:S(2)}, u32[]{:S(2)}) collective-permute-start(bf16[2,128,1024]{2,1,0:T(8,128)(2,1)} %get-tuple-element.30), channel_id=1, source_target_pairs={{0,64},{32,96},{64,0},{96,32},{1,65},{33,97},{65,1},{97,33},{2,66}... | collective-permute-start | bytes 1572872 | tf_op jit(solution)/shard_map/ppermute | solution.py:465
  29.2 30.5 %collective-permute-start.3 = (bf16[2,128,1024]{2,1,0:T(8,128)(2,1)}, bf16[2,128,1024]{2,1,0:T(8,128)(2,1)}, u32[]{:S(2)}, u32[]{:S(2)}) collective-permute-start(bf16[2,128,1024]{2,1,0:T(8,128)(2,1)} %get-tuple-element.31), channel_id=1, source_target_pairs={{0,96},{32,64},{64,32},{96,0},{1,97},{33,65},{65,33},{97,1},{2,98}... | collective-permute-start | bytes 1572872 | tf_op jit(solution)/shard_map/ppermute | solution.py:465
  41.7 1.0 copy-start.3
  46.0 0.8 copy-start.7
  46.9 0.6 copy-start.10
  47.5 25.9 %all-to-all-start.1 = ((bf16[16,128,128]{2,1,0:T(8,128)(2,1)}), bf16[16,128,128]{2,1,0:T(8,128)(2,1)}, u32[]{:S(2)}, u32[]{:S(2)}) async-start(bf16[16,128,128]{2,1,0:T(8,128)(2,1)} %bitcast.17), calls=%async_computation.1 | async-start | bytes 1048576 | tf_op jit(solution)/shard_map/all_to_all | solution.py:456
  52.7 7.0 %copy-start = (bf16[2,128,1024]{2,1,0:T(8,128)(2,1)S(1)}, bf16[2,128,1024]{2,1,0:T(8,128)(2,1)}, u32[]{:S(2)}) copy-start(bf16[2,128,1024]{2,1,0:T(8,128)(2,1)} %get-tuple-element.28.zero.own) | copy-start | bytes 1572868
  52.7 1.0 copy-start.4
  53.7 0.9 copy-start.8
  54.7 0.8 copy-start.11
  59.7 2.8 %copy-start.5 = (f32[8,128,128]{2,1,0:T(8,128)}, f32[8,128,128]{2,1,0:T(8,128)S(1)}, u32[]{:S(2)}) copy-start(f32[8,128,128]{2,1,0:T(8,128)S(1)} %get-tuple-element.25.kept) | copy-start | bytes 1572868
  59.7 1.1 copy-start.9
  60.8 27.3 %copy-start.1 = (bf16[2,128,1024]{2,1,0:T(8,128)(2,1)S(1)}, bf16[2,128,1024]{2,1,0:T(8,128)(2,1)}, u32[]{:S(2)}) copy-start(bf16[2,128,1024]{2,1,0:T(8,128)(2,1)} %get-tuple-element.28.zero.own) | copy-start | bytes 1572868
  60.8 27.3 %copy-start.12 = (s32[2]{0:T(128)S(1)}, s32[2]{0:T(128)}, u32[]{:S(2)}) copy-start(s32[2]{0:T(128)} %pad_add_fusion.1.place) | copy-start | bytes 28
  62.3 18.9 %collective-permute-start.4 = (bf16[4,128,1024]{2,1,0:T(8,128)(2,1)S(1)}, bf16[4,128,1024]{2,1,0:T(8,128)(2,1)S(1)}, u32[]{:S(2)}, u32[]{:S(2)}) collective-permute-start(bf16[4,128,1024]{2,1,0:T(8,128)(2,1)S(1)} %stack_partner.1), channel_id=1, source_target_pairs={{0,16},{16,0},{1,17},{17,1},{2,18},{18,2},{3,19},{19,3},{4,20},{20... | collective-permute-start | bytes 3145736 | tf_op jit(solution)/shard_map/ppermute | solution.py:465
  62.4 11.0 %collective-permute-start = (bf16[8,128,128]{2,1,0:T(8,128)(2,1)S(1)}, bf16[8,128,128]{2,1,0:T(8,128)(2,1)S(1)}, u32[]{:S(2)}, u32[]{:S(2)}) collective-permute-start(bf16[8,128,128]{2,1,0:T(8,128)(2,1)S(1)} %get-tuple-element.26), channel_id=1, source_target_pairs={{0,8},{8,0},{1,9},{9,1},{2,10},{10,2},{3,11},{11,3},{4,12},{12,4},... | collective-permute-start | bytes 786440 | tf_op jit(solution)/shard_map/ppermute | solution.py:465
  73.4 1.0 copy-start.6
  76.3 11.8 %all-to-all-start.2 = ((bf16[8,128,128]{2,1,0:T(8,128)(2,1)}), bf16[8,128,128]{2,1,0:T(8,128)(2,1)S(1)}, u32[]{:S(2)}, u32[]{:S(2)}) async-start(bf16[8,128,128]{2,1,0:T(8,128)(2,1)} %get-tuple-element.27), calls=%async_computation.2 | async-start | bytes 524288 | tf_op jit(solution)/shard_map/all_to_all | solution.py:456
  80.6 5.9 %collective-permute-start.5 = (bf16[4,128,128]{2,1,0:T(8,128)(2,1)S(1)}, bf16[4,128,128]{2,1,0:T(8,128)(2,1)S(1)}, u32[]{:S(2)}, u32[]{:S(2)}) collective-permute-start(bf16[4,128,128]{2,1,0:T(8,128)(2,1)S(1)} %get-tuple-element.33), channel_id=1, source_target_pairs={{0,1},{1,0},{2,3},{3,2},{4,5},{5,4},{6,7},{7,6},{8,9},{9,8},{10,11... | collective-permute-start | bytes 393224 | tf_op jit(solution)/shard_map/ppermute | solution.py:465
  90.8 9.6 %collective-permute-start.6 = (bf16[2,128,128]{2,1,0:T(8,128)(2,1)S(1)}, bf16[2,128,128]{2,1,0:T(8,128)(2,1)S(1)}, u32[]{:S(2)}, u32[]{:S(2)}) collective-permute-start(bf16[2,128,128]{2,1,0:T(8,128)(2,1)S(1)} %get-tuple-element.35), channel_id=1, source_target_pairs={{0,2},{1,3},{2,0},{3,1},{4,6},{5,7},{6,4},{7,5},{8,10},{9,11},{10,... | collective-permute-start | bytes 196616 | tf_op jit(solution)/shard_map/ppermute | solution.py:465
  92.8 20.1 %all-to-all-start.3 = ((bf16[32,32,128]{2,1,0:T(8,128)(2,1)}), bf16[32,32,128]{2,1,0:T(8,128)(2,1)S(1)}, u32[]{:S(2)}, u32[]{:S(2)}) async-start(bf16[32,32,128]{2,1,0:T(8,128)(2,1)} %bitcast.12), calls=%async_computation.3 | async-start | bytes 524288 | tf_op jit(solution)/shard_map/all_to_all | solution.py:456
  100.4 11.0 %collective-permute-start.7 = (bf16[1,128,128]{2,1,0:T(8,128)(2,1)S(1)}, bf16[1,128,128]{2,1,0:T(8,128)(2,1)S(1)}, u32[]{:S(2)}, u32[]{:S(2)}) collective-permute-start(bf16[1,128,128]{2,1,0:T(8,128)(2,1)S(1)} %slice.15), channel_id=1, source_target_pairs={{0,4},{1,5},{2,6},{3,7},{4,0},{5,1},{6,2},{7,3},{8,12},{9,13},{10,... | collective-permute-start | bytes 98312 | tf_op jit(solution)/shard_map/ppermute | solution.py:465

commit v3 on v2

v3 whole, which is shorter than its diff:
```python
import math

import jax
import jax.numpy as jnp
from jax import lax
from jax.experimental import pallas as pl
from jax.experimental.pallas import tpu as pltpu
from jax.sharding import Mesh, PartitionSpec as P

HEAD_SIZE = 128
QUERY_HEADS = 8
BLOCK = 64
BLOCKS = 32
NDOC = 8
ROWS = 128
KEYS = 2048
N_CTX = 16
CHUNK = 256
MOST = 1024
SPAN_BLOCKS = MOST // BLOCK + 1
SPAN = SPAN_BLOCKS * BLOCK
GROUP = 4
GROUPS = QUERY_HEADS // GROUP
LANES = GROUP * BLOCK
SCALE = HEAD_SIZE**-0.5
SCALE_LOG2 = SCALE * math.log2(math.e)
MASKED = -1e30
WIDTH = 512
VMEM_LIMIT = 16 * 1024 * 1024
NT = (((1,), (1,)), ((), ()))

CTX = ("yhi", "z")
NEAR = ("x", "core")
FAR = ("ylo", "yhi", "z")


def chunks():
    return [(start, min(CHUNK, SPAN - start)) for start in range(0, SPAN, CHUNK)]


def fold_rows(tile, op):
    return op(tile.reshape(tile.shape[0] // 8, 8, tile.shape[1]), axis=0)


def heads_of(array, half, group):
    rows = slice(half * BLOCK, (half + 1) * BLOCK)
    first = group * GROUP
    return jnp.concatenate(
        [
            array[rows, (first + head) * HEAD_SIZE : (first + head + 1) * HEAD_SIZE]
            for head in range(GROUP)
        ],
        axis=0,
    )


def invert_order(scalars, slots):
    for slot in range(BLOCKS):
        slots[scalars[slot]] = slot


def span_of(scalars, half):
    own = scalars[2 * scalars[BLOCKS + NDOC] + half]
    start, end = jnp.int32(0), jnp.int32(0)
    for doc in range(NDOC):
        end = end + scalars[BLOCKS + doc]
        start = jnp.where(own * BLOCK >= end, end, start)
    return own, start // BLOCK


def slot_of(slots, first, step):
    return slots[jnp.minimum(first + step, BLOCKS - 1)]


def slot_rows(slots, first, step):
    return pl.ds(pl.multiple_of(slot_of(slots, first, step) * BLOCK, BLOCK), BLOCK)


def key_block(kv, slots, first, step):
    slot = slot_of(slots, first, step)
    rows = pl.ds(pl.multiple_of((slot % 2) * BLOCK, BLOCK), BLOCK)
    return kv[slot // 2, rows, :]


def value_block(kv, far_values, slots, first, step, half):
    slot = slot_of(slots, first, step)
    return jnp.where(slot % 2 == half, kv[slot // 2, ROWS:, :], far_values[slot // 2])


def write_bias(scalars, own, first, bias):
    lane = lax.broadcasted_iota(jnp.int32, (1, HEAD_SIZE), 1)
    high = own * BLOCK + lane % BLOCK
    low, end = jnp.zeros_like(high), jnp.int32(0)
    for doc in range(NDOC):
        end = end + scalars[BLOCKS + doc]
        low = jnp.where(high >= end, end, low)
    for start, size in chunks():
        row = lax.broadcasted_iota(jnp.int32, (size, HEAD_SIZE), 0)
        position = first * BLOCK + start + row
        allowed = (position <= high) & (position >= low)
        bias[start : start + size, :] = jnp.where(allowed, 0.0, MASKED)


def probs_kernel(
    scalars,
    query,
    cotangent,
    kv,
    probs,
    value_part,
    slots,
    keys,
    bias,
    scores,
    parts,
    low_parts,
    queries_in,
    gradients_in,
    done,
):
    fetches = [
        pltpu.make_async_copy(query, queries_in, done.at[0]),
        pltpu.make_async_copy(cotangent, gradients_in, done.at[1]),
    ]
    for copy in fetches:
        copy.start()
    invert_order(scalars, slots)
    parts[...] = jnp.zeros_like(parts)
    for half in range(2):
        own, first = span_of(scalars, half)
        for step in range(SPAN_BLOCKS):
            keys[step * BLOCK : (step + 1) * BLOCK, :] = key_block(kv, slots, first, step)
        write_bias(scalars, own, first, bias)
        if half == 0:
            fetches[0].wait()
        shares = []
        for group in range(GROUPS):
            tile_index = half * GROUPS + group
            queries = heads_of(queries_in, half, group)
            top = jnp.full((8, LANES), MASKED, jnp.float32)
            for start, size in chunks():
                rows = slice(start, start + size)
                raw = lax.dot_general(
                    keys[rows, :], queries, NT, preferred_element_type=jnp.float32
                )
                add = bias[rows, :]
                tile = raw * SCALE_LOG2 + jnp.concatenate([add, add], axis=1)
                scores[rows, :] = tile
                top = jnp.maximum(top, fold_rows(tile, jnp.max))
            top = jnp.max(top, axis=0, keepdims=True)
            total = jnp.zeros((8, LANES), jnp.float32)
            for start, size in chunks():
                rows = slice(start, start + size)
                tile = jnp.exp2(scores[rows, :] - top)
                probs[tile_index, rows, :] = tile.astype(jnp.bfloat16)
                total = total + fold_rows(tile, jnp.sum)
            share = 1.0 / jnp.sum(total, axis=0, keepdims=True)
            shares.append(share)
            share = jnp.broadcast_to(share, (8, LANES))
            coarse = share.astype(jnp.bfloat16)
            rest = (share - coarse.astype(jnp.float32)).astype(jnp.bfloat16)
            probs[tile_index, SPAN:, :] = jnp.concatenate([coarse, rest], axis=0)
        if half == 0:
            fetches[1].wait()
        gradients = []
        for group in range(GROUPS):
            by_row = jnp.broadcast_to(shares[group], (HEAD_SIZE, LANES)).T
            gradients.append(
                (heads_of(gradients_in, half, group).astype(jnp.float32) * by_row).astype(
                    jnp.bfloat16
                )
            )
        for start, size in chunks():
            rows = slice(start, start + size)
            add = sum(
                jnp.dot(
                    probs[half * GROUPS + group, rows, :],
                    gradients[group],
                    preferred_element_type=jnp.float32,
                )
                for group in range(GROUPS)
            )
            for step in range(size // BLOCK):
                target = slot_rows(slots, first, start // BLOCK + step)
                parts[target, :] += add[step * BLOCK : (step + 1) * BLOCK]
    low_parts[...] = parts[...].astype(jnp.bfloat16)
    copy = pltpu.make_async_copy(low_parts, value_part, done.at[2])
    copy.start()
    copy.wait()


def grads_kernel(
    scalars,
    query,
    output,
    cotangent,
    kv,
    far_values,
    probs,
    query_grad,
    key_sent,
    key_kept,
    slots,
    keys,
    values,
    key_turned,
    parts,
    queries_in,
    output_in,
    gradients_in,
    done,
):
    fetches = [
        pltpu.make_async_copy(source, target, done.at[index])
        for index, (source, target) in enumerate(
            ((cotangent, gradients_in), (output, output_in), (query, queries_in))
        )
    ]
    for copy in fetches:
        copy.start()
    me = scalars[BLOCKS + NDOC]
    invert_order(scalars, slots)
    parts[...] = jnp.zeros_like(parts)
    for half in range(2):
        _, first = span_of(scalars, half)
        for step in range(SPAN_BLOCKS):
            rows = slice(step * BLOCK, (step + 1) * BLOCK)
            keys[rows, :] = key_block(kv, slots, first, step)
            values[rows, :] = value_block(kv, far_values, slots, first, step, me // 8)
        key_turned[...] = keys[...].T
        if half == 0:
            for copy in fetches:
                copy.wait()
        queries, gradients, deltas, shares, turned = [], [], [], [], []
        for group in range(GROUPS):
            queries.append(heads_of(queries_in, half, group))
            gradients.append(heads_of(gradients_in, half, group))
            forward = heads_of(output_in, half, group).astype(jnp.float32)
            product = gradients[group].astype(jnp.float32) * forward
            deltas.append(jnp.sum(product.T, axis=0, keepdims=True))
            pieces = probs[half * GROUPS + group, SPAN:, :].astype(jnp.float32)
            shares.append(pieces[:1] + pieces[8:9])
            turned.append(jnp.zeros((HEAD_SIZE, LANES), jnp.float32))
        for start, size in chunks():
            rows = slice(start, start + size)
            add = 0.0
            for group in range(GROUPS):
                dprobs = lax.dot_general(
                    values[rows, :],
                    gradients[group],
                    NT,
                    preferred_element_type=jnp.float32,
                )
                weight = probs[half * GROUPS + group, rows, :].astype(jnp.float32) * shares[group]
                dscores = (weight * (dprobs - deltas[group])).astype(jnp.bfloat16)
                add = add + jnp.dot(dscores, queries[group], preferred_element_type=jnp.float32)
                turned[group] = turned[group] + jnp.dot(
                    key_turned[:, rows], dscores, preferred_element_type=jnp.float32
                )
            for step in range(size // BLOCK):
                target = slot_rows(slots, first, start // BLOCK + step)
                parts[target, :] += add[step * BLOCK : (step + 1) * BLOCK]
        for group in range(GROUPS):
            by_row = (turned[group] * SCALE).T.astype(jnp.bfloat16)
            for head in range(GROUP):
                column = (group * GROUP + head) * HEAD_SIZE
                query_grad[
                    half * BLOCK : (half + 1) * BLOCK, column : column + HEAD_SIZE
                ] = by_row[head * BLOCK : (head + 1) * BLOCK]
    for slot, relative in enumerate((0, 7, 2, 5, 1, 6, 3, 4)):
        for half, part in enumerate((key_kept, key_sent)):
            start = pl.multiple_of((me ^ (half * 8 + relative)) * ROWS, ROWS)
            part[slot] = (parts[pl.ds(start, ROWS), :] * SCALE).astype(part.dtype)


def in_vmem(array):
    return pltpu.with_memory_space_constraint(array, pltpu.VMEM)


def in_hbm(array):
    return pltpu.with_memory_space_constraint(array, pltpu.HBM)


VMEM_SPEC = pl.BlockSpec(memory_space=pltpu.VMEM)
HBM_SPEC = pl.BlockSpec(memory_space=pltpu.HBM)
SMEM_SPEC = pl.BlockSpec(memory_space=pltpu.SMEM)
PARAMS = pltpu.CompilerParams(vmem_limit_bytes=VMEM_LIMIT)


def attention_probs(scalars, query, cotangent, kv):
    return pl.pallas_call(
        probs_kernel,
        in_specs=[SMEM_SPEC, HBM_SPEC, HBM_SPEC, VMEM_SPEC],
        out_specs=[VMEM_SPEC, HBM_SPEC],
        out_shape=[
            jax.ShapeDtypeStruct((2 * GROUPS, SPAN + 16, LANES), jnp.bfloat16),
            pltpu.HBM((KEYS, HEAD_SIZE), jnp.bfloat16),
        ],
        scratch_shapes=[
            pltpu.SMEM((BLOCKS,), jnp.int32),
            pltpu.VMEM((SPAN, HEAD_SIZE), jnp.bfloat16),
            pltpu.VMEM((SPAN, HEAD_SIZE), jnp.float32),
            pltpu.VMEM((SPAN, LANES), jnp.float32),
            pltpu.VMEM((KEYS, HEAD_SIZE), jnp.float32),
            pltpu.VMEM((KEYS, HEAD_SIZE), jnp.bfloat16),
            pltpu.VMEM((ROWS, QUERY_HEADS * HEAD_SIZE), jnp.bfloat16),
            pltpu.VMEM((ROWS, QUERY_HEADS * HEAD_SIZE), jnp.bfloat16),
            pltpu.SemaphoreType.DMA((3,)),
        ],
        compiler_params=PARAMS,
        name="probs_and_value_part",
    )(scalars, in_hbm(query), in_hbm(cotangent), kv)


def attention_grads(scalars, query, output, cotangent, kv, far_values, probs):
    return pl.pallas_call(
        grads_kernel,
        in_specs=[SMEM_SPEC] + [HBM_SPEC] * 3 + [VMEM_SPEC] * 3,
        out_specs=[VMEM_SPEC] * 3,
        out_shape=[
            jax.ShapeDtypeStruct((ROWS, QUERY_HEADS * HEAD_SIZE), jnp.bfloat16),
            jax.ShapeDtypeStruct((8, ROWS, HEAD_SIZE), jnp.bfloat16),
            jax.ShapeDtypeStruct((8, ROWS, HEAD_SIZE), jnp.float32),
        ],
        scratch_shapes=[
            pltpu.SMEM((BLOCKS,), jnp.int32),
            pltpu.VMEM((SPAN, HEAD_SIZE), jnp.bfloat16),
            pltpu.VMEM((SPAN, HEAD_SIZE), jnp.bfloat16),
            pltpu.VMEM((HEAD_SIZE, SPAN), jnp.bfloat16),
            pltpu.VMEM((KEYS, HEAD_SIZE), jnp.float32),
            pltpu.VMEM((ROWS, QUERY_HEADS * HEAD_SIZE), jnp.bfloat16),
            pltpu.VMEM((ROWS, QUERY_HEADS * HEAD_SIZE), jnp.bfloat16),
            pltpu.VMEM((ROWS, QUERY_HEADS * HEAD_SIZE), jnp.bfloat16),
            pltpu.SemaphoreType.DMA((3,)),
        ],
        compiler_params=PARAMS,
        name="query_and_key_part",
    )(scalars, *map(in_hbm, (query, output, cotangent)), kv, far_values, probs)


def stack_kernel(zero, one, two, three, after, stacked, staged, done):
    fetches = [
        pltpu.make_async_copy(piece.at[1], staged.at[relative], done.at[relative])
        for relative, piece in enumerate((zero, one, two, three))
    ]
    stores = [
        pltpu.make_async_copy(staged.at[relative], stacked.at[relative], done.at[relative])
        for relative in range(4)
    ]
    for copy in fetches:
        copy.start()
    for copy, store in zip(fetches, stores):
        copy.wait()
        store.start()
    for store in stores:
        store.wait()


def stack_partner(pieces, after):
    shape = (4,) + pieces[0].shape[1:]
    return pl.pallas_call(
        stack_kernel,
        in_specs=[HBM_SPEC] * 5,
        out_specs=HBM_SPEC,
        out_shape=pltpu.HBM(shape, jnp.bfloat16),
        scratch_shapes=[pltpu.VMEM(shape, jnp.bfloat16), pltpu.SemaphoreType.DMA((4,))],
        compiler_params=PARAMS,
        name="stack_partner",
    )(*map(in_hbm, pieces), in_hbm(after))


def load_kernel(zero, one, two, three, partner, sources, done):
    copies = []
    for relative, mine in enumerate((zero, one, two, three)):
        for other, source in enumerate((mine.at[0], partner.at[relative])):
            target = sources.at[relative, pl.ds(other * ROWS, ROWS), :]
            copies.append(pltpu.make_async_copy(source, target, done.at[2 * relative + other]))
    for copy in copies:
        copy.start()
    for copy in copies:
        copy.wait()


def load_inputs(pieces, partner):
    return pl.pallas_call(
        load_kernel,
        in_specs=[HBM_SPEC] * 5,
        out_specs=VMEM_SPEC,
        out_shape=pltpu.VMEM((4, 2 * ROWS, pieces[0].shape[2]), jnp.bfloat16),
        scratch_shapes=[pltpu.SemaphoreType.DMA((8,))],
        compiler_params=PARAMS,
        name="load_inputs",
    )(*map(in_hbm, pieces), in_hbm(partner))


def split_kernel(place, inputs, zero, one, two, three, staged, done):
    x, core = place[0], place[1]
    fetches, stores = [], []
    for relative, part in enumerate((zero, one, two, three)):
        for other in range(2):
            index = 2 * relative + other
            near = (x ^ relative) * 2 + (core ^ other)
            for low in range(2):
                start = pl.multiple_of((low * 8 + near) * WIDTH, WIDTH)
                fetches.append(
                    pltpu.make_async_copy(
                        inputs.at[:, pl.ds(start, WIDTH)],
                        staged.at[index, :, pl.ds(low * WIDTH, WIDTH)],
                        done.at[2 * index + low],
                    )
                )
            stores.append(
                pltpu.make_async_copy(staged.at[index], part.at[other], done.at[2 * index])
            )
    for copy in fetches:
        copy.start()
    for index, store in enumerate(stores):
        fetches[2 * index].wait()
        fetches[2 * index + 1].wait()
        store.start()
    for store in stores:
        store.wait()


def split_inputs(place, inputs):
    return pl.pallas_call(
        split_kernel,
        in_specs=[SMEM_SPEC, HBM_SPEC],
        out_specs=[HBM_SPEC] * 4,
        out_shape=[pltpu.HBM((2, ROWS, 2 * WIDTH), jnp.bfloat16)] * 4,
        scratch_shapes=[
            pltpu.VMEM((8, ROWS, 2 * WIDTH), jnp.bfloat16),
            pltpu.SemaphoreType.DMA((16,)),
        ],
        compiler_params=PARAMS,
        name="split_inputs",
    )(place, in_hbm(inputs))


def fold(kept, received, next_kept, next_sent):
    total = kept[...] + received[...].astype(jnp.float32)
    count = next_kept.shape[0]
    next_kept[...] = total[:count]
    next_sent[...] = total[count:].astype(jnp.bfloat16)


def halves_of(kept):
    half = (kept.shape[0] // 2,) + kept.shape[1:]
    return [
        jax.ShapeDtypeStruct(half, jnp.float32),
        jax.ShapeDtypeStruct(half, jnp.bfloat16),
    ]


def spread_kernel(
    blocks, kept, received, value_grad, spread, next_kept, next_sent, arrived, low, old, done
):
    count = blocks.shape[0]
    fetches = [
        pltpu.make_async_copy(blocks.at[block], arrived.at[block], done.at[block])
        for block in range(count)
    ]
    fetch_old = pltpu.make_async_copy(kept, old, done.at[count])
    for copy in fetches + [fetch_old]:
        copy.start()
    total = 0.0
    for block in range(count):
        fetches[block].wait()
        total = total + arrived[block].astype(jnp.float32)
    low[...] = total.astype(jnp.bfloat16)
    value_grad[...] = low[...]
    stores = [
        pltpu.make_async_copy(low, spread.at[copy], done.at[copy])
        for copy in range(spread.shape[0])
    ]
    for copy in stores:
        copy.start()
    fetch_old.wait()
    fold(old, received, next_kept, next_sent)
    for copy in stores:
        copy.wait()


def sum_and_spread(blocks, count, kept, received):
    shape = blocks.shape[1:]
    return pl.pallas_call(
        spread_kernel,
        in_specs=[HBM_SPEC, HBM_SPEC, VMEM_SPEC],
        out_specs=[VMEM_SPEC, HBM_SPEC, VMEM_SPEC, VMEM_SPEC],
        out_shape=[
            jax.ShapeDtypeStruct(shape, jnp.bfloat16),
            pltpu.HBM((count,) + shape, jnp.bfloat16),
        ]
        + halves_of(kept),
        scratch_shapes=[
            pltpu.VMEM(blocks.shape, jnp.bfloat16),
            pltpu.VMEM(shape, jnp.bfloat16),
            pltpu.VMEM(kept.shape, jnp.float32),
            pltpu.SemaphoreType.DMA((blocks.shape[0] + 1,)),
        ],
        compiler_params=PARAMS,
        name="sum_and_spread",
    )(in_hbm(blocks), in_hbm(kept), received)


def join_kernel(key, value, joined, both, done):
    copies = []
    for half in range(2):
        both[half, :ROWS] = key[...]
        both[half, ROWS:] = value[half * BLOCK : (half + 1) * BLOCK]
        for copy in range(half * N_CTX // 2, (half + 1) * N_CTX // 2):
            copies.append(pltpu.make_async_copy(both.at[half], joined.at[copy], done.at[copy]))
            copies[-1].start()
    for copy in copies:
        copy.wait()


def join_keys_values(key, value):
    return pl.pallas_call(
        join_kernel,
        in_specs=[VMEM_SPEC] * 2,
        out_specs=HBM_SPEC,
        out_shape=pltpu.HBM((N_CTX, ROWS + BLOCK, HEAD_SIZE), jnp.bfloat16),
        scratch_shapes=[
            pltpu.VMEM((2, ROWS + BLOCK, HEAD_SIZE), jnp.bfloat16),
            pltpu.SemaphoreType.DMA((N_CTX,)),
        ],
        name="join_keys_values",
    )(key, value)


def weight_kernel(place, values, sources, kept, received, weight_part, next_kept, next_sent):
    x, core = place[0], place[1]
    total = 0.0
    for relative in range(4):
        near = (x ^ relative) * 2
        lhs = jnp.concatenate([values[near + core].T, values[near + (1 - core)].T], axis=1)
        total = total + jnp.dot(lhs, sources[relative], preferred_element_type=jnp.float32)
    for block in range(weight_part.shape[0] // HEAD_SIZE):
        columns = pl.ds(block * HEAD_SIZE, HEAD_SIZE)
        weight_part[columns, :] = total[:, block * HEAD_SIZE : (block + 1) * HEAD_SIZE].T.astype(
            jnp.bfloat16
        )
    fold(kept, received, next_kept, next_sent)


def weight_product(place, values, sources, kept, received):
    return pl.pallas_call(
        weight_kernel,
        in_specs=[SMEM_SPEC] + [VMEM_SPEC] * 4,
        out_specs=[VMEM_SPEC] * 3,
        out_shape=[jax.ShapeDtypeStruct((2 * WIDTH, HEAD_SIZE), jnp.bfloat16)] + halves_of(kept),
        compiler_params=PARAMS,
        name="weight_product",
    )(place, values, in_vmem(sources), kept, received)


def exchange(blocks, axes):
    return lax.all_to_all(blocks, axes, 0, 0, tiled=False)


def summed(blocks):
    return jnp.sum(blocks.astype(jnp.float32), axis=0)


def swapped(block, axis, shift):
    count = lax.axis_size(axis)
    return lax.ppermute(block, axis, [(i, i ^ shift) for i in range(count)])


def local(query, key, value, output, output_cotangent, inputs, doc_lengths, block_order):
    scalars = jnp.concatenate(
        [block_order, doc_lengths[0], lax.axis_index(CTX).astype(jnp.int32)[None]]
    )
    place = jnp.stack([lax.axis_index("x"), lax.axis_index("core")]).astype(jnp.int32)
    near_count, far_count = lax.axis_size(NEAR), lax.axis_size(FAR)
    kv = exchange(join_keys_values(key[0], value[0]), CTX)
    far_values = swapped(kv[:, ROWS:], "yhi", 1)

    parts = split_inputs(place, inputs)
    pieces = [parts[0]] + [swapped(parts[r], "x", r) for r in range(1, 4)]
    probs, value_part = attention_probs(scalars, query[0], output_cotangent[0], kv)
    value_blocks = exchange(value_part.reshape(N_CTX, ROWS, HEAD_SIZE), CTX)
    query_grad, key_sent, key_kept = attention_grads(
        scalars, query[0], output[0], output_cotangent[0], kv, far_values, probs
    )
    partner = swapped(stack_partner(pieces, key_kept), "core", 1)
    sources = load_inputs(pieces, partner)
    value_grad, spread, key_kept, key_sent = sum_and_spread(
        value_blocks, near_count, key_kept, swapped(key_sent, "yhi", 1)
    )
    near_values = exchange(spread, NEAR)
    weight_part, key_kept, key_sent = weight_product(
        place, near_values, sources, key_kept, swapped(key_sent, "z", 1)
    )
    weight_blocks = exchange(weight_part.reshape(far_count, -1, HEAD_SIZE), FAR)
    key_sum = key_kept + swapped(key_sent, "z", 2).astype(jnp.float32)
    received = swapped(key_sum[1:].astype(jnp.bfloat16), "z", 7)
    key_grad = (key_sum[:1] + received.astype(jnp.float32)).astype(jnp.bfloat16)
    weight_grad = summed(weight_blocks)
    return query_grad[None], key_grad, value_grad[None], weight_grad


def solution(mesh):
    fine = Mesh(
        mesh.devices.reshape(2, 4, 2, 2, 8), ("ylo", "x", "core", "yhi", "z")
    )
    dp = ("ylo", "x", "core")
    tokens = P(dp, CTX, None)
    flat = P(dp + CTX, None)
    return jax.shard_map(
        local,
        mesh=fine,
        in_specs=(tokens,) * 5 + (flat, P(dp, None), P()),
        out_specs=(tokens, tokens, tokens, flat),
        check_vma=False,
    )
```

time: 115 us -> 108 us (0.939)
  local copies, waits for them, and re-layouts: 7.28 us -> 1.53 us
  waiting for transfers between devices: 34.1 us -> 37.1 us
  Pallas kernels: 25.9 us -> 23.4 us
    unnamed x30 -> x6, local copies, waits for them, and re-layouts: 7.27 us -> 0.8 us
    all_to_all x4, waiting for transfers between devices: 14.3 us -> 19.1 us  [exchange(): return lax.all_to_all(blocks, axes, 0, 0, tiled=False)]
    pallas_call x7 -> x8, Pallas kernels: 25.9 us -> 23.4 us  [the longest x1 5.64 us: attention_grads(): pl.pallas_call(grads_kernel, in_specs=[SMEM_SPEC] + [HBM_SPEC] * 3 + [VME...]
    ppermute x8 -> x9, waiting for transfers between devices: 19.7 us -> 18 us  [swapped(): return lax.ppermute(block, axis, [(i, i ^ shift) for i in range(count)])]
    ppermute x8 -> x9, starting transfers between devices: 15 us -> 15.1 us  [swapped(): return lax.ppermute(block, axis, [(i, i ^ shift) for i in range(count)])]
  transfers between devices with their start and end apart: 12 -> 13, of which waited for: 6 -> 6; matrix products, arithmetic and copies ran while one was open for 1% -> 1% of each run, Pallas kernels for 19% -> 18%
where the time goes in v3:
time: 108 us
  starting transfers between devices  43.3 us (40%)
  waiting for transfers between devices  37.1 us (34%)
  Pallas kernels  23.4 us (22%)
  local copies, waits for them, and re-layouts  1.53 us (1%)
  other arithmetic  1.44 us (1%)
    all_to_all x4, starting transfers between devices, exchange(): return lax.all_to_all(blocks, axes, 0, 0, tiled=False)  28.2 us
    all_to_all x4, waiting for transfers between devices, exchange(): return lax.all_to_all(blocks, axes, 0, 0, tiled=False)  19.1 us
    ppermute x9, waiting for transfers between devices, swapped(): return lax.ppermute(block, axis, [(i, i ^ shift) for i in range(count)])  18 us
    ppermute x9, starting transfers between devices, swapped(): return lax.ppermute(block, axis, [(i, i ^ shift) for i in range(count)])  15.1 us
    pallas_call x1, Pallas kernels, attention_grads(): pl.pallas_call(grads_kernel, in_specs=[SMEM_SPEC] + [HBM_SPEC] * 3 + [VME...  5.64 us
    pallas_call x1, Pallas kernels, attention_probs(): pl.pallas_call(probs_kernel, in_specs=[SMEM_SPEC, HBM_SPEC, HBM_SPEC, VME...  5.01 us
    pallas_call x1, Pallas kernels, split_inputs(): pl.pallas_call(split_kernel, in_specs=[SMEM_SPEC, HBM_SPEC], out_specs=[H...  3.13 us
    pallas_call x1, Pallas kernels, sum_and_spread(): pl.pallas_call(spread_kernel, in_specs=[HBM_SPEC, HBM_SPEC, VMEM_SPEC], o...  2.49 us
  transfers between devices with their start and end apart: 13, of which 6 were waited for; matrix products, arithmetic and copies ran while one was open for 1% of the time, Pallas kernels for 18%

profile of v3, /device:TPU:32, one launch (start us, length us, event | category | flops | bytes accessed | tf_op | source)
XLA Modules:
  0.0 107.5 jit_solution(7508971763544256194)
XLA Ops:
  0.6 1.8 %join_keys_values.1 = bf16[16,192,128]{2,1,0:T(8,128)(2,1)} custom-call(bf16[128,128]{1,0:T(8,128)(2,1)} %bitcast.19, bf16[128,128]{1,0:T(8,128)(2,1)} %bitcast.20), custom_call_target="tpu_custom_call" | custom-call | tf_op jit(solution)/shard_map/join_keys_values/pallas_call | solution.py:519
  2.5 11.2 %all-to-all-start = ((bf16[16,192,128]{2,1,0:T(8,128)(2,1)}), bf16[16,192,128]{2,1,0:T(8,128)(2,1)S(1)}, u32[]{:S(2)}, u32[]{:S(2)}) async-start(bf16[16,192,128]{2,1,0:T(8,128)(2,1)} %join_keys_values.1), calls=%async_computation | async-start | bytes 1572864 | tf_op jit(solution)/shard_map/all_to_all | solution.py:559
  13.8 3.1 %split_inputs.1 = (bf16[2,128,1024]{2,1,0:T(8,128)(2,1)}, bf16[2,128,1024]{2,1,0:T(8,128)(2,1)}, bf16[2,128,1024]{2,1,0:T(8,128)(2,1)}, bf16[2,128,1024]{2,1,0:T(8,128)(2,1)}) custom-call(s32[2]{0:T(128)S(1)} %pad_add_fusion.1.place, bf16[128,8192]{1,0:T(8,128)(2,1)} %inputs.1), custom_call_target="tpu_custom_call" | custom-call | tf_op jit(solution)/shard_map/split_inputs/pallas_call | solution.py:426
  16.9 1.6 %collective-permute-start.2 = (bf16[2,128,1024]{2,1,0:T(8,128)(2,1)}, bf16[2,128,1024]{2,1,0:T(8,128)(2,1)}, u32[]{:S(2)}, u32[]{:S(2)}) collective-permute-start(bf16[2,128,1024]{2,1,0:T(8,128)(2,1)} %get-tuple-element.27), channel_id=1, source_target_pairs={{0,32},{32,0},{64,96},{96,64},{1,33},{33,1},{65,97},{97,65},{2,34}... | collective-permute-start | bytes 1572872 | tf_op jit(solution)/shard_map/ppermute | solution.py:568
  18.5 2.7 %collective-permute-start.3 = (bf16[2,128,1024]{2,1,0:T(8,128)(2,1)}, bf16[2,128,1024]{2,1,0:T(8,128)(2,1)}, u32[]{:S(2)}, u32[]{:S(2)}) collective-permute-start(bf16[2,128,1024]{2,1,0:T(8,128)(2,1)} %get-tuple-element.28), channel_id=1, source_target_pairs={{0,64},{32,96},{64,0},{96,32},{1,65},{33,97},{65,1},{97,33},{2,66}... | collective-permute-start | bytes 1572872 | tf_op jit(solution)/shard_map/ppermute | solution.py:568
  21.2 0.5 collective-permute-start.4
  21.7 14.3 %all-to-all-done.kv = bf16[16,192,128]{2,1,0:T(8,128)(2,1)S(1)} async-done(((bf16[16,192,128]{2,1,0:T(8,128)(2,1)}), bf16[16,192,128]{2,1,0:T(8,128)(2,1)S(1)}, u32[]{:S(2)}, u32[]{:S(2)}) %all-to-all-start) | async-done | bytes 786464 | tf_op jit(solution)/shard_map/all_to_all | solution.py:559
  36.0 0.7 slice.13
  36.7 1.3 %collective-permute-start = (bf16[16,64,128]{2,1,0:T(8,128)(2,1)}, bf16[16,64,128]{2,1,0:T(8,128)(2,1)S(1)}, u32[]{:S(2)}, u32[]{:S(2)}) collective-permute-start(bf16[16,64,128]{2,1,0:T(8,128)(2,1)} %slice.13), channel_id=1, source_target_pairs={{0,8},{8,0},{1,9},{9,1},{2,10},{10,2},{3,11},{11,3},{4,12},{12,4},... | collective-permute-start | bytes 786440 | tf_op jit(solution)/shard_map/ppermute | solution.py:568
  38.0 0.1 pad_add_fusion.scalars
  38.1 5.0 %probs_and_value_part.1 = (bf16[4,1104,256]{2,1,0:T(8,128)(2,1)S(1)}, bf16[2048,128]{1,0:T(8,128)(2,1)}) custom-call(s32[41]{0:T(128)S(1)} %pad_add_fusion.scalars, bf16[128,1024]{1,0:T(8,128)(2,1)} %bitcast.13, bf16[128,1024]{1,0:T(8,128)(2,1)} %bitcast.15, bf16[16,192,128]{2,1,0:T(8,128)(2,1)S(1)} %all-to-all-done.kv), custom_call_target="tpu_custom_call" | custom-call | tf_op jit(solution)/shard_map/probs_and_value_part/pallas_call | solution.py:291
  43.1 5.4 %all-to-all-start.1 = ((bf16[16,128,128]{2,1,0:T(8,128)(2,1)}), bf16[16,128,128]{2,1,0:T(8,128)(2,1)}, u32[]{:S(2)}, u32[]{:S(2)}) async-start(bf16[16,128,128]{2,1,0:T(8,128)(2,1)} %bitcast.17), calls=%async_computation.1 | async-start | bytes 1048576 | tf_op jit(solution)/shard_map/all_to_all | solution.py:559
  48.5 5.6 %query_and_key_part.1 = (bf16[128,1024]{1,0:T(8,128)(2,1)}, bf16[8,128,128]{2,1,0:T(8,128)(2,1)S(1)}, f32[8,128,128]{2,1,0:T(8,128)S(1)}) custom-call(s32[41]{0:T(128)S(1)} %pad_add_fusion.scalars, bf16[128,1024]{1,0:T(8,128)(2,1)} %bitcast.14, bf16[128,1024]{1,0:T(8,128)(2,1)} %bitcast.18, bf16[128,1024]{1,0:T(8,128)(2,1)} %bitcast.16, ...), custom_call_target="tpu_custom_call" | custom-call | tf_op jit(solution)/shard_map/query_and_key_part/pallas_call | solution.py:316
  54.2 0.8 copy-done
  55.0 2.0 %stack_partner.1 = bf16[4,128,1024]{2,1,0:T(8,128)(2,1)} custom-call(bf16[2,128,1024]{2,1,0:T(8,128)(2,1)} %get-tuple-element.26.zero, bf16[2,128,1024]{2,1,0:T(8,128)(2,1)} %collective-permute-done.2.one, bf16[2,128,1024]{2,1,0:T(8,128)(2,1)} %collective-permute-done.3.two, bf16[2,128,1024]{2,1,0:T(8,128)(2,1)} %collective-permute-done.4.three, ...), custom_call_target="tpu_custom_call" | custom-call | tf_op jit(solution)/shard_map/stack_partner/pallas_call | solution.py:361
  56.9 0.1 collective-permute-start.5
  57.0 3.1 %collective-permute-start.1 = (bf16[8,128,128]{2,1,0:T(8,128)(2,1)S(1)}, bf16[8,128,128]{2,1,0:T(8,128)(2,1)S(1)}, u32[]{:S(2)}, u32[]{:S(2)}) collective-permute-start(bf16[8,128,128]{2,1,0:T(8,128)(2,1)S(1)} %get-tuple-element.24), channel_id=1, source_target_pairs={{0,8},{8,0},{1,9},{9,1},{2,10},{10,2},{3,11},{11,3},{4,12},{12,4},... | collective-permute-start | bytes 786440 | tf_op jit(solution)/shard_map/ppermute | solution.py:568
  60.1 8.3 %collective-permute-done.1.received = bf16[8,128,128]{2,1,0:T(8,128)(2,1)S(1)} collective-permute-done((bf16[8,128,128]{2,1,0:T(8,128)(2,1)S(1)}, bf16[8,128,128]{2,1,0:T(8,128)(2,1)S(1)}, u32[]{:S(2)}, u32[]{:S(2)}) %collective-permute-start.1) | collective-permute-done | bytes 262176 | tf_op jit(solution)/shard_map/ppermute | solution.py:568
  68.4 2.5 %sum_and_spread.1 = (bf16[128,128]{1,0:T(8,128)(2,1)}, bf16[8,128,128]{2,1,0:T(8,128)(2,1)}, f32[4,128,128]{2,1,0:T(8,128)S(1)}, bf16[4,128,128]{2,1,0:T(8,128)(2,1)S(1)}) custom-call(bf16[16,128,128]{2,1,0:T(8,128)(2,1)} %all-to-all-done.1.blocks, f32[8,128,128]{2,1,0:T(8,128)} %copy-done, bf16[8,128,128]{2,1,0:T(8,128)(2,1)S(1)} %collective-permute-done.1.received), custom_call_target="tpu_custom_call" | custom-call | tf_op jit(solution)/shard_map/sum_and_spread/pallas_call | solution.py:486
  70.9 4.3 %all-to-all-start.2 = ((bf16[8,128,128]{2,1,0:T(8,128)(2,1)}), bf16[8,128,128]{2,1,0:T(8,128)(2,1)S(1)}, u32[]{:S(2)}, u32[]{:S(2)}) async-start(bf16[8,128,128]{2,1,0:T(8,128)(2,1)} %get-tuple-element.25), calls=%async_computation.2 | async-start | bytes 524288 | tf_op jit(solution)/shard_map/all_to_all | solution.py:559
  75.2 0.3 collective-permute-start.6
  75.5 1.6 %load_inputs.1.sources = bf16[4,256,1024]{2,1,0:T(8,128)(2,1)S(1)} custom-call(bf16[2,128,1024]{2,1,0:T(8,128)(2,1)} %get-tuple-element.26.zero, bf16[2,128,1024]{2,1,0:T(8,128)(2,1)} %collective-permute-done.2.one, bf16[2,128,1024]{2,1,0:T(8,128)(2,1)} %collective-permute-done.3.two, bf16[2,128,1024]{2,1,0:T(8,128)(2,1)} %collective-permute-done.4.three, ...), custom_call_target="tpu_custom_call" | custom-call | tf_op jit(solution)/shard_map/load_inputs/pallas_call | solution.py:385
  77.1 4.0 %collective-permute-done.6.received = bf16[4,128,128]{2,1,0:T(8,128)(2,1)S(1)} collective-permute-done((bf16[4,128,128]{2,1,0:T(8,128)(2,1)S(1)}, bf16[4,128,128]{2,1,0:T(8,128)(2,1)S(1)}, u32[]{:S(2)}, u32[]{:S(2)}) %collective-permute-start.6) | collective-permute-done | bytes 131104 | tf_op jit(solution)/shard_map/ppermute | solution.py:568
  81.1 1.6 %all-to-all-done.2.values = bf16[8,128,128]{2,1,0:T(8,128)(2,1)S(1)} async-done(((bf16[8,128,128]{2,1,0:T(8,128)(2,1)}), bf16[8,128,128]{2,1,0:T(8,128)(2,1)S(1)}, u32[]{:S(2)}, u32[]{:S(2)}) %all-to-all-start.2) | async-done | bytes 262176 | tf_op jit(solution)/shard_map/all_to_all | solution.py:559
  82.7 1.8 %weight_product.1 = (bf16[1024,128]{1,0:T(8,128)(2,1)}, f32[2,128,128]{2,1,0:T(8,128)S(1)}, bf16[2,128,128]{2,1,0:T(8,128)(2,1)S(1)}) custom-call(s32[2]{0:T(128)S(1)} %pad_add_fusion.1.place, bf16[8,128,128]{2,1,0:T(8,128)(2,1)S(1)} %all-to-all-done.2.values, bf16[4,256,1024]{2,1,0:T(8,128)(2,1)S(1)} %load_inputs.1.sources, ...), custom_call_target="tpu_custom_call" | custom-call | tf_op jit(solution)/shard_map/weight_product/pallas_call | solution.py:548
  84.5 1.9 %collective-permute-start.7 = (bf16[2,128,128]{2,1,0:T(8,128)(2,1)S(1)}, bf16[2,128,128]{2,1,0:T(8,128)(2,1)S(1)}, u32[]{:S(2)}, u32[]{:S(2)}) collective-permute-start(bf16[2,128,128]{2,1,0:T(8,128)(2,1)S(1)} %get-tuple-element.33), channel_id=1, source_target_pairs={{0,2},{1,3},{2,0},{3,1},{4,6},{5,7},{6,4},{7,5},{8,10},{9,11},{10,... | collective-permute-start | bytes 196616 | tf_op jit(solution)/shard_map/ppermute | solution.py:568
  86.5 7.3 %all-to-all-start.3 = ((bf16[32,32,128]{2,1,0:T(8,128)(2,1)}), bf16[32,32,128]{2,1,0:T(8,128)(2,1)S(1)}, u32[]{:S(2)}, u32[]{:S(2)}) async-start(bf16[32,32,128]{2,1,0:T(8,128)(2,1)} %bitcast.12), calls=%async_computation.3 | async-start | bytes 524288 | tf_op jit(solution)/shard_map/all_to_all | solution.py:559
  93.8 3.7 %collective-permute-start.8 = (bf16[1,128,128]{2,1,0:T(8,128)(2,1)S(1)}, bf16[1,128,128]{2,1,0:T(8,128)(2,1)S(1)}, u32[]{:S(2)}, u32[]{:S(2)}) collective-permute-start(bf16[1,128,128]{2,1,0:T(8,128)(2,1)S(1)} %slice.20), channel_id=1, source_target_pairs={{0,7},{1,6},{2,5},{3,4},{4,3},{5,2},{6,1},{7,0},{8,15},{9,14},{10,... | collective-permute-start | bytes 98312 | tf_op jit(solution)/shard_map/ppermute | solution.py:568
  97.5 5.6 %collective-permute-done.8 = bf16[1,128,128]{2,1,0:T(8,128)(2,1)S(1)} collective-permute-done((bf16[1,128,128]{2,1,0:T(8,128)(2,1)S(1)}, bf16[1,128,128]{2,1,0:T(8,128)(2,1)S(1)}, u32[]{:S(2)}, u32[]{:S(2)}) %collective-permute-start.8) | collective-permute-done | bytes 32800 | tf_op jit(solution)/shard_map/ppermute | solution.py:568
  103.0 0.6 fusion
  103.7 3.2 %all-to-all-done.3 = bf16[32,32,128]{2,1,0:T(8,128)(2,1)S(1)} async-done(((bf16[32,32,128]{2,1,0:T(8,128)(2,1)}), bf16[32,32,128]{2,1,0:T(8,128)(2,1)S(1)}, u32[]{:S(2)}, u32[]{:S(2)}) %all-to-all-start.3) | async-done | bytes 262176 | tf_op jit(solution)/shard_map/all_to_all | solution.py:559
  106.9 0.7 convert_reduce_fusion
  (15 shorter events, 0.1 us)
Async XLA Ops:
  2.5 35.5 %copy-start.1 = (s32[1,8]{1,0:T(1,128)S(1)}, s32[1,8]{1,0:T(1,128)}, u32[]{:S(2)}) copy-start(s32[1,8]{1,0:T(1,128)} %param.14) | copy-start | bytes 100
  2.5 35.5 %copy-start.2 = (s32[32]{0:T(128)S(1)}, s32[32]{0:T(128)}, u32[]{:S(2)}) copy-start(s32[32]{0:T(128)} %param.15) | copy-start | bytes 388
  2.5 33.5 %all-to-all-start = ((bf16[16,192,128]{2,1,0:T(8,128)(2,1)}), bf16[16,192,128]{2,1,0:T(8,128)(2,1)S(1)}, u32[]{:S(2)}, u32[]{:S(2)}) async-start(bf16[16,192,128]{2,1,0:T(8,128)(2,1)} %join_keys_values.1), calls=%async_computation | async-start | bytes 1572864 | tf_op jit(solution)/shard_map/all_to_all | solution.py:559
  16.9 38.0 %collective-permute-start.2 = (bf16[2,128,1024]{2,1,0:T(8,128)(2,1)}, bf16[2,128,1024]{2,1,0:T(8,128)(2,1)}, u32[]{:S(2)}, u32[]{:S(2)}) collective-permute-start(bf16[2,128,1024]{2,1,0:T(8,128)(2,1)} %get-tuple-element.27), channel_id=1, source_target_pairs={{0,32},{32,0},{64,96},{96,64},{1,33},{33,1},{65,97},{97,65},{2,34}... | collective-permute-start | bytes 1572872 | tf_op jit(solution)/shard_map/ppermute | solution.py:568
  18.5 36.5 %collective-permute-start.3 = (bf16[2,128,1024]{2,1,0:T(8,128)(2,1)}, bf16[2,128,1024]{2,1,0:T(8,128)(2,1)}, u32[]{:S(2)}, u32[]{:S(2)}) collective-permute-start(bf16[2,128,1024]{2,1,0:T(8,128)(2,1)} %get-tuple-element.28), channel_id=1, source_target_pairs={{0,64},{32,96},{64,0},{96,32},{1,65},{33,97},{65,1},{97,33},{2,66}... | collective-permute-start | bytes 1572872 | tf_op jit(solution)/shard_map/ppermute | solution.py:568
  21.2 33.7 %collective-permute-start.4 = (bf16[2,128,1024]{2,1,0:T(8,128)(2,1)}, bf16[2,128,1024]{2,1,0:T(8,128)(2,1)}, u32[]{:S(2)}, u32[]{:S(2)}) collective-permute-start(bf16[2,128,1024]{2,1,0:T(8,128)(2,1)} %get-tuple-element.29), channel_id=1, source_target_pairs={{0,96},{32,64},{64,32},{96,0},{1,97},{33,65},{65,33},{97,1},{2,98}... | collective-permute-start | bytes 1572872 | tf_op jit(solution)/shard_map/ppermute | solution.py:568
  36.7 11.8 %collective-permute-start = (bf16[16,64,128]{2,1,0:T(8,128)(2,1)}, bf16[16,64,128]{2,1,0:T(8,128)(2,1)S(1)}, u32[]{:S(2)}, u32[]{:S(2)}) collective-permute-start(bf16[16,64,128]{2,1,0:T(8,128)(2,1)} %slice.13), channel_id=1, source_target_pairs={{0,8},{8,0},{1,9},{9,1},{2,10},{10,2},{3,11},{11,3},{4,12},{12,4},... | collective-permute-start | bytes 786440 | tf_op jit(solution)/shard_map/ppermute | solution.py:568
  43.1 25.3 %all-to-all-start.1 = ((bf16[16,128,128]{2,1,0:T(8,128)(2,1)}), bf16[16,128,128]{2,1,0:T(8,128)(2,1)}, u32[]{:S(2)}, u32[]{:S(2)}) async-start(bf16[16,128,128]{2,1,0:T(8,128)(2,1)} %bitcast.17), calls=%async_computation.1 | async-start | bytes 1048576 | tf_op jit(solution)/shard_map/all_to_all | solution.py:559
  54.1 0.8 copy-start
  56.9 18.6 %collective-permute-start.5 = (bf16[4,128,1024]{2,1,0:T(8,128)(2,1)}, bf16[4,128,1024]{2,1,0:T(8,128)(2,1)}, u32[]{:S(2)}, u32[]{:S(2)}) collective-permute-start(bf16[4,128,1024]{2,1,0:T(8,128)(2,1)} %stack_partner.1), channel_id=1, source_target_pairs={{0,16},{16,0},{1,17},{17,1},{2,18},{18,2},{3,19},{19,3},{4,20},{20... | collective-permute-start | bytes 3145736 | tf_op jit(solution)/shard_map/ppermute | solution.py:568
  57.0 11.4 %collective-permute-start.1 = (bf16[8,128,128]{2,1,0:T(8,128)(2,1)S(1)}, bf16[8,128,128]{2,1,0:T(8,128)(2,1)S(1)}, u32[]{:S(2)}, u32[]{:S(2)}) collective-permute-start(bf16[8,128,128]{2,1,0:T(8,128)(2,1)S(1)} %get-tuple-element.24), channel_id=1, source_target_pairs={{0,8},{8,0},{1,9},{9,1},{2,10},{10,2},{3,11},{11,3},{4,12},{12,4},... | collective-permute-start | bytes 786440 | tf_op jit(solution)/shard_map/ppermute | solution.py:568
  70.9 11.9 %all-to-all-start.2 = ((bf16[8,128,128]{2,1,0:T(8,128)(2,1)}), bf16[8,128,128]{2,1,0:T(8,128)(2,1)S(1)}, u32[]{:S(2)}, u32[]{:S(2)}) async-start(bf16[8,128,128]{2,1,0:T(8,128)(2,1)} %get-tuple-element.25), calls=%async_computation.2 | async-start | bytes 524288 | tf_op jit(solution)/shard_map/all_to_all | solution.py:559
  75.2 5.9 %collective-permute-start.6 = (bf16[4,128,128]{2,1,0:T(8,128)(2,1)S(1)}, bf16[4,128,128]{2,1,0:T(8,128)(2,1)S(1)}, u32[]{:S(2)}, u32[]{:S(2)}) collective-permute-start(bf16[4,128,128]{2,1,0:T(8,128)(2,1)S(1)} %get-tuple-element.31), channel_id=1, source_target_pairs={{0,1},{1,0},{2,3},{3,2},{4,5},{5,4},{6,7},{7,6},{8,9},{9,8},{10,11... | collective-permute-start | bytes 393224 | tf_op jit(solution)/shard_map/ppermute | solution.py:568
  84.5 9.2 %collective-permute-start.7 = (bf16[2,128,128]{2,1,0:T(8,128)(2,1)S(1)}, bf16[2,128,128]{2,1,0:T(8,128)(2,1)S(1)}, u32[]{:S(2)}, u32[]{:S(2)}) collective-permute-start(bf16[2,128,128]{2,1,0:T(8,128)(2,1)S(1)} %get-tuple-element.33), channel_id=1, source_target_pairs={{0,2},{1,3},{2,0},{3,1},{4,6},{5,7},{6,4},{7,5},{8,10},{9,11},{10,... | collective-permute-start | bytes 196616 | tf_op jit(solution)/shard_map/ppermute | solution.py:568
  86.5 20.4 %all-to-all-start.3 = ((bf16[32,32,128]{2,1,0:T(8,128)(2,1)}), bf16[32,32,128]{2,1,0:T(8,128)(2,1)S(1)}, u32[]{:S(2)}, u32[]{:S(2)}) async-start(bf16[32,32,128]{2,1,0:T(8,128)(2,1)} %bitcast.12), calls=%async_computation.3 | async-start | bytes 524288 | tf_op jit(solution)/shard_map/all_to_all | solution.py:559
  93.8 9.2 %collective-permute-start.8 = (bf16[1,128,128]{2,1,0:T(8,128)(2,1)S(1)}, bf16[1,128,128]{2,1,0:T(8,128)(2,1)S(1)}, u32[]{:S(2)}, u32[]{:S(2)}) collective-permute-start(bf16[1,128,128]{2,1,0:T(8,128)(2,1)S(1)} %slice.20), channel_id=1, source_target_pairs={{0,7},{1,6},{2,5},{3,4},{4,3},{5,2},{6,1},{7,0},{8,15},{9,14},{10,... | collective-permute-start | bytes 98312 | tf_op jit(solution)/shard_map/ppermute | solution.py:568

commit v4 on v3

--- a/solution.py
+++ b/solution.py
@@ -183,10 +183,18 @@
             for step in range(size // BLOCK):
                 target = slot_rows(slots, first, start // BLOCK + step)
                 parts[target, :] += add[step * BLOCK : (step + 1) * BLOCK]
-    low_parts[...] = parts[...].astype(jnp.bfloat16)
-    copy = pltpu.make_async_copy(low_parts, value_part, done.at[2])
-    copy.start()
-    copy.wait()
+    copies = []
+    for piece in range(4):
+        rows = pl.ds(piece * KEYS // 4, KEYS // 4)
+        low_parts[rows, :] = parts[rows, :].astype(jnp.bfloat16)
+        copies.append(
+            pltpu.make_async_copy(
+                low_parts.at[rows, :], value_part.at[rows, :], done.at[2 + piece]
+            )
+        )
+        copies[-1].start()
+    for copy in copies:
+        copy.wait()
 
 
 def grads_kernel(
@@ -197,17 +205,24 @@
     kv,
     far_values,
     probs,
-    query_grad,
+    zero,
+    one,
+    two,
+    three,
     key_sent,
     key_kept,
+    stacked,
+    dscores_out,
+    keys_out,
     slots,
     keys,
     values,
-    key_turned,
     parts,
     queries_in,
     output_in,
     gradients_in,
+    staged,
+    kept,
     done,
 ):
     fetches = [
@@ -216,7 +231,15 @@
             ((cotangent, gradients_in), (output, output_in), (query, queries_in))
         )
     ]
-    for copy in fetches:
+    stacks = [
+        pltpu.make_async_copy(piece.at[1], staged.at[relative], done.at[3 + relative])
+        for relative, piece in enumerate((zero, one, two, three))
+    ]
+    stores = [
+        pltpu.make_async_copy(staged.at[relative], stacked.at[relative], done.at[3 + relative])
+        for relative in range(4)
+    ]
+    for copy in fetches + stacks:
         copy.start()
     me = scalars[BLOCKS + NDOC]
     invert_order(scalars, slots)
@@ -227,11 +250,11 @@
             rows = slice(step * BLOCK, (step + 1) * BLOCK)
             keys[rows, :] = key_block(kv, slots, first, step)
             values[rows, :] = value_block(kv, far_values, slots, first, step, me // 8)
-        key_turned[...] = keys[...].T
+        keys_out[half] = keys[...]
         if half == 0:
             for copy in fetches:
                 copy.wait()
-        queries, gradients, deltas, shares, turned = [], [], [], [], []
+        queries, gradients, deltas, shares = [], [], [], []
         for group in range(GROUPS):
             queries.append(heads_of(queries_in, half, group))
             gradients.append(heads_of(gradients_in, half, group))
@@ -240,7 +263,6 @@
             deltas.append(jnp.sum(product.T, axis=0, keepdims=True))
             pieces = probs[half * GROUPS + group, SPAN:, :].astype(jnp.float32)
             shares.append(pieces[:1] + pieces[8:9])
-            turned.append(jnp.zeros((HEAD_SIZE, LANES), jnp.float32))
         for start, size in chunks():
             rows = slice(start, start + size)
             add = 0.0
@@ -254,23 +276,57 @@
                 weight = probs[half * GROUPS + group, rows, :].astype(jnp.float32) * shares[group]
                 dscores = (weight * (dprobs - deltas[group])).astype(jnp.bfloat16)
                 add = add + jnp.dot(dscores, queries[group], preferred_element_type=jnp.float32)
-                turned[group] = turned[group] + jnp.dot(
-                    key_turned[:, rows], dscores, preferred_element_type=jnp.float32
-                )
+                dscores_out[half * GROUPS + group, rows, :] = dscores
             for step in range(size // BLOCK):
                 target = slot_rows(slots, first, start // BLOCK + step)
                 parts[target, :] += add[step * BLOCK : (step + 1) * BLOCK]
+        if half == 0:
+            for copy, store in zip(stacks, stores):
+                copy.wait()
+                store.start()
+    keep = pltpu.make_async_copy(kept, key_kept, done.at[7])
+    for half, part in enumerate((kept, key_sent)):
+        for slot, relative in enumerate((0, 7, 2, 5, 1, 6, 3, 4)):
+            start = pl.multiple_of((me ^ (half * 8 + relative)) * ROWS, ROWS)
+            part[slot] = (parts[pl.ds(start, ROWS), :] * SCALE).astype(part.dtype)
+        if half == 0:
+            keep.start()
+    for copy in stores + [keep]:
+        copy.wait()
+
+
+def query_kernel(keys, dscores, query_grad, key_turned, staged, done):
+    for half in range(2):
+        key_turned[...] = keys[half].T
         for group in range(GROUPS):
-            by_row = (turned[group] * SCALE).T.astype(jnp.bfloat16)
+            turned = jnp.dot(
+                key_turned[...], dscores[half * GROUPS + group], preferred_element_type=jnp.float32
+            )
+            by_row = (turned * SCALE).T.astype(jnp.bfloat16)
             for head in range(GROUP):
                 column = (group * GROUP + head) * HEAD_SIZE
-                query_grad[
+                staged[
                     half * BLOCK : (half + 1) * BLOCK, column : column + HEAD_SIZE
                 ] = by_row[head * BLOCK : (head + 1) * BLOCK]
-    for slot, relative in enumerate((0, 7, 2, 5, 1, 6, 3, 4)):
-        for half, part in enumerate((key_kept, key_sent)):
-            start = pl.multiple_of((me ^ (half * 8 + relative)) * ROWS, ROWS)
-            part[slot] = (parts[pl.ds(start, ROWS), :] * SCALE).astype(part.dtype)
+    copy = pltpu.make_async_copy(staged, query_grad, done)
+    copy.start()
+    copy.wait()
+
+
+def query_product(keys, dscores):
+    return pl.pallas_call(
+        query_kernel,
+        in_specs=[VMEM_SPEC] * 2,
+        out_specs=HBM_SPEC,
+        out_shape=pltpu.HBM((ROWS, QUERY_HEADS * HEAD_SIZE), jnp.bfloat16),
+        scratch_shapes=[
+            pltpu.VMEM((HEAD_SIZE, SPAN), jnp.bfloat16),
+            pltpu.VMEM((ROWS, QUERY_HEADS * HEAD_SIZE), jnp.bfloat16),
+            pltpu.SemaphoreType.DMA,
+        ],
+        compiler_params=PARAMS,
+        name="query_product",
+    )(keys, dscores)
 
 
 def in_vmem(array):
@@ -305,68 +361,40 @@
             pltpu.VMEM((KEYS, HEAD_SIZE), jnp.bfloat16),
             pltpu.VMEM((ROWS, QUERY_HEADS * HEAD_SIZE), jnp.bfloat16),
             pltpu.VMEM((ROWS, QUERY_HEADS * HEAD_SIZE), jnp.bfloat16),
-            pltpu.SemaphoreType.DMA((3,)),
+            pltpu.SemaphoreType.DMA((6,)),
         ],
         compiler_params=PARAMS,
         name="probs_and_value_part",
     )(scalars, in_hbm(query), in_hbm(cotangent), kv)
 
 
-def attention_grads(scalars, query, output, cotangent, kv, far_values, probs):
+def attention_grads(scalars, query, output, cotangent, kv, far_values, probs, pieces):
     return pl.pallas_call(
         grads_kernel,
-        in_specs=[SMEM_SPEC] + [HBM_SPEC] * 3 + [VMEM_SPEC] * 3,
-        out_specs=[VMEM_SPEC] * 3,
+        in_specs=[SMEM_SPEC] + [HBM_SPEC] * 3 + [VMEM_SPEC] * 3 + [HBM_SPEC] * 4,
+        out_specs=[VMEM_SPEC] + [HBM_SPEC] * 2 + [VMEM_SPEC] * 2,
         out_shape=[
-            jax.ShapeDtypeStruct((ROWS, QUERY_HEADS * HEAD_SIZE), jnp.bfloat16),
             jax.ShapeDtypeStruct((8, ROWS, HEAD_SIZE), jnp.bfloat16),
-            jax.ShapeDtypeStruct((8, ROWS, HEAD_SIZE), jnp.float32),
+            pltpu.HBM((8, ROWS, HEAD_SIZE), jnp.bfloat16),
+            pltpu.HBM((4,) + pieces[0].shape[1:], jnp.bfloat16),
+            jax.ShapeDtypeStruct((2 * GROUPS, SPAN, LANES), jnp.bfloat16),
+            jax.ShapeDtypeStruct((2, SPAN, HEAD_SIZE), jnp.bfloat16),
         ],
         scratch_shapes=[
             pltpu.SMEM((BLOCKS,), jnp.int32),
             pltpu.VMEM((SPAN, HEAD_SIZE), jnp.bfloat16),
             pltpu.VMEM((SPAN, HEAD_SIZE), jnp.bfloat16),
-            pltpu.VMEM((HEAD_SIZE, SPAN), jnp.bfloat16),
             pltpu.VMEM((KEYS, HEAD_SIZE), jnp.float32),
             pltpu.VMEM((ROWS, QUERY_HEADS * HEAD_SIZE), jnp.bfloat16),
             pltpu.VMEM((ROWS, QUERY_HEADS * HEAD_SIZE), jnp.bfloat16),
             pltpu.VMEM((ROWS, QUERY_HEADS * HEAD_SIZE), jnp.bfloat16),
-            pltpu.SemaphoreType.DMA((3,)),
+            pltpu.VMEM((4,) + pieces[0].shape[1:], jnp.bfloat16),
+            pltpu.VMEM((8, ROWS, HEAD_SIZE), jnp.bfloat16),
+            pltpu.SemaphoreType.DMA((8,)),
         ],
         compiler_params=PARAMS,
-        name="query_and_key_part",
-    )(scalars, *map(in_hbm, (query, output, cotangent)), kv, far_values, probs)
-
-
-def stack_kernel(zero, one, two, three, after, stacked, staged, done):
-    fetches = [
-        pltpu.make_async_copy(piece.at[1], staged.at[relative], done.at[relative])
-        for relative, piece in enumerate((zero, one, two, three))
-    ]
-    stores = [
-        pltpu.make_async_copy(staged.at[relative], stacked.at[relative], done.at[relative])
-        for relative in range(4)
-    ]
-    for copy in fetches:
-        copy.start()
-    for copy, store in zip(fetches, stores):
-        copy.wait()
-        store.start()
-    for store in stores:
-        store.wait()
-
-
-def stack_partner(pieces, after):
-    shape = (4,) + pieces[0].shape[1:]
-    return pl.pallas_call(
-        stack_kernel,
-        in_specs=[HBM_SPEC] * 5,
-        out_specs=HBM_SPEC,
-        out_shape=pltpu.HBM(shape, jnp.bfloat16),
-        scratch_shapes=[pltpu.VMEM(shape, jnp.bfloat16), pltpu.SemaphoreType.DMA((4,))],
-        compiler_params=PARAMS,
-        name="stack_partner",
-    )(*map(in_hbm, pieces), in_hbm(after))
+        name="key_part",
+    )(scalars, *map(in_hbm, (query, output, cotangent)), kv, far_values, probs, *map(in_hbm, pieces))
 
 
 def load_kernel(zero, one, two, three, partner, sources, done):
@@ -438,7 +466,7 @@
 
 
 def fold(kept, received, next_kept, next_sent):
-    total = kept[...] + received[...].astype(jnp.float32)
+    total = kept[...].astype(jnp.float32) + received[...].astype(jnp.float32)
     count = next_kept.shape[0]
     next_kept[...] = total[:count]
     next_sent[...] = total[count:].astype(jnp.bfloat16)
@@ -453,7 +481,7 @@
 
 
 def spread_kernel(
-    blocks, kept, received, value_grad, spread, next_kept, next_sent, arrived, low, old, done
+    blocks, kept, received, after, value_grad, spread, next_kept, next_sent, arrived, low, old, done
 ):
     count = blocks.shape[0]
     fetches = [
@@ -481,11 +509,11 @@
         copy.wait()
 
 
-def sum_and_spread(blocks, count, kept, received):
+def sum_and_spread(blocks, count, kept, received, after):
     shape = blocks.shape[1:]
     return pl.pallas_call(
         spread_kernel,
-        in_specs=[HBM_SPEC, HBM_SPEC, VMEM_SPEC],
+        in_specs=[HBM_SPEC, HBM_SPEC, VMEM_SPEC, HBM_SPEC],
         out_specs=[VMEM_SPEC, HBM_SPEC, VMEM_SPEC, VMEM_SPEC],
         out_shape=[
             jax.ShapeDtypeStruct(shape, jnp.bfloat16),
@@ -495,12 +523,12 @@
         scratch_shapes=[
             pltpu.VMEM(blocks.shape, jnp.bfloat16),
             pltpu.VMEM(shape, jnp.bfloat16),
-            pltpu.VMEM(kept.shape, jnp.float32),
+            pltpu.VMEM(kept.shape, jnp.bfloat16),
             pltpu.SemaphoreType.DMA((blocks.shape[0] + 1,)),
         ],
         compiler_params=PARAMS,
         name="sum_and_spread",
-    )(in_hbm(blocks), in_hbm(kept), received)
+    )(in_hbm(blocks), in_hbm(kept), received, in_hbm(after))
 
 
 def join_kernel(key, value, joined, both, done):
@@ -581,13 +609,14 @@
     pieces = [parts[0]] + [swapped(parts[r], "x", r) for r in range(1, 4)]
     probs, value_part = attention_probs(scalars, query[0], output_cotangent[0], kv)
     value_blocks = exchange(value_part.reshape(N_CTX, ROWS, HEAD_SIZE), CTX)
-    query_grad, key_sent, key_kept = attention_grads(
-        scalars, query[0], output[0], output_cotangent[0], kv, far_values, probs
+    key_sent, key_kept, stacked, dscores, reached = attention_grads(
+        scalars, query[0], output[0], output_cotangent[0], kv, far_values, probs, pieces
     )
-    partner = swapped(stack_partner(pieces, key_kept), "core", 1)
+    query_grad = query_product(reached, dscores)
+    partner = swapped(stacked, "core", 1)
     sources = load_inputs(pieces, partner)
     value_grad, spread, key_kept, key_sent = sum_and_spread(
-        value_blocks, near_count, key_kept, swapped(key_sent, "yhi", 1)
+        value_blocks, near_count, key_kept, swapped(key_sent, "yhi", 1), query_grad
     )
     near_values = exchange(spread, NEAR)
     weight_part, key_kept, key_sent = weight_product(

time: 108 us -> 106 us (0.981)
  Pallas kernels: 23.4 us -> 22.1 us
where the time goes in v4:
time: 106 us; the launch traced here: 105 us
  starting transfers between devices  43.3 us (41%)
  waiting for transfers between devices  36.9 us (35%)
  Pallas kernels  22.1 us (21%)
  other arithmetic  1.44 us (1%)
    all_to_all x4, starting transfers between devices, exchange(): return lax.all_to_all(blocks, axes, 0, 0, tiled=False)  28.1 us
    all_to_all x4, waiting for transfers between devices, exchange(): return lax.all_to_all(blocks, axes, 0, 0, tiled=False)  19.1 us
    ppermute x9, waiting for transfers between devices, swapped(): return lax.ppermute(block, axis, [(i, i ^ shift) for i in range(count)])  17.8 us
    ppermute x9, starting transfers between devices, swapped(): return lax.ppermute(block, axis, [(i, i ^ shift) for i in range(count)])  15.2 us
    pallas_call x1, Pallas kernels, attention_probs(): pl.pallas_call(probs_kernel, in_specs=[SMEM_SPEC, HBM_SPEC, HBM_SPEC, VME...  5.02 us
    pallas_call x1, Pallas kernels, attention_grads(): pl.pallas_call(grads_kernel, in_specs=[SMEM_SPEC] + [HBM_SPEC] * 3 + [VME...  4.96 us
    pallas_call x1, Pallas kernels, split_inputs(): pl.pallas_call(split_kernel, in_specs=[SMEM_SPEC, HBM_SPEC], out_specs=[H...  3.13 us
    pallas_call x1, Pallas kernels, sum_and_spread(): pl.pallas_call(spread_kernel, in_specs=[HBM_SPEC, HBM_SPEC, VMEM_SPEC, HB...  2.49 us
  transfers between devices with their start and end apart: 13, of which 6 were waited for; matrix products, arithmetic and copies ran while one was open for 1% of the time, Pallas kernels for 18%

profile of v4, /device:TPU:32, one launch (start us, length us, event | category | flops | bytes accessed | tf_op | source)
XLA Modules:
  0.0 105.2 jit_solution(7629220526923748549)
XLA Ops:
  0.6 1.8 %join_keys_values.1 = bf16[16,192,128]{2,1,0:T(8,128)(2,1)} custom-call(bf16[128,128]{1,0:T(8,128)(2,1)} %bitcast.20, bf16[128,128]{1,0:T(8,128)(2,1)} %bitcast.21), custom_call_target="tpu_custom_call" | custom-call | tf_op jit(solution)/shard_map/join_keys_values/pallas_call | solution.py:547
  2.5 11.2 %all-to-all-start = ((bf16[16,192,128]{2,1,0:T(8,128)(2,1)}), bf16[16,192,128]{2,1,0:T(8,128)(2,1)S(1)}, u32[]{:S(2)}, u32[]{:S(2)}) async-start(bf16[16,192,128]{2,1,0:T(8,128)(2,1)} %join_keys_values.1), calls=%async_computation | async-start | bytes 1572864 | tf_op jit(solution)/shard_map/all_to_all | solution.py:587
  13.7 0.1 pad_add_fusion.1.place
  13.8 3.1 %split_inputs.1 = (bf16[2,128,1024]{2,1,0:T(8,128)(2,1)}, bf16[2,128,1024]{2,1,0:T(8,128)(2,1)}, bf16[2,128,1024]{2,1,0:T(8,128)(2,1)}, bf16[2,128,1024]{2,1,0:T(8,128)(2,1)}) custom-call(s32[2]{0:T(128)S(1)} %pad_add_fusion.1.place, bf16[128,8192]{1,0:T(8,128)(2,1)} %inputs.1), custom_call_target="tpu_custom_call" | custom-call | tf_op jit(solution)/shard_map/split_inputs/pallas_call | solution.py:454
  16.9 1.6 %collective-permute-start.1 = (bf16[2,128,1024]{2,1,0:T(8,128)(2,1)}, bf16[2,128,1024]{2,1,0:T(8,128)(2,1)}, u32[]{:S(2)}, u32[]{:S(2)}) collective-permute-start(bf16[2,128,1024]{2,1,0:T(8,128)(2,1)} %get-tuple-element.24), channel_id=1, source_target_pairs={{0,32},{32,0},{64,96},{96,64},{1,33},{33,1},{65,97},{97,65},{2,34}... | collective-permute-start | bytes 1572872 | tf_op jit(solution)/shard_map/ppermute | solution.py:596
  18.5 2.7 %collective-permute-start.2 = (bf16[2,128,1024]{2,1,0:T(8,128)(2,1)}, bf16[2,128,1024]{2,1,0:T(8,128)(2,1)}, u32[]{:S(2)}, u32[]{:S(2)}) collective-permute-start(bf16[2,128,1024]{2,1,0:T(8,128)(2,1)} %get-tuple-element.25), channel_id=1, source_target_pairs={{0,64},{32,96},{64,0},{96,32},{1,65},{33,97},{65,1},{97,33},{2,66}... | collective-permute-start | bytes 1572872 | tf_op jit(solution)/shard_map/ppermute | solution.py:596
  21.2 0.5 collective-permute-start.3
  21.7 14.3 %all-to-all-done.kv = bf16[16,192,128]{2,1,0:T(8,128)(2,1)S(1)} async-done(((bf16[16,192,128]{2,1,0:T(8,128)(2,1)}), bf16[16,192,128]{2,1,0:T(8,128)(2,1)S(1)}, u32[]{:S(2)}, u32[]{:S(2)}) %all-to-all-start) | async-done | bytes 786464 | tf_op jit(solution)/shard_map/all_to_all | solution.py:587
  36.0 0.7 slice.13
  36.7 1.3 %collective-permute-start = (bf16[16,64,128]{2,1,0:T(8,128)(2,1)}, bf16[16,64,128]{2,1,0:T(8,128)(2,1)S(1)}, u32[]{:S(2)}, u32[]{:S(2)}) collective-permute-start(bf16[16,64,128]{2,1,0:T(8,128)(2,1)} %slice.13), channel_id=1, source_target_pairs={{0,8},{8,0},{1,9},{9,1},{2,10},{10,2},{3,11},{11,3},{4,12},{12,4},... | collective-permute-start | bytes 786440 | tf_op jit(solution)/shard_map/ppermute | solution.py:596
  38.0 0.1 pad_add_fusion.scalars
  38.1 5.0 %probs_and_value_part.1 = (bf16[4,1104,256]{2,1,0:T(8,128)(2,1)S(1)}, bf16[2048,128]{1,0:T(8,128)(2,1)}) custom-call(s32[41]{0:T(128)S(1)} %pad_add_fusion.scalars, bf16[128,1024]{1,0:T(8,128)(2,1)} %bitcast.13, bf16[128,1024]{1,0:T(8,128)(2,1)} %bitcast.15, bf16[16,192,128]{2,1,0:T(8,128)(2,1)S(1)} %all-to-all-done.kv), custom_call_target="tpu_custom_call" | custom-call | tf_op jit(solution)/shard_map/probs_and_value_part/pallas_call | solution.py:347
  43.1 5.4 %all-to-all-start.1 = ((bf16[16,128,128]{2,1,0:T(8,128)(2,1)}), bf16[16,128,128]{2,1,0:T(8,128)(2,1)}, u32[]{:S(2)}, u32[]{:S(2)}) async-start(bf16[16,128,128]{2,1,0:T(8,128)(2,1)} %bitcast.18), calls=%async_computation.1 | async-start | bytes 1048576 | tf_op jit(solution)/shard_map/all_to_all | solution.py:587
  48.5 5.0 %key_part.1 = (bf16[8,128,128]{2,1,0:T(8,128)(2,1)S(1)}, bf16[8,128,128]{2,1,0:T(8,128)(2,1)}, bf16[4,128,1024]{2,1,0:T(8,128)(2,1)}, bf16[4,1088,256]{2,1,0:T(8,128)(2,1)S(1)}, bf16[2,1088,128]{2,1,0:T(8,128)(2,1)S(1)}) custom-call(s32[41]{0:T(128)S(1)} %pad_add_fusion.scalars, bf16[128,1024]{1,0:T(8,128)(2,1)} %bitcast.14, bf16[128,1024]{1,0:T(8,128)(2,1)} %bitcast.19, ...), custom_call_target="tpu_custom_call" | custom-call | tf_op jit(solution)/shard_map/key_part/pallas_call | solution.py:372
  53.5 0.1 collective-permute-start.5
  53.6 3.1 %collective-permute-start.4 = (bf16[8,128,128]{2,1,0:T(8,128)(2,1)S(1)}, bf16[8,128,128]{2,1,0:T(8,128)(2,1)S(1)}, u32[]{:S(2)}, u32[]{:S(2)}) collective-permute-start(bf16[8,128,128]{2,1,0:T(8,128)(2,1)S(1)} %get-tuple-element.31), channel_id=1, source_target_pairs={{0,8},{8,0},{1,9},{9,1},{2,10},{10,2},{3,11},{11,3},{4,12},{12,4},... | collective-permute-start | bytes 786440 | tf_op jit(solution)/shard_map/ppermute | solution.py:596
  56.6 1.3 %query_product.1.after = bf16[128,1024]{1,0:T(8,128)(2,1)} custom-call(bf16[2,1088,128]{2,1,0:T(8,128)(2,1)S(1)} %get-tuple-element.27.keys, bf16[4,1088,256]{2,1,0:T(8,128)(2,1)S(1)} %get-tuple-element.28.dscores), custom_call_target="tpu_custom_call" | custom-call | tf_op jit(solution)/shard_map/query_product/pallas_call | solution.py:317
  58.0 8.4 %collective-permute-done.4.received = bf16[8,128,128]{2,1,0:T(8,128)(2,1)S(1)} collective-permute-done((bf16[8,128,128]{2,1,0:T(8,128)(2,1)S(1)}, bf16[8,128,128]{2,1,0:T(8,128)(2,1)S(1)}, u32[]{:S(2)}, u32[]{:S(2)}) %collective-permute-start.4) | collective-permute-done | bytes 262176 | tf_op jit(solution)/shard_map/ppermute | solution.py:596
  66.4 2.5 %sum_and_spread.1 = (bf16[128,128]{1,0:T(8,128)(2,1)}, bf16[8,128,128]{2,1,0:T(8,128)(2,1)}, f32[4,128,128]{2,1,0:T(8,128)S(1)}, bf16[4,128,128]{2,1,0:T(8,128)(2,1)S(1)}) custom-call(bf16[16,128,128]{2,1,0:T(8,128)(2,1)} %all-to-all-done.1.blocks, bf16[8,128,128]{2,1,0:T(8,128)(2,1)} %get-tuple-element.30.kept, ...), custom_call_target="tpu_custom_call" | custom-call | tf_op jit(solution)/shard_map/sum_and_spread/pallas_call | solution.py:514
  68.9 4.3 %all-to-all-start.2 = ((bf16[8,128,128]{2,1,0:T(8,128)(2,1)}), bf16[8,128,128]{2,1,0:T(8,128)(2,1)S(1)}, u32[]{:S(2)}, u32[]{:S(2)}) async-start(bf16[8,128,128]{2,1,0:T(8,128)(2,1)} %get-tuple-element.32), calls=%async_computation.2 | async-start | bytes 524288 | tf_op jit(solution)/shard_map/all_to_all | solution.py:587
  73.2 0.5 collective-permute-start.6
  73.7 1.6 %load_inputs.1.sources = bf16[4,256,1024]{2,1,0:T(8,128)(2,1)S(1)} custom-call(bf16[2,128,1024]{2,1,0:T(8,128)(2,1)} %get-tuple-element.23.zero, bf16[2,128,1024]{2,1,0:T(8,128)(2,1)} %collective-permute-done.1.one, bf16[2,128,1024]{2,1,0:T(8,128)(2,1)} %collective-permute-done.2.two, bf16[2,128,1024]{2,1,0:T(8,128)(2,1)} %collective-permute-done.3.three, ...), custom_call_target="tpu_custom_call" | custom-call | tf_op jit(solution)/shard_map/load_inputs/pallas_call | solution.py:413
  75.3 3.8 %collective-permute-done.6.received = bf16[4,128,128]{2,1,0:T(8,128)(2,1)S(1)} collective-permute-done((bf16[4,128,128]{2,1,0:T(8,128)(2,1)S(1)}, bf16[4,128,128]{2,1,0:T(8,128)(2,1)S(1)}, u32[]{:S(2)}, u32[]{:S(2)}) %collective-permute-start.6) | collective-permute-done | bytes 131104 | tf_op jit(solution)/shard_map/ppermute | solution.py:596
  79.1 1.6 %all-to-all-done.2.values = bf16[8,128,128]{2,1,0:T(8,128)(2,1)S(1)} async-done(((bf16[8,128,128]{2,1,0:T(8,128)(2,1)}), bf16[8,128,128]{2,1,0:T(8,128)(2,1)S(1)}, u32[]{:S(2)}, u32[]{:S(2)}) %all-to-all-start.2) | async-done | bytes 262176 | tf_op jit(solution)/shard_map/all_to_all | solution.py:587
  80.7 1.8 %weight_product.1 = (bf16[1024,128]{1,0:T(8,128)(2,1)}, f32[2,128,128]{2,1,0:T(8,128)S(1)}, bf16[2,128,128]{2,1,0:T(8,128)(2,1)S(1)}) custom-call(s32[2]{0:T(128)S(1)} %pad_add_fusion.1.place, bf16[8,128,128]{2,1,0:T(8,128)(2,1)S(1)} %all-to-all-done.2.values, bf16[4,256,1024]{2,1,0:T(8,128)(2,1)S(1)} %load_inputs.1.sources, ...), custom_call_target="tpu_custom_call" | custom-call | tf_op jit(solution)/shard_map/weight_product/pallas_call | solution.py:576
  82.5 1.8 %collective-permute-start.7 = (bf16[2,128,128]{2,1,0:T(8,128)(2,1)S(1)}, bf16[2,128,128]{2,1,0:T(8,128)(2,1)S(1)}, u32[]{:S(2)}, u32[]{:S(2)}) collective-permute-start(bf16[2,128,128]{2,1,0:T(8,128)(2,1)S(1)} %get-tuple-element.37), channel_id=1, source_target_pairs={{0,2},{1,3},{2,0},{3,1},{4,6},{5,7},{6,4},{7,5},{8,10},{9,11},{10,... | collective-permute-start | bytes 196616 | tf_op jit(solution)/shard_map/ppermute | solution.py:596
  84.3 7.1 %all-to-all-start.3 = ((bf16[32,32,128]{2,1,0:T(8,128)(2,1)}), bf16[32,32,128]{2,1,0:T(8,128)(2,1)S(1)}, u32[]{:S(2)}, u32[]{:S(2)}) async-start(bf16[32,32,128]{2,1,0:T(8,128)(2,1)} %bitcast.12), calls=%async_computation.3 | async-start | bytes 524288 | tf_op jit(solution)/shard_map/all_to_all | solution.py:587
  91.5 3.7 %collective-permute-start.8 = (bf16[1,128,128]{2,1,0:T(8,128)(2,1)S(1)}, bf16[1,128,128]{2,1,0:T(8,128)(2,1)S(1)}, u32[]{:S(2)}, u32[]{:S(2)}) collective-permute-start(bf16[1,128,128]{2,1,0:T(8,128)(2,1)S(1)} %slice.20), channel_id=1, source_target_pairs={{0,7},{1,6},{2,5},{3,4},{4,3},{5,2},{6,1},{7,0},{8,15},{9,14},{10,... | collective-permute-start | bytes 98312 | tf_op jit(solution)/shard_map/ppermute | solution.py:596
  95.2 5.6 %collective-permute-done.8 = bf16[1,128,128]{2,1,0:T(8,128)(2,1)S(1)} collective-permute-done((bf16[1,128,128]{2,1,0:T(8,128)(2,1)S(1)}, bf16[1,128,128]{2,1,0:T(8,128)(2,1)S(1)}, u32[]{:S(2)}, u32[]{:S(2)}) %collective-permute-start.8) | collective-permute-done | bytes 32800 | tf_op jit(solution)/shard_map/ppermute | solution.py:596
  100.8 0.6 fusion
  101.4 3.2 %all-to-all-done.3 = bf16[32,32,128]{2,1,0:T(8,128)(2,1)S(1)} async-done(((bf16[32,32,128]{2,1,0:T(8,128)(2,1)}), bf16[32,32,128]{2,1,0:T(8,128)(2,1)S(1)}, u32[]{:S(2)}, u32[]{:S(2)}) %all-to-all-start.3) | async-done | bytes 262176 | tf_op jit(solution)/shard_map/all_to_all | solution.py:587
  104.6 0.7 convert_reduce_fusion
  (13 shorter events, 0.1 us)
Async XLA Ops:
  2.4 35.5 %copy-start = (s32[1,8]{1,0:T(1,128)S(1)}, s32[1,8]{1,0:T(1,128)}, u32[]{:S(2)}) copy-start(s32[1,8]{1,0:T(1,128)} %param.14) | copy-start | bytes 100
  2.5 35.5 %copy-start.1 = (s32[32]{0:T(128)S(1)}, s32[32]{0:T(128)}, u32[]{:S(2)}) copy-start(s32[32]{0:T(128)} %param.15) | copy-start | bytes 388
  2.5 33.5 %all-to-all-start = ((bf16[16,192,128]{2,1,0:T(8,128)(2,1)}), bf16[16,192,128]{2,1,0:T(8,128)(2,1)S(1)}, u32[]{:S(2)}, u32[]{:S(2)}) async-start(bf16[16,192,128]{2,1,0:T(8,128)(2,1)} %join_keys_values.1), calls=%async_computation | async-start | bytes 1572864 | tf_op jit(solution)/shard_map/all_to_all | solution.py:587
  16.9 31.6 %collective-permute-start.1 = (bf16[2,128,1024]{2,1,0:T(8,128)(2,1)}, bf16[2,128,1024]{2,1,0:T(8,128)(2,1)}, u32[]{:S(2)}, u32[]{:S(2)}) collective-permute-start(bf16[2,128,1024]{2,1,0:T(8,128)(2,1)} %get-tuple-element.24), channel_id=1, source_target_pairs={{0,32},{32,0},{64,96},{96,64},{1,33},{33,1},{65,97},{97,65},{2,34}... | collective-permute-start | bytes 1572872 | tf_op jit(solution)/shard_map/ppermute | solution.py:596
  18.5 30.0 %collective-permute-start.2 = (bf16[2,128,1024]{2,1,0:T(8,128)(2,1)}, bf16[2,128,1024]{2,1,0:T(8,128)(2,1)}, u32[]{:S(2)}, u32[]{:S(2)}) collective-permute-start(bf16[2,128,1024]{2,1,0:T(8,128)(2,1)} %get-tuple-element.25), channel_id=1, source_target_pairs={{0,64},{32,96},{64,0},{96,32},{1,65},{33,97},{65,1},{97,33},{2,66}... | collective-permute-start | bytes 1572872 | tf_op jit(solution)/shard_map/ppermute | solution.py:596
  21.2 27.3 %collective-permute-start.3 = (bf16[2,128,1024]{2,1,0:T(8,128)(2,1)}, bf16[2,128,1024]{2,1,0:T(8,128)(2,1)}, u32[]{:S(2)}, u32[]{:S(2)}) collective-permute-start(bf16[2,128,1024]{2,1,0:T(8,128)(2,1)} %get-tuple-element.26), channel_id=1, source_target_pairs={{0,96},{32,64},{64,32},{96,0},{1,97},{33,65},{65,33},{97,1},{2,98}... | collective-permute-start | bytes 1572872 | tf_op jit(solution)/shard_map/ppermute | solution.py:596
  36.7 11.8 %collective-permute-start = (bf16[16,64,128]{2,1,0:T(8,128)(2,1)}, bf16[16,64,128]{2,1,0:T(8,128)(2,1)S(1)}, u32[]{:S(2)}, u32[]{:S(2)}) collective-permute-start(bf16[16,64,128]{2,1,0:T(8,128)(2,1)} %slice.13), channel_id=1, source_target_pairs={{0,8},{8,0},{1,9},{9,1},{2,10},{10,2},{3,11},{11,3},{4,12},{12,4},... | collective-permute-start | bytes 786440 | tf_op jit(solution)/shard_map/ppermute | solution.py:596
  43.1 23.3 %all-to-all-start.1 = ((bf16[16,128,128]{2,1,0:T(8,128)(2,1)}), bf16[16,128,128]{2,1,0:T(8,128)(2,1)}, u32[]{:S(2)}, u32[]{:S(2)}) async-start(bf16[16,128,128]{2,1,0:T(8,128)(2,1)} %bitcast.18), calls=%async_computation.1 | async-start | bytes 1048576 | tf_op jit(solution)/shard_map/all_to_all | solution.py:587
  53.5 20.2 %collective-permute-start.5 = (bf16[4,128,1024]{2,1,0:T(8,128)(2,1)}, bf16[4,128,1024]{2,1,0:T(8,128)(2,1)}, u32[]{:S(2)}, u32[]{:S(2)}) collective-permute-start(bf16[4,128,1024]{2,1,0:T(8,128)(2,1)} %get-tuple-element.33), channel_id=1, source_target_pairs={{0,16},{16,0},{1,17},{17,1},{2,18},{18,2},{3,19},{19,3},{4,20},{20... | collective-permute-start | bytes 3145736 | tf_op jit(solution)/shard_map/ppermute | solution.py:596
  53.6 12.8 %collective-permute-start.4 = (bf16[8,128,128]{2,1,0:T(8,128)(2,1)S(1)}, bf16[8,128,128]{2,1,0:T(8,128)(2,1)S(1)}, u32[]{:S(2)}, u32[]{:S(2)}) collective-permute-start(bf16[8,128,128]{2,1,0:T(8,128)(2,1)S(1)} %get-tuple-element.31), channel_id=1, source_target_pairs={{0,8},{8,0},{1,9},{9,1},{2,10},{10,2},{3,11},{11,3},{4,12},{12,4},... | collective-permute-start | bytes 786440 | tf_op jit(solution)/shard_map/ppermute | solution.py:596
  68.9 11.9 %all-to-all-start.2 = ((bf16[8,128,128]{2,1,0:T(8,128)(2,1)}), bf16[8,128,128]{2,1,0:T(8,128)(2,1)S(1)}, u32[]{:S(2)}, u32[]{:S(2)}) async-start(bf16[8,128,128]{2,1,0:T(8,128)(2,1)} %get-tuple-element.32), calls=%async_computation.2 | async-start | bytes 524288 | tf_op jit(solution)/shard_map/all_to_all | solution.py:587
  73.2 5.9 %collective-permute-start.6 = (bf16[4,128,128]{2,1,0:T(8,128)(2,1)S(1)}, bf16[4,128,128]{2,1,0:T(8,128)(2,1)S(1)}, u32[]{:S(2)}, u32[]{:S(2)}) collective-permute-start(bf16[4,128,128]{2,1,0:T(8,128)(2,1)S(1)} %get-tuple-element.35), channel_id=1, source_target_pairs={{0,1},{1,0},{2,3},{3,2},{4,5},{5,4},{6,7},{7,6},{8,9},{9,8},{10,11... | collective-permute-start | bytes 393224 | tf_op jit(solution)/shard_map/ppermute | solution.py:596
  82.5 8.9 %collective-permute-start.7 = (bf16[2,128,128]{2,1,0:T(8,128)(2,1)S(1)}, bf16[2,128,128]{2,1,0:T(8,128)(2,1)S(1)}, u32[]{:S(2)}, u32[]{:S(2)}) collective-permute-start(bf16[2,128,128]{2,1,0:T(8,128)(2,1)S(1)} %get-tuple-element.37), channel_id=1, source_target_pairs={{0,2},{1,3},{2,0},{3,1},{4,6},{5,7},{6,4},{7,5},{8,10},{9,11},{10,... | collective-permute-start | bytes 196616 | tf_op jit(solution)/shard_map/ppermute | solution.py:596
  84.3 20.3 %all-to-all-start.3 = ((bf16[32,32,128]{2,1,0:T(8,128)(2,1)}), bf16[32,32,128]{2,1,0:T(8,128)(2,1)S(1)}, u32[]{:S(2)}, u32[]{:S(2)}) async-start(bf16[32,32,128]{2,1,0:T(8,128)(2,1)} %bitcast.12), calls=%async_computation.3 | async-start | bytes 524288 | tf_op jit(solution)/shard_map/all_to_all | solution.py:587
  91.5 9.3 %collective-permute-start.8 = (bf16[1,128,128]{2,1,0:T(8,128)(2,1)S(1)}, bf16[1,128,128]{2,1,0:T(8,128)(2,1)S(1)}, u32[]{:S(2)}, u32[]{:S(2)}) collective-permute-start(bf16[1,128,128]{2,1,0:T(8,128)(2,1)S(1)} %slice.20), channel_id=1, source_target_pairs={{0,7},{1,6},{2,5},{3,4},{4,3},{5,2},{6,1},{7,0},{8,15},{9,14},{10,... | collective-permute-start | bytes 98312 | tf_op jit(solution)/shard_map/ppermute | solution.py:596

commit v5 on v4

--- a/solution.py
+++ b/solution.py
@@ -16,6 +16,7 @@
 KEYS = 2048
 N_CTX = 16
 CHUNK = 256
+WIDE_CHUNK = 512
 MOST = 1024
 SPAN_BLOCKS = MOST // BLOCK + 1
 SPAN = SPAN_BLOCKS * BLOCK
@@ -34,8 +35,8 @@
 FAR = ("ylo", "yhi", "z")
 
 
-def chunks():
-    return [(start, min(CHUNK, SPAN - start)) for start in range(0, SPAN, CHUNK)]
+def chunks(most=CHUNK):
+    return [(start, min(most, SPAN - start)) for start in range(0, SPAN, most)]
 
 
 def fold_rows(tile, op):
@@ -126,63 +127,72 @@
         copy.start()
     invert_order(scalars, slots)
     parts[...] = jnp.zeros_like(parts)
+    firsts = []
     for half in range(2):
         own, first = span_of(scalars, half)
+        firsts.append(first)
         for step in range(SPAN_BLOCKS):
-            keys[step * BLOCK : (step + 1) * BLOCK, :] = key_block(kv, slots, first, step)
-        write_bias(scalars, own, first, bias)
-        if half == 0:
-            fetches[0].wait()
-        shares = []
-        for group in range(GROUPS):
-            tile_index = half * GROUPS + group
-            queries = heads_of(queries_in, half, group)
-            top = jnp.full((8, LANES), MASKED, jnp.float32)
-            for start, size in chunks():
-                rows = slice(start, start + size)
-                raw = lax.dot_general(
-                    keys[rows, :], queries, NT, preferred_element_type=jnp.float32
-                )
-                add = bias[rows, :]
-                tile = raw * SCALE_LOG2 + jnp.concatenate([add, add], axis=1)
-                scores[rows, :] = tile
-                top = jnp.maximum(top, fold_rows(tile, jnp.max))
-            top = jnp.max(top, axis=0, keepdims=True)
-            total = jnp.zeros((8, LANES), jnp.float32)
-            for start, size in chunks():
-                rows = slice(start, start + size)
-                tile = jnp.exp2(scores[rows, :] - top)
-                probs[tile_index, rows, :] = tile.astype(jnp.bfloat16)
-                total = total + fold_rows(tile, jnp.sum)
-            share = 1.0 / jnp.sum(total, axis=0, keepdims=True)
-            shares.append(share)
-            share = jnp.broadcast_to(share, (8, LANES))
-            coarse = share.astype(jnp.bfloat16)
-            rest = (share - coarse.astype(jnp.float32)).astype(jnp.bfloat16)
-            probs[tile_index, SPAN:, :] = jnp.concatenate([coarse, rest], axis=0)
-        if half == 0:
-            fetches[1].wait()
-        gradients = []
-        for group in range(GROUPS):
-            by_row = jnp.broadcast_to(shares[group], (HEAD_SIZE, LANES)).T
-            gradients.append(
-                (heads_of(gradients_in, half, group).astype(jnp.float32) * by_row).astype(
-                    jnp.bfloat16
-                )
-            )
+            rows = slice(step * BLOCK, (step + 1) * BLOCK)
+            keys[half, rows, :] = key_block(kv, slots, first, step)
+        write_bias(scalars, own, first, bias.at[half])
+    fetches[0].wait()
+    tiles = 2 * GROUPS
+    queries = [heads_of(queries_in, tile // GROUPS, tile % GROUPS) for tile in range(tiles)]
+    tops = [jnp.full((8, LANES), MASKED, jnp.float32) for _ in range(tiles)]
+    totals = [jnp.zeros((8, LANES), jnp.float32) for _ in range(tiles)]
+    scaled = [None] * tiles
+
+    def score(tile, start, size):
+        rows = slice(start, start + size)
+        half = tile // GROUPS
+        raw = lax.dot_general(
+            keys[half, rows, :], queries[tile], NT, preferred_element_type=jnp.float32
+        )
+        add = bias[half, rows, :]
+        masked = raw * SCALE_LOG2 + jnp.concatenate([add, add], axis=1)
+        scores[tile % 2, rows, :] = masked
+        tops[tile] = jnp.maximum(tops[tile], fold_rows(masked, jnp.max))
+
+    def weigh(tile, start, size):
+        rows = slice(start, start + size)
+        part = jnp.exp2(scores[tile % 2, rows, :] - tops[tile])
+        probs[tile, rows, :] = part.astype(jnp.bfloat16)
+        totals[tile] = totals[tile] + fold_rows(part, jnp.sum)
+
+    def finish(tile):
+        share = 1.0 / jnp.sum(totals[tile], axis=0, keepdims=True)
+        by_row = jnp.broadcast_to(share, (HEAD_SIZE, LANES)).T
+        full = heads_of(gradients_in, tile // GROUPS, tile % GROUPS).astype(jnp.float32)
+        scaled[tile] = (full * by_row).astype(jnp.bfloat16)
+        share = jnp.broadcast_to(share, (8, LANES))
+        coarse = share.astype(jnp.bfloat16)
+        rest = (share - coarse.astype(jnp.float32)).astype(jnp.bfloat16)
+        probs[tile, SPAN:, :] = jnp.concatenate([coarse, rest], axis=0)
+
+    def collect(half, start, size):
+        rows = slice(start, start + size)
+        add = sum(
+            jnp.dot(probs[tile, rows, :], scaled[tile], preferred_element_type=jnp.float32)
+            for tile in range(half * GROUPS, (half + 1) * GROUPS)
+        )
+        for step in range(size // BLOCK):
+            target = slot_rows(slots, firsts[half], start // BLOCK + step)
+            parts[target, :] += add[step * BLOCK : (step + 1) * BLOCK]
+
+    for start, size in chunks():
+        score(0, start, size)
+    fetches[1].wait()
+    for tile in range(tiles):
+        tops[tile] = jnp.max(tops[tile], axis=0, keepdims=True)
         for start, size in chunks():
-            rows = slice(start, start + size)
-            add = sum(
-                jnp.dot(
-                    probs[half * GROUPS + group, rows, :],
-                    gradients[group],
-                    preferred_element_type=jnp.float32,
-                )
-                for group in range(GROUPS)
-            )
-            for step in range(size // BLOCK):
-                target = slot_rows(slots, first, start // BLOCK + step)
-                parts[target, :] += add[step * BLOCK : (step + 1) * BLOCK]
+            if tile + 1 < tiles:
+                score(tile + 1, start, size)
+            weigh(tile, start, size)
+            if tile == tiles - 1:
+                collect(0, start, size)
+        finish(tile)
+    for start, size in chunks():
+        collect(1, start, size)
     copies = []
     for piece in range(4):
         rows = pl.ds(piece * KEYS // 4, KEYS // 4)
@@ -215,7 +225,6 @@
     dscores_out,
     keys_out,
     slots,
-    keys,
     values,
     parts,
     queries_in,
@@ -244,16 +253,18 @@
     me = scalars[BLOCKS + NDOC]
     invert_order(scalars, slots)
     parts[...] = jnp.zeros_like(parts)
+    firsts = []
     for half in range(2):
         _, first = span_of(scalars, half)
+        firsts.append(first)
         for step in range(SPAN_BLOCKS):
             rows = slice(step * BLOCK, (step + 1) * BLOCK)
-            keys[rows, :] = key_block(kv, slots, first, step)
-            values[rows, :] = value_block(kv, far_values, slots, first, step, me // 8)
-        keys_out[half] = keys[...]
-        if half == 0:
-            for copy in fetches:
-                copy.wait()
+            keys_out[half, rows, :] = key_block(kv, slots, first, step)
+            values[half, rows, :] = value_block(kv, far_values, slots, first, step, me // 8)
+    for copy in fetches:
+        copy.wait()
+    for half in range(2):
+        first = firsts[half]
         queries, gradients, deltas, shares = [], [], [], []
         for group in range(GROUPS):
             queries.append(heads_of(queries_in, half, group))
@@ -263,12 +274,12 @@
             deltas.append(jnp.sum(product.T, axis=0, keepdims=True))
             pieces = probs[half * GROUPS + group, SPAN:, :].astype(jnp.float32)
             shares.append(pieces[:1] + pieces[8:9])
-        for start, size in chunks():
+        for start, size in chunks(WIDE_CHUNK):
             rows = slice(start, start + size)
             add = 0.0
             for group in range(GROUPS):
                 dprobs = lax.dot_general(
-                    values[rows, :],
+                    values[half, rows, :],
                     gradients[group],
                     NT,
                     preferred_element_type=jnp.float32,
@@ -354,9 +365,9 @@
         ],
         scratch_shapes=[
             pltpu.SMEM((BLOCKS,), jnp.int32),
-            pltpu.VMEM((SPAN, HEAD_SIZE), jnp.bfloat16),
-            pltpu.VMEM((SPAN, HEAD_SIZE), jnp.float32),
-            pltpu.VMEM((SPAN, LANES), jnp.float32),
+            pltpu.VMEM((2, SPAN, HEAD_SIZE), jnp.bfloat16),
+            pltpu.VMEM((2, SPAN, HEAD_SIZE), jnp.float32),
+            pltpu.VMEM((2, SPAN, LANES), jnp.float32),
             pltpu.VMEM((KEYS, HEAD_SIZE), jnp.float32),
             pltpu.VMEM((KEYS, HEAD_SIZE), jnp.bfloat16),
             pltpu.VMEM((ROWS, QUERY_HEADS * HEAD_SIZE), jnp.bfloat16),
@@ -382,8 +393,7 @@
         ],
         scratch_shapes=[
             pltpu.SMEM((BLOCKS,), jnp.int32),
-            pltpu.VMEM((SPAN, HEAD_SIZE), jnp.bfloat16),
-            pltpu.VMEM((SPAN, HEAD_SIZE), jnp.bfloat16),
+            pltpu.VMEM((2, SPAN, HEAD_SIZE), jnp.bfloat16),
             pltpu.VMEM((KEYS, HEAD_SIZE), jnp.float32),
             pltpu.VMEM((ROWS, QUERY_HEADS * HEAD_SIZE), jnp.bfloat16),
             pltpu.VMEM((ROWS, QUERY_HEADS * HEAD_SIZE), jnp.bfloat16),
@@ -495,8 +505,9 @@
     for block in range(count):
         fetches[block].wait()
         total = total + arrived[block].astype(jnp.float32)
-    low[...] = total.astype(jnp.bfloat16)
-    value_grad[...] = low[...]
+    total = total.astype(jnp.bfloat16)
+    low[...] = total
+    value_grad[...] = total
     stores = [
         pltpu.make_async_copy(low, spread.at[copy], done.at[copy])
         for copy in range(spread.shape[0])

time: 106 us -> 105 us (level)
  transfers between devices with their start and end apart: 13 -> 13, of which waited for: 6 -> 6; matrix products, arithmetic and copies ran while one was open for 1% -> 1% of each run, Pallas kernels for 18% -> 17%
where the time goes in v5:
time: 105 us
  starting transfers between devices  43.1 us (41%)
  waiting for transfers between devices  37.5 us (36%)
  Pallas kernels  21.1 us (20%)
  other arithmetic  1.44 us (1%)
    all_to_all x4, starting transfers between devices, exchange(): return lax.all_to_all(blocks, axes, 0, 0, tiled=False)  28.1 us
    all_to_all x4, waiting for transfers between devices, exchange(): return lax.all_to_all(blocks, axes, 0, 0, tiled=False)  19.1 us
    ppermute x9, waiting for transfers between devices, swapped(): return lax.ppermute(block, axis, [(i, i ^ shift) for i in range(count)])  18.4 us
    ppermute x9, starting transfers between devices, swapped(): return lax.ppermute(block, axis, [(i, i ^ shift) for i in range(count)])  15 us
    pallas_call x1, Pallas kernels, attention_probs(): pl.pallas_call(probs_kernel, in_specs=[SMEM_SPEC, HBM_SPEC, HBM_SPEC, VME...  4.69 us
    pallas_call x1, Pallas kernels, attention_grads(): pl.pallas_call(grads_kernel, in_specs=[SMEM_SPEC] + [HBM_SPEC] * 3 + [VME...  4.33 us
    pallas_call x1, Pallas kernels, split_inputs(): pl.pallas_call(split_kernel, in_specs=[SMEM_SPEC, HBM_SPEC], out_specs=[H...  3.13 us
    pallas_call x1, Pallas kernels, sum_and_spread(): pl.pallas_call(spread_kernel, in_specs=[HBM_SPEC, HBM_SPEC, VMEM_SPEC, HB...  2.49 us
  transfers between devices with their start and end apart: 13, of which 6 were waited for; matrix products, arithmetic and copies ran while one was open for 1% of the time, Pallas kernels for 17%

profile of v5, /device:TPU:32, one launch (start us, length us, event | category | flops | bytes accessed | tf_op | source)
XLA Modules:
  0.0 104.7 jit_solution(13858393648630180615)
XLA Ops:
  0.6 1.8 %join_keys_values.1 = bf16[16,192,128]{2,1,0:T(8,128)(2,1)} custom-call(bf16[128,128]{1,0:T(8,128)(2,1)} %bitcast.20, bf16[128,128]{1,0:T(8,128)(2,1)} %bitcast.21), custom_call_target="tpu_custom_call" | custom-call | tf_op jit(solution)/shard_map/join_keys_values/pallas_call | solution.py:558
  2.5 11.2 %all-to-all-start = ((bf16[16,192,128]{2,1,0:T(8,128)(2,1)}), bf16[16,192,128]{2,1,0:T(8,128)(2,1)S(1)}, u32[]{:S(2)}, u32[]{:S(2)}) async-start(bf16[16,192,128]{2,1,0:T(8,128)(2,1)} %join_keys_values.1), calls=%async_computation | async-start | bytes 1572864 | tf_op jit(solution)/shard_map/all_to_all | solution.py:598
  13.7 0.1 pad_add_fusion.1.place
  13.8 3.1 %split_inputs.1 = (bf16[2,128,1024]{2,1,0:T(8,128)(2,1)}, bf16[2,128,1024]{2,1,0:T(8,128)(2,1)}, bf16[2,128,1024]{2,1,0:T(8,128)(2,1)}, bf16[2,128,1024]{2,1,0:T(8,128)(2,1)}) custom-call(s32[2]{0:T(128)S(1)} %pad_add_fusion.1.place, bf16[128,8192]{1,0:T(8,128)(2,1)} %inputs.1), custom_call_target="tpu_custom_call" | custom-call | tf_op jit(solution)/shard_map/split_inputs/pallas_call | solution.py:464
  16.9 1.6 %collective-permute-start.1 = (bf16[2,128,1024]{2,1,0:T(8,128)(2,1)}, bf16[2,128,1024]{2,1,0:T(8,128)(2,1)}, u32[]{:S(2)}, u32[]{:S(2)}) collective-permute-start(bf16[2,128,1024]{2,1,0:T(8,128)(2,1)} %get-tuple-element.24), channel_id=1, source_target_pairs={{0,32},{32,0},{64,96},{96,64},{1,33},{33,1},{65,97},{97,65},{2,34}... | collective-permute-start | bytes 1572872 | tf_op jit(solution)/shard_map/ppermute | solution.py:607
  18.5 2.7 %collective-permute-start.2 = (bf16[2,128,1024]{2,1,0:T(8,128)(2,1)}, bf16[2,128,1024]{2,1,0:T(8,128)(2,1)}, u32[]{:S(2)}, u32[]{:S(2)}) collective-permute-start(bf16[2,128,1024]{2,1,0:T(8,128)(2,1)} %get-tuple-element.25), channel_id=1, source_target_pairs={{0,64},{32,96},{64,0},{96,32},{1,65},{33,97},{65,1},{97,33},{2,66}... | collective-permute-start | bytes 1572872 | tf_op jit(solution)/shard_map/ppermute | solution.py:607
  21.2 0.5 collective-permute-start.3
  21.7 14.3 %all-to-all-done.kv = bf16[16,192,128]{2,1,0:T(8,128)(2,1)S(1)} async-done(((bf16[16,192,128]{2,1,0:T(8,128)(2,1)}), bf16[16,192,128]{2,1,0:T(8,128)(2,1)S(1)}, u32[]{:S(2)}, u32[]{:S(2)}) %all-to-all-start) | async-done | bytes 786464 | tf_op jit(solution)/shard_map/all_to_all | solution.py:598
  36.0 0.7 slice.13
  36.7 1.3 %collective-permute-start = (bf16[16,64,128]{2,1,0:T(8,128)(2,1)}, bf16[16,64,128]{2,1,0:T(8,128)(2,1)S(1)}, u32[]{:S(2)}, u32[]{:S(2)}) collective-permute-start(bf16[16,64,128]{2,1,0:T(8,128)(2,1)} %slice.13), channel_id=1, source_target_pairs={{0,8},{8,0},{1,9},{9,1},{2,10},{10,2},{3,11},{11,3},{4,12},{12,4},... | collective-permute-start | bytes 786440 | tf_op jit(solution)/shard_map/ppermute | solution.py:607
  38.0 0.1 pad_add_fusion.scalars
  38.1 4.7 %probs_and_value_part.1 = (bf16[4,1104,256]{2,1,0:T(8,128)(2,1)S(1)}, bf16[2048,128]{1,0:T(8,128)(2,1)}) custom-call(s32[41]{0:T(128)S(1)} %pad_add_fusion.scalars, bf16[128,1024]{1,0:T(8,128)(2,1)} %bitcast.13, bf16[128,1024]{1,0:T(8,128)(2,1)} %bitcast.15, bf16[16,192,128]{2,1,0:T(8,128)(2,1)S(1)} %all-to-all-done.kv), custom_call_target="tpu_custom_call" | custom-call | tf_op jit(solution)/shard_map/probs_and_value_part/pallas_call | solution.py:358
  42.8 5.4 %all-to-all-start.1 = ((bf16[16,128,128]{2,1,0:T(8,128)(2,1)}), bf16[16,128,128]{2,1,0:T(8,128)(2,1)}, u32[]{:S(2)}, u32[]{:S(2)}) async-start(bf16[16,128,128]{2,1,0:T(8,128)(2,1)} %bitcast.18), calls=%async_computation.1 | async-start | bytes 1048576 | tf_op jit(solution)/shard_map/all_to_all | solution.py:598
  48.2 4.3 %key_part.1 = (bf16[8,128,128]{2,1,0:T(8,128)(2,1)S(1)}, bf16[8,128,128]{2,1,0:T(8,128)(2,1)}, bf16[4,128,1024]{2,1,0:T(8,128)(2,1)}, bf16[4,1088,256]{2,1,0:T(8,128)(2,1)S(1)}, bf16[2,1088,128]{2,1,0:T(8,128)(2,1)S(1)}) custom-call(s32[41]{0:T(128)S(1)} %pad_add_fusion.scalars, bf16[128,1024]{1,0:T(8,128)(2,1)} %bitcast.14, bf16[128,1024]{1,0:T(8,128)(2,1)} %bitcast.19, ...), custom_call_target="tpu_custom_call" | custom-call | tf_op jit(solution)/shard_map/key_part/pallas_call | solution.py:383
  52.5 0.1 collective-permute-start.5
  52.6 3.1 %collective-permute-start.4 = (bf16[8,128,128]{2,1,0:T(8,128)(2,1)S(1)}, bf16[8,128,128]{2,1,0:T(8,128)(2,1)S(1)}, u32[]{:S(2)}, u32[]{:S(2)}) collective-permute-start(bf16[8,128,128]{2,1,0:T(8,128)(2,1)S(1)} %get-tuple-element.31), channel_id=1, source_target_pairs={{0,8},{8,0},{1,9},{9,1},{2,10},{10,2},{3,11},{11,3},{4,12},{12,4},... | collective-permute-start | bytes 786440 | tf_op jit(solution)/shard_map/ppermute | solution.py:607
  55.7 1.3 %query_product.1.after = bf16[128,1024]{1,0:T(8,128)(2,1)} custom-call(bf16[2,1088,128]{2,1,0:T(8,128)(2,1)S(1)} %get-tuple-element.27.keys, bf16[4,1088,256]{2,1,0:T(8,128)(2,1)S(1)} %get-tuple-element.28.dscores), custom_call_target="tpu_custom_call" | custom-call | tf_op jit(solution)/shard_map/query_product/pallas_call | solution.py:328
  57.0 8.7 %collective-permute-done.4.received = bf16[8,128,128]{2,1,0:T(8,128)(2,1)S(1)} collective-permute-done((bf16[8,128,128]{2,1,0:T(8,128)(2,1)S(1)}, bf16[8,128,128]{2,1,0:T(8,128)(2,1)S(1)}, u32[]{:S(2)}, u32[]{:S(2)}) %collective-permute-start.4) | collective-permute-done | bytes 262176 | tf_op jit(solution)/shard_map/ppermute | solution.py:607
  65.8 2.5 %sum_and_spread.1 = (bf16[128,128]{1,0:T(8,128)(2,1)}, bf16[8,128,128]{2,1,0:T(8,128)(2,1)}, f32[4,128,128]{2,1,0:T(8,128)S(1)}, bf16[4,128,128]{2,1,0:T(8,128)(2,1)S(1)}) custom-call(bf16[16,128,128]{2,1,0:T(8,128)(2,1)} %all-to-all-done.1.blocks, bf16[8,128,128]{2,1,0:T(8,128)(2,1)} %get-tuple-element.30.kept, ...), custom_call_target="tpu_custom_call" | custom-call | tf_op jit(solution)/shard_map/sum_and_spread/pallas_call | solution.py:525
  68.3 4.3 %all-to-all-start.2 = ((bf16[8,128,128]{2,1,0:T(8,128)(2,1)}), bf16[8,128,128]{2,1,0:T(8,128)(2,1)S(1)}, u32[]{:S(2)}, u32[]{:S(2)}) async-start(bf16[8,128,128]{2,1,0:T(8,128)(2,1)} %get-tuple-element.32), calls=%async_computation.2 | async-start | bytes 524288 | tf_op jit(solution)/shard_map/all_to_all | solution.py:598
  72.6 0.2 collective-permute-start.6
  72.8 1.6 %load_inputs.1.sources = bf16[4,256,1024]{2,1,0:T(8,128)(2,1)S(1)} custom-call(bf16[2,128,1024]{2,1,0:T(8,128)(2,1)} %get-tuple-element.23.zero, bf16[2,128,1024]{2,1,0:T(8,128)(2,1)} %collective-permute-done.1.one, bf16[2,128,1024]{2,1,0:T(8,128)(2,1)} %collective-permute-done.2.two, bf16[2,128,1024]{2,1,0:T(8,128)(2,1)} %collective-permute-done.3.three, ...), custom_call_target="tpu_custom_call" | custom-call | tf_op jit(solution)/shard_map/load_inputs/pallas_call | solution.py:423
  74.4 4.1 %collective-permute-done.6.received = bf16[4,128,128]{2,1,0:T(8,128)(2,1)S(1)} collective-permute-done((bf16[4,128,128]{2,1,0:T(8,128)(2,1)S(1)}, bf16[4,128,128]{2,1,0:T(8,128)(2,1)S(1)}, u32[]{:S(2)}, u32[]{:S(2)}) %collective-permute-start.6) | collective-permute-done | bytes 131104 | tf_op jit(solution)/shard_map/ppermute | solution.py:607
  78.5 1.6 %all-to-all-done.2.values = bf16[8,128,128]{2,1,0:T(8,128)(2,1)S(1)} async-done(((bf16[8,128,128]{2,1,0:T(8,128)(2,1)}), bf16[8,128,128]{2,1,0:T(8,128)(2,1)S(1)}, u32[]{:S(2)}, u32[]{:S(2)}) %all-to-all-start.2) | async-done | bytes 262176 | tf_op jit(solution)/shard_map/all_to_all | solution.py:598
  80.1 1.8 %weight_product.1 = (bf16[1024,128]{1,0:T(8,128)(2,1)}, f32[2,128,128]{2,1,0:T(8,128)S(1)}, bf16[2,128,128]{2,1,0:T(8,128)(2,1)S(1)}) custom-call(s32[2]{0:T(128)S(1)} %pad_add_fusion.1.place, bf16[8,128,128]{2,1,0:T(8,128)(2,1)S(1)} %all-to-all-done.2.values, bf16[4,256,1024]{2,1,0:T(8,128)(2,1)S(1)} %load_inputs.1.sources, ...), custom_call_target="tpu_custom_call" | custom-call | tf_op jit(solution)/shard_map/weight_product/pallas_call | solution.py:587
  81.9 1.8 %collective-permute-start.7 = (bf16[2,128,128]{2,1,0:T(8,128)(2,1)S(1)}, bf16[2,128,128]{2,1,0:T(8,128)(2,1)S(1)}, u32[]{:S(2)}, u32[]{:S(2)}) collective-permute-start(bf16[2,128,128]{2,1,0:T(8,128)(2,1)S(1)} %get-tuple-element.37), channel_id=1, source_target_pairs={{0,2},{1,3},{2,0},{3,1},{4,6},{5,7},{6,4},{7,5},{8,10},{9,11},{10,... | collective-permute-start | bytes 196616 | tf_op jit(solution)/shard_map/ppermute | solution.py:607
  83.7 7.2 %all-to-all-start.3 = ((bf16[32,32,128]{2,1,0:T(8,128)(2,1)}), bf16[32,32,128]{2,1,0:T(8,128)(2,1)S(1)}, u32[]{:S(2)}, u32[]{:S(2)}) async-start(bf16[32,32,128]{2,1,0:T(8,128)(2,1)} %bitcast.12), calls=%async_computation.3 | async-start | bytes 524288 | tf_op jit(solution)/shard_map/all_to_all | solution.py:598
  91.0 3.7 %collective-permute-start.8 = (bf16[1,128,128]{2,1,0:T(8,128)(2,1)S(1)}, bf16[1,128,128]{2,1,0:T(8,128)(2,1)S(1)}, u32[]{:S(2)}, u32[]{:S(2)}) collective-permute-start(bf16[1,128,128]{2,1,0:T(8,128)(2,1)S(1)} %slice.20), channel_id=1, source_target_pairs={{0,7},{1,6},{2,5},{3,4},{4,3},{5,2},{6,1},{7,0},{8,15},{9,14},{10,... | collective-permute-start | bytes 98312 | tf_op jit(solution)/shard_map/ppermute | solution.py:607
  94.6 5.6 %collective-permute-done.8 = bf16[1,128,128]{2,1,0:T(8,128)(2,1)S(1)} collective-permute-done((bf16[1,128,128]{2,1,0:T(8,128)(2,1)S(1)}, bf16[1,128,128]{2,1,0:T(8,128)(2,1)S(1)}, u32[]{:S(2)}, u32[]{:S(2)}) %collective-permute-start.8) | collective-permute-done | bytes 32800 | tf_op jit(solution)/shard_map/ppermute | solution.py:607
  100.2 0.6 fusion
  100.9 3.2 %all-to-all-done.3 = bf16[32,32,128]{2,1,0:T(8,128)(2,1)S(1)} async-done(((bf16[32,32,128]{2,1,0:T(8,128)(2,1)}), bf16[32,32,128]{2,1,0:T(8,128)(2,1)S(1)}, u32[]{:S(2)}, u32[]{:S(2)}) %all-to-all-start.3) | async-done | bytes 262176 | tf_op jit(solution)/shard_map/all_to_all | solution.py:598
  104.1 0.7 convert_reduce_fusion
  (13 shorter events, 0.1 us)
Async XLA Ops:
  2.4 35.5 %copy-start = (s32[1,8]{1,0:T(1,128)S(1)}, s32[1,8]{1,0:T(1,128)}, u32[]{:S(2)}) copy-start(s32[1,8]{1,0:T(1,128)} %param.14) | copy-start | bytes 100
  2.5 35.5 %copy-start.1 = (s32[32]{0:T(128)S(1)}, s32[32]{0:T(128)}, u32[]{:S(2)}) copy-start(s32[32]{0:T(128)} %param.15) | copy-start | bytes 388
  2.5 33.5 %all-to-all-start = ((bf16[16,192,128]{2,1,0:T(8,128)(2,1)}), bf16[16,192,128]{2,1,0:T(8,128)(2,1)S(1)}, u32[]{:S(2)}, u32[]{:S(2)}) async-start(bf16[16,192,128]{2,1,0:T(8,128)(2,1)} %join_keys_values.1), calls=%async_computation | async-start | bytes 1572864 | tf_op jit(solution)/shard_map/all_to_all | solution.py:598
  16.9 31.2 %collective-permute-start.1 = (bf16[2,128,1024]{2,1,0:T(8,128)(2,1)}, bf16[2,128,1024]{2,1,0:T(8,128)(2,1)}, u32[]{:S(2)}, u32[]{:S(2)}) collective-permute-start(bf16[2,128,1024]{2,1,0:T(8,128)(2,1)} %get-tuple-element.24), channel_id=1, source_target_pairs={{0,32},{32,0},{64,96},{96,64},{1,33},{33,1},{65,97},{97,65},{2,34}... | collective-permute-start | bytes 1572872 | tf_op jit(solution)/shard_map/ppermute | solution.py:607
  18.5 29.7 %collective-permute-start.2 = (bf16[2,128,1024]{2,1,0:T(8,128)(2,1)}, bf16[2,128,1024]{2,1,0:T(8,128)(2,1)}, u32[]{:S(2)}, u32[]{:S(2)}) collective-permute-start(bf16[2,128,1024]{2,1,0:T(8,128)(2,1)} %get-tuple-element.25), channel_id=1, source_target_pairs={{0,64},{32,96},{64,0},{96,32},{1,65},{33,97},{65,1},{97,33},{2,66}... | collective-permute-start | bytes 1572872 | tf_op jit(solution)/shard_map/ppermute | solution.py:607
  21.2 27.0 %collective-permute-start.3 = (bf16[2,128,1024]{2,1,0:T(8,128)(2,1)}, bf16[2,128,1024]{2,1,0:T(8,128)(2,1)}, u32[]{:S(2)}, u32[]{:S(2)}) collective-permute-start(bf16[2,128,1024]{2,1,0:T(8,128)(2,1)} %get-tuple-element.26), channel_id=1, source_target_pairs={{0,96},{32,64},{64,32},{96,0},{1,97},{33,65},{65,33},{97,1},{2,98}... | collective-permute-start | bytes 1572872 | tf_op jit(solution)/shard_map/ppermute | solution.py:607
  36.7 11.5 %collective-permute-start = (bf16[16,64,128]{2,1,0:T(8,128)(2,1)}, bf16[16,64,128]{2,1,0:T(8,128)(2,1)S(1)}, u32[]{:S(2)}, u32[]{:S(2)}) collective-permute-start(bf16[16,64,128]{2,1,0:T(8,128)(2,1)} %slice.13), channel_id=1, source_target_pairs={{0,8},{8,0},{1,9},{9,1},{2,10},{10,2},{3,11},{11,3},{4,12},{12,4},... | collective-permute-start | bytes 786440 | tf_op jit(solution)/shard_map/ppermute | solution.py:607
  42.8 23.0 %all-to-all-start.1 = ((bf16[16,128,128]{2,1,0:T(8,128)(2,1)}), bf16[16,128,128]{2,1,0:T(8,128)(2,1)}, u32[]{:S(2)}, u32[]{:S(2)}) async-start(bf16[16,128,128]{2,1,0:T(8,128)(2,1)} %bitcast.18), calls=%async_computation.1 | async-start | bytes 1048576 | tf_op jit(solution)/shard_map/all_to_all | solution.py:598
  52.5 20.3 %collective-permute-start.5 = (bf16[4,128,1024]{2,1,0:T(8,128)(2,1)}, bf16[4,128,1024]{2,1,0:T(8,128)(2,1)}, u32[]{:S(2)}, u32[]{:S(2)}) collective-permute-start(bf16[4,128,1024]{2,1,0:T(8,128)(2,1)} %get-tuple-element.33), channel_id=1, source_target_pairs={{0,16},{16,0},{1,17},{17,1},{2,18},{18,2},{3,19},{19,3},{4,20},{20... | collective-permute-start | bytes 3145736 | tf_op jit(solution)/shard_map/ppermute | solution.py:607
  52.6 13.1 %collective-permute-start.4 = (bf16[8,128,128]{2,1,0:T(8,128)(2,1)S(1)}, bf16[8,128,128]{2,1,0:T(8,128)(2,1)S(1)}, u32[]{:S(2)}, u32[]{:S(2)}) collective-permute-start(bf16[8,128,128]{2,1,0:T(8,128)(2,1)S(1)} %get-tuple-element.31), channel_id=1, source_target_pairs={{0,8},{8,0},{1,9},{9,1},{2,10},{10,2},{3,11},{11,3},{4,12},{12,4},... | collective-permute-start | bytes 786440 | tf_op jit(solution)/shard_map/ppermute | solution.py:607
  68.3 11.8 %all-to-all-start.2 = ((bf16[8,128,128]{2,1,0:T(8,128)(2,1)}), bf16[8,128,128]{2,1,0:T(8,128)(2,1)S(1)}, u32[]{:S(2)}, u32[]{:S(2)}) async-start(bf16[8,128,128]{2,1,0:T(8,128)(2,1)} %get-tuple-element.32), calls=%async_computation.2 | async-start | bytes 524288 | tf_op jit(solution)/shard_map/all_to_all | solution.py:598
  72.6 5.9 %collective-permute-start.6 = (bf16[4,128,128]{2,1,0:T(8,128)(2,1)S(1)}, bf16[4,128,128]{2,1,0:T(8,128)(2,1)S(1)}, u32[]{:S(2)}, u32[]{:S(2)}) collective-permute-start(bf16[4,128,128]{2,1,0:T(8,128)(2,1)S(1)} %get-tuple-element.35), channel_id=1, source_target_pairs={{0,1},{1,0},{2,3},{3,2},{4,5},{5,4},{6,7},{7,6},{8,9},{9,8},{10,11... | collective-permute-start | bytes 393224 | tf_op jit(solution)/shard_map/ppermute | solution.py:607
  81.9 9.0 %collective-permute-start.7 = (bf16[2,128,128]{2,1,0:T(8,128)(2,1)S(1)}, bf16[2,128,128]{2,1,0:T(8,128)(2,1)S(1)}, u32[]{:S(2)}, u32[]{:S(2)}) collective-permute-start(bf16[2,128,128]{2,1,0:T(8,128)(2,1)S(1)} %get-tuple-element.37), channel_id=1, source_target_pairs={{0,2},{1,3},{2,0},{3,1},{4,6},{5,7},{6,4},{7,5},{8,10},{9,11},{10,... | collective-permute-start | bytes 196616 | tf_op jit(solution)/shard_map/ppermute | solution.py:607
  83.7 20.3 %all-to-all-start.3 = ((bf16[32,32,128]{2,1,0:T(8,128)(2,1)}), bf16[32,32,128]{2,1,0:T(8,128)(2,1)S(1)}, u32[]{:S(2)}, u32[]{:S(2)}) async-start(bf16[32,32,128]{2,1,0:T(8,128)(2,1)} %bitcast.12), calls=%async_computation.3 | async-start | bytes 524288 | tf_op jit(solution)/shard_map/all_to_all | solution.py:598
  91.0 9.2 %collective-permute-start.8 = (bf16[1,128,128]{2,1,0:T(8,128)(2,1)S(1)}, bf16[1,128,128]{2,1,0:T(8,128)(2,1)S(1)}, u32[]{:S(2)}, u32[]{:S(2)}) collective-permute-start(bf16[1,128,128]{2,1,0:T(8,128)(2,1)S(1)} %slice.20), channel_id=1, source_target_pairs={{0,7},{1,6},{2,5},{3,4},{4,3},{5,2},{6,1},{7,0},{8,15},{9,14},{10,... | collective-permute-start | bytes 98312 | tf_op jit(solution)/shard_map/ppermute | solution.py:607

commit v6 on v5

--- a/solution.py
+++ b/solution.py
@@ -109,6 +109,7 @@
     kv,
     probs,
     value_part,
+    far_sent,
     slots,
     keys,
     bias,
@@ -123,7 +124,8 @@
         pltpu.make_async_copy(query, queries_in, done.at[0]),
         pltpu.make_async_copy(cotangent, gradients_in, done.at[1]),
     ]
-    for copy in fetches:
+    far = pltpu.make_async_copy(kv.at[:, pl.ds(ROWS, BLOCK), :], far_sent, done.at[6])
+    for copy in fetches + [far]:
         copy.start()
     invert_order(scalars, slots)
     parts[...] = jnp.zeros_like(parts)
@@ -203,7 +205,7 @@
             )
         )
         copies[-1].start()
-    for copy in copies:
+    for copy in copies + [far]:
         copy.wait()
 
 
@@ -358,10 +360,11 @@
     return pl.pallas_call(
         probs_kernel,
         in_specs=[SMEM_SPEC, HBM_SPEC, HBM_SPEC, VMEM_SPEC],
-        out_specs=[VMEM_SPEC, HBM_SPEC],
+        out_specs=[VMEM_SPEC, HBM_SPEC, HBM_SPEC],
         out_shape=[
             jax.ShapeDtypeStruct((2 * GROUPS, SPAN + 16, LANES), jnp.bfloat16),
             pltpu.HBM((KEYS, HEAD_SIZE), jnp.bfloat16),
+            pltpu.HBM((N_CTX, BLOCK, HEAD_SIZE), jnp.bfloat16),
         ],
         scratch_shapes=[
             pltpu.SMEM((BLOCKS,), jnp.int32),
@@ -372,7 +375,7 @@
             pltpu.VMEM((KEYS, HEAD_SIZE), jnp.bfloat16),
             pltpu.VMEM((ROWS, QUERY_HEADS * HEAD_SIZE), jnp.bfloat16),
             pltpu.VMEM((ROWS, QUERY_HEADS * HEAD_SIZE), jnp.bfloat16),
-            pltpu.SemaphoreType.DMA((6,)),
+            pltpu.SemaphoreType.DMA((7,)),
         ],
         compiler_params=PARAMS,
         name="probs_and_value_part",
@@ -614,11 +617,11 @@
     place = jnp.stack([lax.axis_index("x"), lax.axis_index("core")]).astype(jnp.int32)
     near_count, far_count = lax.axis_size(NEAR), lax.axis_size(FAR)
     kv = exchange(join_keys_values(key[0], value[0]), CTX)
-    far_values = swapped(kv[:, ROWS:], "yhi", 1)
 
     parts = split_inputs(place, inputs)
     pieces = [parts[0]] + [swapped(parts[r], "x", r) for r in range(1, 4)]
-    probs, value_part = attention_probs(scalars, query[0], output_cotangent[0], kv)
+    probs, value_part, far_sent = attention_probs(scalars, query[0], output_cotangent[0], kv)
+    far_values = swapped(far_sent, "yhi", 1)
     value_blocks = exchange(value_part.reshape(N_CTX, ROWS, HEAD_SIZE), CTX)
     key_sent, key_kept, stacked, dscores, reached = attention_grads(
         scalars, query[0], output[0], output_cotangent[0], kv, far_values, probs, pieces

time: 105 us -> 105 us (level)
  starting transfers between devices: 43.1 us -> 41.5 us
  waiting for transfers between devices: 37.5 us -> 39.1 us
    ppermute x9, waiting for transfers between devices: 18.4 us -> 20.1 us  [swapped(): return lax.ppermute(block, axis, [(i, i ^ shift) for i in range(count)])]
    ppermute x9, starting transfers between devices: 15 us -> 13.4 us  [swapped(): return lax.ppermute(block, axis, [(i, i ^ shift) for i in range(count)])]
  transfers between devices with their start and end apart: 13 -> 13, of which waited for: 6 -> 7; matrix products, arithmetic and copies ran while one was open for 1% -> 1% of each run, Pallas kernels for 17% -> 17%
where the time goes in v6:
time: 105 us; the launch traced here: 104 us
  starting transfers between devices  41.5 us (40%)
  waiting for transfers between devices  39.1 us (37%)
  Pallas kernels  21.2 us (20%)
  other arithmetic  1.44 us (1%)
    all_to_all x4, starting transfers between devices, exchange(): return lax.all_to_all(blocks, axes, 0, 0, tiled=False)  28.1 us
    ppermute x9, waiting for transfers between devices, swapped(): return lax.ppermute(block, axis, [(i, i ^ shift) for i in range(count)])  20.1 us
    all_to_all x4, waiting for transfers between devices, exchange(): return lax.all_to_all(blocks, axes, 0, 0, tiled=False)  19 us
    ppermute x9, starting transfers between devices, swapped(): return lax.ppermute(block, axis, [(i, i ^ shift) for i in range(count)])  13.4 us
    pallas_call x1, Pallas kernels, attention_probs(): pl.pallas_call(probs_kernel, in_specs=[SMEM_SPEC, HBM_SPEC, HBM_SPEC, VME...  4.79 us
    pallas_call x1, Pallas kernels, attention_grads(): pl.pallas_call(grads_kernel, in_specs=[SMEM_SPEC] + [HBM_SPEC] * 3 + [VME...  4.31 us
    pallas_call x1, Pallas kernels, split_inputs(): pl.pallas_call(split_kernel, in_specs=[SMEM_SPEC, HBM_SPEC], out_specs=[H...  3.13 us
    pallas_call x1, Pallas kernels, sum_and_spread(): pl.pallas_call(spread_kernel, in_specs=[HBM_SPEC, HBM_SPEC, VMEM_SPEC, HB...  2.49 us
  transfers between devices with their start and end apart: 13, of which 7 were waited for; matrix products, arithmetic and copies ran while one was open for 1% of the time, Pallas kernels for 17%

profile of v6, /device:TPU:32, one launch (start us, length us, event | category | flops | bytes accessed | tf_op | source)
XLA Modules:
  0.0 104.1 jit_solution(12709203283580706514)
XLA Ops:
  0.7 1.8 %join_keys_values.1 = bf16[16,192,128]{2,1,0:T(8,128)(2,1)} custom-call(bf16[128,128]{1,0:T(8,128)(2,1)} %bitcast.20, bf16[128,128]{1,0:T(8,128)(2,1)} %bitcast.21), custom_call_target="tpu_custom_call" | custom-call | tf_op jit(solution)/shard_map/join_keys_values/pallas_call | solution.py:561
  2.5 11.2 %all-to-all-start = ((bf16[16,192,128]{2,1,0:T(8,128)(2,1)}), bf16[16,192,128]{2,1,0:T(8,128)(2,1)S(1)}, u32[]{:S(2)}, u32[]{:S(2)}) async-start(bf16[16,192,128]{2,1,0:T(8,128)(2,1)} %join_keys_values.1), calls=%async_computation | async-start | bytes 1572864 | tf_op jit(solution)/shard_map/all_to_all | solution.py:601
  13.7 0.1 pad_add_fusion.1.place
  13.8 3.1 %split_inputs.1 = (bf16[2,128,1024]{2,1,0:T(8,128)(2,1)}, bf16[2,128,1024]{2,1,0:T(8,128)(2,1)}, bf16[2,128,1024]{2,1,0:T(8,128)(2,1)}, bf16[2,128,1024]{2,1,0:T(8,128)(2,1)}) custom-call(s32[2]{0:T(128)S(1)} %pad_add_fusion.1.place, bf16[128,8192]{1,0:T(8,128)(2,1)} %inputs.1), custom_call_target="tpu_custom_call" | custom-call | tf_op jit(solution)/shard_map/split_inputs/pallas_call | solution.py:467
  16.9 1.6 %collective-permute-start.1 = (bf16[2,128,1024]{2,1,0:T(8,128)(2,1)}, bf16[2,128,1024]{2,1,0:T(8,128)(2,1)}, u32[]{:S(2)}, u32[]{:S(2)}) collective-permute-start(bf16[2,128,1024]{2,1,0:T(8,128)(2,1)} %get-tuple-element.26), channel_id=1, source_target_pairs={{0,32},{32,0},{64,96},{96,64},{1,33},{33,1},{65,97},{97,65},{2,34}... | collective-permute-start | bytes 1572872 | tf_op jit(solution)/shard_map/ppermute | solution.py:610
  18.5 2.7 %collective-permute-start.2 = (bf16[2,128,1024]{2,1,0:T(8,128)(2,1)}, bf16[2,128,1024]{2,1,0:T(8,128)(2,1)}, u32[]{:S(2)}, u32[]{:S(2)}) collective-permute-start(bf16[2,128,1024]{2,1,0:T(8,128)(2,1)} %get-tuple-element.27), channel_id=1, source_target_pairs={{0,64},{32,96},{64,0},{96,32},{1,65},{33,97},{65,1},{97,33},{2,66}... | collective-permute-start | bytes 1572872 | tf_op jit(solution)/shard_map/ppermute | solution.py:610
  21.2 0.5 collective-permute-start.3
  21.7 0.1 pad_add_fusion.scalars
  21.8 14.2 %all-to-all-done.kv = bf16[16,192,128]{2,1,0:T(8,128)(2,1)S(1)} async-done(((bf16[16,192,128]{2,1,0:T(8,128)(2,1)}), bf16[16,192,128]{2,1,0:T(8,128)(2,1)S(1)}, u32[]{:S(2)}, u32[]{:S(2)}) %all-to-all-start) | async-done | bytes 786464 | tf_op jit(solution)/shard_map/all_to_all | solution.py:601
  36.0 4.8 %probs_and_value_part.1 = (bf16[4,1104,256]{2,1,0:T(8,128)(2,1)S(1)}, bf16[2048,128]{1,0:T(8,128)(2,1)}, bf16[16,64,128]{2,1,0:T(8,128)(2,1)}) custom-call(s32[41]{0:T(128)S(1)} %pad_add_fusion.scalars, bf16[128,1024]{1,0:T(8,128)(2,1)} %bitcast.13, bf16[128,1024]{1,0:T(8,128)(2,1)} %bitcast.15, bf16[16,192,128]{2,1,0:T(8,128)(2,1)S(1)} %all-to-all-done.kv), custom_call_target="tpu_custom_call" | custom-call | tf_op jit(solution)/shard_map/probs_and_value_part/pallas_call | solution.py:360
  40.8 1.4 %collective-permute-start = (bf16[16,64,128]{2,1,0:T(8,128)(2,1)}, bf16[16,64,128]{2,1,0:T(8,128)(2,1)S(1)}, u32[]{:S(2)}, u32[]{:S(2)}) collective-permute-start(bf16[16,64,128]{2,1,0:T(8,128)(2,1)} %get-tuple-element.23), channel_id=1, source_target_pairs={{0,8},{8,0},{1,9},{9,1},{2,10},{10,2},{3,11},{11,3},{4,12},{12,4},... | collective-permute-start | bytes 786440 | tf_op jit(solution)/shard_map/ppermute | solution.py:610
  42.2 5.4 %all-to-all-start.1 = ((bf16[16,128,128]{2,1,0:T(8,128)(2,1)}), bf16[16,128,128]{2,1,0:T(8,128)(2,1)}, u32[]{:S(2)}, u32[]{:S(2)}) async-start(bf16[16,128,128]{2,1,0:T(8,128)(2,1)} %bitcast.18), calls=%async_computation.1 | async-start | bytes 1048576 | tf_op jit(solution)/shard_map/all_to_all | solution.py:601
  47.6 1.4 %collective-permute-done.far_values = bf16[16,64,128]{2,1,0:T(8,128)(2,1)S(1)} collective-permute-done((bf16[16,64,128]{2,1,0:T(8,128)(2,1)}, bf16[16,64,128]{2,1,0:T(8,128)(2,1)S(1)}, u32[]{:S(2)}, u32[]{:S(2)}) %collective-permute-start) | collective-permute-done | bytes 262176 | tf_op jit(solution)/shard_map/ppermute | solution.py:610
  48.9 4.3 %key_part.1 = (bf16[8,128,128]{2,1,0:T(8,128)(2,1)S(1)}, bf16[8,128,128]{2,1,0:T(8,128)(2,1)}, bf16[4,128,1024]{2,1,0:T(8,128)(2,1)}, bf16[4,1088,256]{2,1,0:T(8,128)(2,1)S(1)}, bf16[2,1088,128]{2,1,0:T(8,128)(2,1)S(1)}) custom-call(s32[41]{0:T(128)S(1)} %pad_add_fusion.scalars, bf16[128,1024]{1,0:T(8,128)(2,1)} %bitcast.14, bf16[128,1024]{1,0:T(8,128)(2,1)} %bitcast.19, ...), custom_call_target="tpu_custom_call" | custom-call | tf_op jit(solution)/shard_map/key_part/pallas_call | solution.py:386
  53.3 0.1 collective-permute-start.5
  53.4 1.7 %collective-permute-start.4 = (bf16[8,128,128]{2,1,0:T(8,128)(2,1)S(1)}, bf16[8,128,128]{2,1,0:T(8,128)(2,1)S(1)}, u32[]{:S(2)}, u32[]{:S(2)}) collective-permute-start(bf16[8,128,128]{2,1,0:T(8,128)(2,1)S(1)} %get-tuple-element.33), channel_id=1, source_target_pairs={{0,8},{8,0},{1,9},{9,1},{2,10},{10,2},{3,11},{11,3},{4,12},{12,4},... | collective-permute-start | bytes 786440 | tf_op jit(solution)/shard_map/ppermute | solution.py:610
  55.1 1.3 %query_product.1.after = bf16[128,1024]{1,0:T(8,128)(2,1)} custom-call(bf16[2,1088,128]{2,1,0:T(8,128)(2,1)S(1)} %get-tuple-element.29.keys, bf16[4,1088,256]{2,1,0:T(8,128)(2,1)S(1)} %get-tuple-element.30.dscores), custom_call_target="tpu_custom_call" | custom-call | tf_op jit(solution)/shard_map/query_product/pallas_call | solution.py:330
  56.4 9.3 %collective-permute-done.4.received = bf16[8,128,128]{2,1,0:T(8,128)(2,1)S(1)} collective-permute-done((bf16[8,128,128]{2,1,0:T(8,128)(2,1)S(1)}, bf16[8,128,128]{2,1,0:T(8,128)(2,1)S(1)}, u32[]{:S(2)}, u32[]{:S(2)}) %collective-permute-start.4) | collective-permute-done | bytes 262176 | tf_op jit(solution)/shard_map/ppermute | solution.py:610
  65.7 2.5 %sum_and_spread.1 = (bf16[128,128]{1,0:T(8,128)(2,1)}, bf16[8,128,128]{2,1,0:T(8,128)(2,1)}, f32[4,128,128]{2,1,0:T(8,128)S(1)}, bf16[4,128,128]{2,1,0:T(8,128)(2,1)S(1)}) custom-call(bf16[16,128,128]{2,1,0:T(8,128)(2,1)} %all-to-all-done.1.blocks, bf16[8,128,128]{2,1,0:T(8,128)(2,1)} %get-tuple-element.32.kept, ...), custom_call_target="tpu_custom_call" | custom-call | tf_op jit(solution)/shard_map/sum_and_spread/pallas_call | solution.py:528
  68.2 4.3 %all-to-all-start.2 = ((bf16[8,128,128]{2,1,0:T(8,128)(2,1)}), bf16[8,128,128]{2,1,0:T(8,128)(2,1)S(1)}, u32[]{:S(2)}, u32[]{:S(2)}) async-start(bf16[8,128,128]{2,1,0:T(8,128)(2,1)} %get-tuple-element.34), calls=%async_computation.2 | async-start | bytes 524288 | tf_op jit(solution)/shard_map/all_to_all | solution.py:601
  72.5 0.5 collective-permute-start.6
  73.0 1.6 %load_inputs.1.sources = bf16[4,256,1024]{2,1,0:T(8,128)(2,1)S(1)} custom-call(bf16[2,128,1024]{2,1,0:T(8,128)(2,1)} %get-tuple-element.25.zero, bf16[2,128,1024]{2,1,0:T(8,128)(2,1)} %collective-permute-done.1.one, bf16[2,128,1024]{2,1,0:T(8,128)(2,1)} %collective-permute-done.2.two, bf16[2,128,1024]{2,1,0:T(8,128)(2,1)} %collective-permute-done.3.three, ...), custom_call_target="tpu_custom_call" | custom-call | tf_op jit(solution)/shard_map/load_inputs/pallas_call | solution.py:426
  74.6 3.8 %collective-permute-done.6.received = bf16[4,128,128]{2,1,0:T(8,128)(2,1)S(1)} collective-permute-done((bf16[4,128,128]{2,1,0:T(8,128)(2,1)S(1)}, bf16[4,128,128]{2,1,0:T(8,128)(2,1)S(1)}, u32[]{:S(2)}, u32[]{:S(2)}) %collective-permute-start.6) | collective-permute-done | bytes 131104 | tf_op jit(solution)/shard_map/ppermute | solution.py:610
  78.4 1.6 %all-to-all-done.2.values = bf16[8,128,128]{2,1,0:T(8,128)(2,1)S(1)} async-done(((bf16[8,128,128]{2,1,0:T(8,128)(2,1)}), bf16[8,128,128]{2,1,0:T(8,128)(2,1)S(1)}, u32[]{:S(2)}, u32[]{:S(2)}) %all-to-all-start.2) | async-done | bytes 262176 | tf_op jit(solution)/shard_map/all_to_all | solution.py:601
  80.1 1.8 %weight_product.1 = (bf16[1024,128]{1,0:T(8,128)(2,1)}, f32[2,128,128]{2,1,0:T(8,128)S(1)}, bf16[2,128,128]{2,1,0:T(8,128)(2,1)S(1)}) custom-call(s32[2]{0:T(128)S(1)} %pad_add_fusion.1.place, bf16[8,128,128]{2,1,0:T(8,128)(2,1)S(1)} %all-to-all-done.2.values, bf16[4,256,1024]{2,1,0:T(8,128)(2,1)S(1)} %load_inputs.1.sources, ...), custom_call_target="tpu_custom_call" | custom-call | tf_op jit(solution)/shard_map/weight_product/pallas_call | solution.py:590
  81.9 1.3 %collective-permute-start.7 = (bf16[2,128,128]{2,1,0:T(8,128)(2,1)S(1)}, bf16[2,128,128]{2,1,0:T(8,128)(2,1)S(1)}, u32[]{:S(2)}, u32[]{:S(2)}) collective-permute-start(bf16[2,128,128]{2,1,0:T(8,128)(2,1)S(1)} %get-tuple-element.39), channel_id=1, source_target_pairs={{0,2},{1,3},{2,0},{3,1},{4,6},{5,7},{6,4},{7,5},{8,10},{9,11},{10,... | collective-permute-start | bytes 196616 | tf_op jit(solution)/shard_map/ppermute | solution.py:610
  83.1 7.2 %all-to-all-start.3 = ((bf16[32,32,128]{2,1,0:T(8,128)(2,1)}), bf16[32,32,128]{2,1,0:T(8,128)(2,1)S(1)}, u32[]{:S(2)}, u32[]{:S(2)}) async-start(bf16[32,32,128]{2,1,0:T(8,128)(2,1)} %bitcast.12), calls=%async_computation.3 | async-start | bytes 524288 | tf_op jit(solution)/shard_map/all_to_all | solution.py:601
  90.4 3.7 %collective-permute-start.8 = (bf16[1,128,128]{2,1,0:T(8,128)(2,1)S(1)}, bf16[1,128,128]{2,1,0:T(8,128)(2,1)S(1)}, u32[]{:S(2)}, u32[]{:S(2)}) collective-permute-start(bf16[1,128,128]{2,1,0:T(8,128)(2,1)S(1)} %slice.15), channel_id=1, source_target_pairs={{0,7},{1,6},{2,5},{3,4},{4,3},{5,2},{6,1},{7,0},{8,15},{9,14},{10,... | collective-permute-start | bytes 98312 | tf_op jit(solution)/shard_map/ppermute | solution.py:610
  94.0 5.6 %collective-permute-done.8 = bf16[1,128,128]{2,1,0:T(8,128)(2,1)S(1)} collective-permute-done((bf16[1,128,128]{2,1,0:T(8,128)(2,1)S(1)}, bf16[1,128,128]{2,1,0:T(8,128)(2,1)S(1)}, u32[]{:S(2)}, u32[]{:S(2)}) %collective-permute-start.8) | collective-permute-done | bytes 32800 | tf_op jit(solution)/shard_map/ppermute | solution.py:610
  99.6 0.6 fusion
  100.2 3.2 %all-to-all-done.3 = bf16[32,32,128]{2,1,0:T(8,128)(2,1)S(1)} async-done(((bf16[32,32,128]{2,1,0:T(8,128)(2,1)}), bf16[32,32,128]{2,1,0:T(8,128)(2,1)S(1)}, u32[]{:S(2)}, u32[]{:S(2)}) %all-to-all-start.3) | async-done | bytes 262176 | tf_op jit(solution)/shard_map/all_to_all | solution.py:601
  103.4 0.7 convert_reduce_fusion
  (12 shorter events, 0.0 us)
Async XLA Ops:
  0.6 21.1 %copy-start = (s32[1,8]{1,0:T(1,128)S(1)}, s32[1,8]{1,0:T(1,128)}, u32[]{:S(2)}) copy-start(s32[1,8]{1,0:T(1,128)} %param.14) | copy-start | bytes 100
  0.6 21.1 %copy-start.1 = (s32[32]{0:T(128)S(1)}, s32[32]{0:T(128)}, u32[]{:S(2)}) copy-start(s32[32]{0:T(128)} %param.15) | copy-start | bytes 388
  2.5 33.5 %all-to-all-start = ((bf16[16,192,128]{2,1,0:T(8,128)(2,1)}), bf16[16,192,128]{2,1,0:T(8,128)(2,1)S(1)}, u32[]{:S(2)}, u32[]{:S(2)}) async-start(bf16[16,192,128]{2,1,0:T(8,128)(2,1)} %join_keys_values.1), calls=%async_computation | async-start | bytes 1572864 | tf_op jit(solution)/shard_map/all_to_all | solution.py:601
  16.9 30.6 %collective-permute-start.1 = (bf16[2,128,1024]{2,1,0:T(8,128)(2,1)}, bf16[2,128,1024]{2,1,0:T(8,128)(2,1)}, u32[]{:S(2)}, u32[]{:S(2)}) collective-permute-start(bf16[2,128,1024]{2,1,0:T(8,128)(2,1)} %get-tuple-element.26), channel_id=1, source_target_pairs={{0,32},{32,0},{64,96},{96,64},{1,33},{33,1},{65,97},{97,65},{2,34}... | collective-permute-start | bytes 1572872 | tf_op jit(solution)/shard_map/ppermute | solution.py:610
  18.5 29.1 %collective-permute-start.2 = (bf16[2,128,1024]{2,1,0:T(8,128)(2,1)}, bf16[2,128,1024]{2,1,0:T(8,128)(2,1)}, u32[]{:S(2)}, u32[]{:S(2)}) collective-permute-start(bf16[2,128,1024]{2,1,0:T(8,128)(2,1)} %get-tuple-element.27), channel_id=1, source_target_pairs={{0,64},{32,96},{64,0},{96,32},{1,65},{33,97},{65,1},{97,33},{2,66}... | collective-permute-start | bytes 1572872 | tf_op jit(solution)/shard_map/ppermute | solution.py:610
  21.2 26.3 %collective-permute-start.3 = (bf16[2,128,1024]{2,1,0:T(8,128)(2,1)}, bf16[2,128,1024]{2,1,0:T(8,128)(2,1)}, u32[]{:S(2)}, u32[]{:S(2)}) collective-permute-start(bf16[2,128,1024]{2,1,0:T(8,128)(2,1)} %get-tuple-element.28), channel_id=1, source_target_pairs={{0,96},{32,64},{64,32},{96,0},{1,97},{33,65},{65,33},{97,1},{2,98}... | collective-permute-start | bytes 1572872 | tf_op jit(solution)/shard_map/ppermute | solution.py:610
  40.8 8.2 %collective-permute-start = (bf16[16,64,128]{2,1,0:T(8,128)(2,1)}, bf16[16,64,128]{2,1,0:T(8,128)(2,1)S(1)}, u32[]{:S(2)}, u32[]{:S(2)}) collective-permute-start(bf16[16,64,128]{2,1,0:T(8,128)(2,1)} %get-tuple-element.23), channel_id=1, source_target_pairs={{0,8},{8,0},{1,9},{9,1},{2,10},{10,2},{3,11},{11,3},{4,12},{12,4},... | collective-permute-start | bytes 786440 | tf_op jit(solution)/shard_map/ppermute | solution.py:610
  42.2 23.6 %all-to-all-start.1 = ((bf16[16,128,128]{2,1,0:T(8,128)(2,1)}), bf16[16,128,128]{2,1,0:T(8,128)(2,1)}, u32[]{:S(2)}, u32[]{:S(2)}) async-start(bf16[16,128,128]{2,1,0:T(8,128)(2,1)} %bitcast.18), calls=%async_computation.1 | async-start | bytes 1048576 | tf_op jit(solution)/shard_map/all_to_all | solution.py:601
  53.3 19.8 %collective-permute-start.5 = (bf16[4,128,1024]{2,1,0:T(8,128)(2,1)}, bf16[4,128,1024]{2,1,0:T(8,128)(2,1)}, u32[]{:S(2)}, u32[]{:S(2)}) collective-permute-start(bf16[4,128,1024]{2,1,0:T(8,128)(2,1)} %get-tuple-element.35), channel_id=1, source_target_pairs={{0,16},{16,0},{1,17},{17,1},{2,18},{18,2},{3,19},{19,3},{4,20},{20... | collective-permute-start | bytes 3145736 | tf_op jit(solution)/shard_map/ppermute | solution.py:610
  53.4 12.4 %collective-permute-start.4 = (bf16[8,128,128]{2,1,0:T(8,128)(2,1)S(1)}, bf16[8,128,128]{2,1,0:T(8,128)(2,1)S(1)}, u32[]{:S(2)}, u32[]{:S(2)}) collective-permute-start(bf16[8,128,128]{2,1,0:T(8,128)(2,1)S(1)} %get-tuple-element.33), channel_id=1, source_target_pairs={{0,8},{8,0},{1,9},{9,1},{2,10},{10,2},{3,11},{11,3},{4,12},{12,4},... | collective-permute-start | bytes 786440 | tf_op jit(solution)/shard_map/ppermute | solution.py:610
  68.2 11.9 %all-to-all-start.2 = ((bf16[8,128,128]{2,1,0:T(8,128)(2,1)}), bf16[8,128,128]{2,1,0:T(8,128)(2,1)S(1)}, u32[]{:S(2)}, u32[]{:S(2)}) async-start(bf16[8,128,128]{2,1,0:T(8,128)(2,1)} %get-tuple-element.34), calls=%async_computation.2 | async-start | bytes 524288 | tf_op jit(solution)/shard_map/all_to_all | solution.py:601
  72.5 5.9 %collective-permute-start.6 = (bf16[4,128,128]{2,1,0:T(8,128)(2,1)S(1)}, bf16[4,128,128]{2,1,0:T(8,128)(2,1)S(1)}, u32[]{:S(2)}, u32[]{:S(2)}) collective-permute-start(bf16[4,128,128]{2,1,0:T(8,128)(2,1)S(1)} %get-tuple-element.37), channel_id=1, source_target_pairs={{0,1},{1,0},{2,3},{3,2},{4,5},{5,4},{6,7},{7,6},{8,9},{9,8},{10,11... | collective-permute-start | bytes 393224 | tf_op jit(solution)/shard_map/ppermute | solution.py:610
  81.9 8.5 %collective-permute-start.7 = (bf16[2,128,128]{2,1,0:T(8,128)(2,1)S(1)}, bf16[2,128,128]{2,1,0:T(8,128)(2,1)S(1)}, u32[]{:S(2)}, u32[]{:S(2)}) collective-permute-start(bf16[2,128,128]{2,1,0:T(8,128)(2,1)S(1)} %get-tuple-element.39), channel_id=1, source_target_pairs={{0,2},{1,3},{2,0},{3,1},{4,6},{5,7},{6,4},{7,5},{8,10},{9,11},{10,... | collective-permute-start | bytes 196616 | tf_op jit(solution)/shard_map/ppermute | solution.py:610
  83.1 20.3 %all-to-all-start.3 = ((bf16[32,32,128]{2,1,0:T(8,128)(2,1)}), bf16[32,32,128]{2,1,0:T(8,128)(2,1)S(1)}, u32[]{:S(2)}, u32[]{:S(2)}) async-start(bf16[32,32,128]{2,1,0:T(8,128)(2,1)} %bitcast.12), calls=%async_computation.3 | async-start | bytes 524288 | tf_op jit(solution)/shard_map/all_to_all | solution.py:601
  90.4 9.3 %collective-permute-start.8 = (bf16[1,128,128]{2,1,0:T(8,128)(2,1)S(1)}, bf16[1,128,128]{2,1,0:T(8,128)(2,1)S(1)}, u32[]{:S(2)}, u32[]{:S(2)}) collective-permute-start(bf16[1,128,128]{2,1,0:T(8,128)(2,1)S(1)} %slice.15), channel_id=1, source_target_pairs={{0,7},{1,6},{2,5},{3,4},{4,3},{5,2},{6,1},{7,0},{8,15},{9,14},{10,... | collective-permute-start | bytes 98312 | tf_op jit(solution)/shard_map/ppermute | solution.py:610

commit v7 on v6

--- a/solution.py
+++ b/solution.py
@@ -597,12 +597,30 @@
     )(place, values, in_vmem(sources), kept, received)
 
 
+def last_sums_kernel(blocks, kept, received, weight_grad, key_grad):
+    total = blocks[0].astype(jnp.float32)
+    for block in range(1, blocks.shape[0]):
+        total = total + blocks[block].astype(jnp.float32)
+    weight_grad[...] = total
+    key_grad[...] = (kept[:1] + received[...].astype(jnp.float32)).astype(jnp.bfloat16)
+
+
+def last_sums(blocks, kept, received):
+    return pl.pallas_call(
+        last_sums_kernel,
+        in_specs=[VMEM_SPEC] * 3,
+        out_specs=[VMEM_SPEC] * 2,
+        out_shape=[
+            jax.ShapeDtypeStruct(blocks.shape[1:], jnp.float32),
+            jax.ShapeDtypeStruct(received.shape, jnp.bfloat16),
+        ],
+        compiler_params=PARAMS,
+        name="last_sums",
+    )(blocks, kept, received)
+
+
 def exchange(blocks, axes):
     return lax.all_to_all(blocks, axes, 0, 0, tiled=False)
-
-
-def summed(blocks):
-    return jnp.sum(blocks.astype(jnp.float32), axis=0)
 
 
 def swapped(block, axis, shift):
@@ -639,8 +657,7 @@
     weight_blocks = exchange(weight_part.reshape(far_count, -1, HEAD_SIZE), FAR)
     key_sum = key_kept + swapped(key_sent, "z", 2).astype(jnp.float32)
     received = swapped(key_sum[1:].astype(jnp.bfloat16), "z", 7)
-    key_grad = (key_sum[:1] + received.astype(jnp.float32)).astype(jnp.bfloat16)
-    weight_grad = summed(weight_blocks)
+    weight_grad, key_grad = last_sums(weight_blocks, key_sum, received)
     return query_grad[None], key_grad, value_grad[None], weight_grad
 
 

time: 105 us -> 107 us (1.019)
  starting transfers between devices: 41.5 us -> 43.5 us
  other arithmetic: 1.44 us -> 0.16 us
    all_to_all x4, waiting for transfers between devices: 19 us -> 15.8 us  [exchange(): return lax.all_to_all(blocks, axes, 0, 0, tiled=False)]
    ppermute x9, waiting for transfers between devices: 20.1 us -> 23.3 us  [swapped(): return lax.ppermute(block, axis, [(i, i ^ shift) for i in range(count)])]
    ppermute x9, starting transfers between devices: 13.4 us -> 15.3 us  [swapped(): return lax.ppermute(block, axis, [(i, i ^ shift) for i in range(count)])]
  transfers between devices with their start and end apart: 13 -> 13, of which waited for: 7 -> 7; matrix products, arithmetic and copies ran while one was open for 1% -> 0% of each run, Pallas kernels for 17% -> 17%
where the time goes in v7:
time: 107 us; the launch traced here: 105 us
  starting transfers between devices  43.5 us (41%)
  waiting for transfers between devices  39.1 us (37%)
  Pallas kernels  21.9 us (20%)
    all_to_all x4, starting transfers between devices, exchange(): return lax.all_to_all(blocks, axes, 0, 0, tiled=False)  28.2 us
    ppermute x9, waiting for transfers between devices, swapped(): return lax.ppermute(block, axis, [(i, i ^ shift) for i in range(count)])  23.3 us
    all_to_all x4, waiting for transfers between devices, exchange(): return lax.all_to_all(blocks, axes, 0, 0, tiled=False)  15.8 us
    ppermute x9, starting transfers between devices, swapped(): return lax.ppermute(block, axis, [(i, i ^ shift) for i in range(count)])  15.3 us
    pallas_call x1, Pallas kernels, attention_probs(): pl.pallas_call(probs_kernel, in_specs=[SMEM_SPEC, HBM_SPEC, HBM_SPEC, VME...  4.78 us
    pallas_call x1, Pallas kernels, attention_grads(): pl.pallas_call(grads_kernel, in_specs=[SMEM_SPEC] + [HBM_SPEC] * 3 + [VME...  4.32 us
    pallas_call x1, Pallas kernels, split_inputs(): pl.pallas_call(split_kernel, in_specs=[SMEM_SPEC, HBM_SPEC], out_specs=[H...  3.14 us
    pallas_call x1, Pallas kernels, sum_and_spread(): pl.pallas_call(spread_kernel, in_specs=[HBM_SPEC, HBM_SPEC, VMEM_SPEC, HB...  2.49 us
  transfers between devices with their start and end apart: 13, of which 7 were waited for; matrix products, arithmetic and copies ran while one was open for 0% of the time, Pallas kernels for 17%

profile of v7, /device:TPU:32, one launch (start us, length us, event | category | flops | bytes accessed | tf_op | source)
XLA Modules:
  0.0 105.4 jit_solution(17050115965851316446)
XLA Ops:
  0.7 1.8 %join_keys_values.1 = bf16[16,192,128]{2,1,0:T(8,128)(2,1)} custom-call(bf16[128,128]{1,0:T(8,128)(2,1)} %bitcast.20, bf16[128,128]{1,0:T(8,128)(2,1)} %bitcast.21), custom_call_target="tpu_custom_call" | custom-call | tf_op jit(solution)/shard_map/join_keys_values/pallas_call | solution.py:561
  2.5 11.2 %all-to-all-start = ((bf16[16,192,128]{2,1,0:T(8,128)(2,1)}), bf16[16,192,128]{2,1,0:T(8,128)(2,1)S(1)}, u32[]{:S(2)}, u32[]{:S(2)}) async-start(bf16[16,192,128]{2,1,0:T(8,128)(2,1)} %join_keys_values.1), calls=%async_computation | async-start | bytes 1572864 | tf_op jit(solution)/shard_map/all_to_all | solution.py:623
  13.7 0.1 pad_add_fusion.1.place
  13.8 3.1 %split_inputs.1 = (bf16[2,128,1024]{2,1,0:T(8,128)(2,1)}, bf16[2,128,1024]{2,1,0:T(8,128)(2,1)}, bf16[2,128,1024]{2,1,0:T(8,128)(2,1)}, bf16[2,128,1024]{2,1,0:T(8,128)(2,1)}) custom-call(s32[2]{0:T(128)S(1)} %pad_add_fusion.1.place, bf16[128,8192]{1,0:T(8,128)(2,1)} %inputs.1), custom_call_target="tpu_custom_call" | custom-call | tf_op jit(solution)/shard_map/split_inputs/pallas_call | solution.py:467
  16.9 1.6 %collective-permute-start.1 = (bf16[2,128,1024]{2,1,0:T(8,128)(2,1)}, bf16[2,128,1024]{2,1,0:T(8,128)(2,1)}, u32[]{:S(2)}, u32[]{:S(2)}) collective-permute-start(bf16[2,128,1024]{2,1,0:T(8,128)(2,1)} %get-tuple-element.28), channel_id=1, source_target_pairs={{0,32},{32,0},{64,96},{96,64},{1,33},{33,1},{65,97},{97,65},{2,34}... | collective-permute-start | bytes 1572872 | tf_op jit(solution)/shard_map/ppermute | solution.py:628
  18.5 2.7 %collective-permute-start.2 = (bf16[2,128,1024]{2,1,0:T(8,128)(2,1)}, bf16[2,128,1024]{2,1,0:T(8,128)(2,1)}, u32[]{:S(2)}, u32[]{:S(2)}) collective-permute-start(bf16[2,128,1024]{2,1,0:T(8,128)(2,1)} %get-tuple-element.29), channel_id=1, source_target_pairs={{0,64},{32,96},{64,0},{96,32},{1,65},{33,97},{65,1},{97,33},{2,66}... | collective-permute-start | bytes 1572872 | tf_op jit(solution)/shard_map/ppermute | solution.py:628
  21.2 0.5 collective-permute-start.3
  21.7 0.1 pad_add_fusion.scalars
  21.8 14.2 %all-to-all-done.kv = bf16[16,192,128]{2,1,0:T(8,128)(2,1)S(1)} async-done(((bf16[16,192,128]{2,1,0:T(8,128)(2,1)}), bf16[16,192,128]{2,1,0:T(8,128)(2,1)S(1)}, u32[]{:S(2)}, u32[]{:S(2)}) %all-to-all-start) | async-done | bytes 786464 | tf_op jit(solution)/shard_map/all_to_all | solution.py:623
  36.0 4.8 %probs_and_value_part.1 = (bf16[4,1104,256]{2,1,0:T(8,128)(2,1)S(1)}, bf16[2048,128]{1,0:T(8,128)(2,1)}, bf16[16,64,128]{2,1,0:T(8,128)(2,1)}) custom-call(s32[41]{0:T(128)S(1)} %pad_add_fusion.scalars, bf16[128,1024]{1,0:T(8,128)(2,1)} %bitcast.13, bf16[128,1024]{1,0:T(8,128)(2,1)} %bitcast.15, bf16[16,192,128]{2,1,0:T(8,128)(2,1)S(1)} %all-to-all-done.kv), custom_call_target="tpu_custom_call" | custom-call | tf_op jit(solution)/shard_map/probs_and_value_part/pallas_call | solution.py:360
  40.8 1.4 %collective-permute-start = (bf16[16,64,128]{2,1,0:T(8,128)(2,1)}, bf16[16,64,128]{2,1,0:T(8,128)(2,1)S(1)}, u32[]{:S(2)}, u32[]{:S(2)}) collective-permute-start(bf16[16,64,128]{2,1,0:T(8,128)(2,1)} %get-tuple-element.25), channel_id=1, source_target_pairs={{0,8},{8,0},{1,9},{9,1},{2,10},{10,2},{3,11},{11,3},{4,12},{12,4},... | collective-permute-start | bytes 786440 | tf_op jit(solution)/shard_map/ppermute | solution.py:628
  42.2 5.4 %all-to-all-start.1 = ((bf16[16,128,128]{2,1,0:T(8,128)(2,1)}), bf16[16,128,128]{2,1,0:T(8,128)(2,1)}, u32[]{:S(2)}, u32[]{:S(2)}) async-start(bf16[16,128,128]{2,1,0:T(8,128)(2,1)} %bitcast.18), calls=%async_computation.1 | async-start | bytes 1048576 | tf_op jit(solution)/shard_map/all_to_all | solution.py:623
  47.5 0.0 collective-permute-done.1.one
  47.6 1.4 %collective-permute-done.far_values = bf16[16,64,128]{2,1,0:T(8,128)(2,1)S(1)} collective-permute-done((bf16[16,64,128]{2,1,0:T(8,128)(2,1)}, bf16[16,64,128]{2,1,0:T(8,128)(2,1)S(1)}, u32[]{:S(2)}, u32[]{:S(2)}) %collective-permute-start) | collective-permute-done | bytes 262176 | tf_op jit(solution)/shard_map/ppermute | solution.py:628
  48.9 4.3 %key_part.1 = (bf16[8,128,128]{2,1,0:T(8,128)(2,1)S(1)}, bf16[8,128,128]{2,1,0:T(8,128)(2,1)}, bf16[4,128,1024]{2,1,0:T(8,128)(2,1)}, bf16[4,1088,256]{2,1,0:T(8,128)(2,1)S(1)}, bf16[2,1088,128]{2,1,0:T(8,128)(2,1)S(1)}) custom-call(s32[41]{0:T(128)S(1)} %pad_add_fusion.scalars, bf16[128,1024]{1,0:T(8,128)(2,1)} %bitcast.14, bf16[128,1024]{1,0:T(8,128)(2,1)} %bitcast.19, ...), custom_call_target="tpu_custom_call" | custom-call | tf_op jit(solution)/shard_map/key_part/pallas_call | solution.py:386
  53.3 0.1 collective-permute-start.5
  53.4 1.7 %collective-permute-start.4 = (bf16[8,128,128]{2,1,0:T(8,128)(2,1)S(1)}, bf16[8,128,128]{2,1,0:T(8,128)(2,1)S(1)}, u32[]{:S(2)}, u32[]{:S(2)}) collective-permute-start(bf16[8,128,128]{2,1,0:T(8,128)(2,1)S(1)} %get-tuple-element.35), channel_id=1, source_target_pairs={{0,8},{8,0},{1,9},{9,1},{2,10},{10,2},{3,11},{11,3},{4,12},{12,4},... | collective-permute-start | bytes 786440 | tf_op jit(solution)/shard_map/ppermute | solution.py:628
  55.1 1.3 %query_product.1.after = bf16[128,1024]{1,0:T(8,128)(2,1)} custom-call(bf16[2,1088,128]{2,1,0:T(8,128)(2,1)S(1)} %get-tuple-element.31.keys, bf16[4,1088,256]{2,1,0:T(8,128)(2,1)S(1)} %get-tuple-element.32.dscores), custom_call_target="tpu_custom_call" | custom-call | tf_op jit(solution)/shard_map/query_product/pallas_call | solution.py:330
  56.4 9.3 %collective-permute-done.4.received = bf16[8,128,128]{2,1,0:T(8,128)(2,1)S(1)} collective-permute-done((bf16[8,128,128]{2,1,0:T(8,128)(2,1)S(1)}, bf16[8,128,128]{2,1,0:T(8,128)(2,1)S(1)}, u32[]{:S(2)}, u32[]{:S(2)}) %collective-permute-start.4) | collective-permute-done | bytes 262176 | tf_op jit(solution)/shard_map/ppermute | solution.py:628
  65.7 2.5 %sum_and_spread.1 = (bf16[128,128]{1,0:T(8,128)(2,1)}, bf16[8,128,128]{2,1,0:T(8,128)(2,1)}, f32[4,128,128]{2,1,0:T(8,128)S(1)}, bf16[4,128,128]{2,1,0:T(8,128)(2,1)S(1)}) custom-call(bf16[16,128,128]{2,1,0:T(8,128)(2,1)} %all-to-all-done.1.blocks, bf16[8,128,128]{2,1,0:T(8,128)(2,1)} %get-tuple-element.34.kept, ...), custom_call_target="tpu_custom_call" | custom-call | tf_op jit(solution)/shard_map/sum_and_spread/pallas_call | solution.py:528
  68.2 4.3 %all-to-all-start.2 = ((bf16[8,128,128]{2,1,0:T(8,128)(2,1)}), bf16[8,128,128]{2,1,0:T(8,128)(2,1)S(1)}, u32[]{:S(2)}, u32[]{:S(2)}) async-start(bf16[8,128,128]{2,1,0:T(8,128)(2,1)} %get-tuple-element.36), calls=%async_computation.2 | async-start | bytes 524288 | tf_op jit(solution)/shard_map/all_to_all | solution.py:623
  72.5 0.5 collective-permute-start.6
  73.0 1.6 %load_inputs.1.sources = bf16[4,256,1024]{2,1,0:T(8,128)(2,1)S(1)} custom-call(bf16[2,128,1024]{2,1,0:T(8,128)(2,1)} %get-tuple-element.27.zero, bf16[2,128,1024]{2,1,0:T(8,128)(2,1)} %collective-permute-done.1.one, bf16[2,128,1024]{2,1,0:T(8,128)(2,1)} %collective-permute-done.2.two, bf16[2,128,1024]{2,1,0:T(8,128)(2,1)} %collective-permute-done.3.three, ...), custom_call_target="tpu_custom_call" | custom-call | tf_op jit(solution)/shard_map/load_inputs/pallas_call | solution.py:426
  74.6 3.8 %collective-permute-done.6.received = bf16[4,128,128]{2,1,0:T(8,128)(2,1)S(1)} collective-permute-done((bf16[4,128,128]{2,1,0:T(8,128)(2,1)S(1)}, bf16[4,128,128]{2,1,0:T(8,128)(2,1)S(1)}, u32[]{:S(2)}, u32[]{:S(2)}) %collective-permute-start.6) | collective-permute-done | bytes 131104 | tf_op jit(solution)/shard_map/ppermute | solution.py:628
  78.4 1.6 %all-to-all-done.2.values = bf16[8,128,128]{2,1,0:T(8,128)(2,1)S(1)} async-done(((bf16[8,128,128]{2,1,0:T(8,128)(2,1)}), bf16[8,128,128]{2,1,0:T(8,128)(2,1)S(1)}, u32[]{:S(2)}, u32[]{:S(2)}) %all-to-all-start.2) | async-done | bytes 262176 | tf_op jit(solution)/shard_map/all_to_all | solution.py:623
  80.1 1.8 %weight_product.1 = (bf16[1024,128]{1,0:T(8,128)(2,1)}, f32[2,128,128]{2,1,0:T(8,128)S(1)}, bf16[2,128,128]{2,1,0:T(8,128)(2,1)S(1)}) custom-call(s32[2]{0:T(128)S(1)} %pad_add_fusion.1.place, bf16[8,128,128]{2,1,0:T(8,128)(2,1)S(1)} %all-to-all-done.2.values, bf16[4,256,1024]{2,1,0:T(8,128)(2,1)S(1)} %load_inputs.1.sources, ...), custom_call_target="tpu_custom_call" | custom-call | tf_op jit(solution)/shard_map/weight_product/pallas_call | solution.py:590
  81.9 7.3 %all-to-all-start.3 = ((bf16[32,32,128]{2,1,0:T(8,128)(2,1)}), bf16[32,32,128]{2,1,0:T(8,128)(2,1)S(1)}, u32[]{:S(2)}, u32[]{:S(2)}) async-start(bf16[32,32,128]{2,1,0:T(8,128)(2,1)} %bitcast.11), calls=%async_computation.3 | async-start | bytes 524288 | tf_op jit(solution)/shard_map/all_to_all | solution.py:623
  89.2 2.4 %collective-permute-start.7 = (bf16[2,128,128]{2,1,0:T(8,128)(2,1)S(1)}, bf16[2,128,128]{2,1,0:T(8,128)(2,1)S(1)}, u32[]{:S(2)}, u32[]{:S(2)}) collective-permute-start(bf16[2,128,128]{2,1,0:T(8,128)(2,1)S(1)} %get-tuple-element.42), channel_id=1, source_target_pairs={{0,2},{1,3},{2,0},{3,1},{4,6},{5,7},{6,4},{7,5},{8,10},{9,11},{10,... | collective-permute-start | bytes 196616 | tf_op jit(solution)/shard_map/ppermute | solution.py:628
  91.6 6.1 %collective-permute-done.7 = bf16[2,128,128]{2,1,0:T(8,128)(2,1)S(1)} collective-permute-done((bf16[2,128,128]{2,1,0:T(8,128)(2,1)S(1)}, bf16[2,128,128]{2,1,0:T(8,128)(2,1)S(1)}, u32[]{:S(2)}, u32[]{:S(2)}) %collective-permute-start.7) | collective-permute-done | bytes 65568 | tf_op jit(solution)/shard_map/ppermute | solution.py:628
  97.8 4.3 %collective-permute-start.8 = (bf16[1,128,128]{2,1,0:T(8,128)(2,1)S(1)}, bf16[1,128,128]{2,1,0:T(8,128)(2,1)S(1)}, u32[]{:S(2)}, u32[]{:S(2)}) collective-permute-start(bf16[1,128,128]{2,1,0:T(8,128)(2,1)S(1)} %slice.7), channel_id=1, source_target_pairs={{0,7},{1,6},{2,5},{3,4},{4,3},{5,2},{6,1},{7,0},{8,15},{9,14},{10,... | collective-permute-start | bytes 98312 | tf_op jit(solution)/shard_map/ppermute | solution.py:628
  102.1 2.7 %collective-permute-done.8.received = bf16[1,128,128]{2,1,0:T(8,128)(2,1)S(1)} collective-permute-done((bf16[1,128,128]{2,1,0:T(8,128)(2,1)S(1)}, bf16[1,128,128]{2,1,0:T(8,128)(2,1)S(1)}, u32[]{:S(2)}, u32[]{:S(2)}) %collective-permute-start.8) | collective-permute-done | bytes 32800 | tf_op jit(solution)/shard_map/ppermute | solution.py:628
  104.8 0.7 last_sums.1
  (11 shorter events, 0.0 us)
Async XLA Ops:
  0.6 21.1 %copy-start = (s32[1,8]{1,0:T(1,128)S(1)}, s32[1,8]{1,0:T(1,128)}, u32[]{:S(2)}) copy-start(s32[1,8]{1,0:T(1,128)} %param.14) | copy-start | bytes 100
  0.6 21.1 %copy-start.1 = (s32[32]{0:T(128)S(1)}, s32[32]{0:T(128)}, u32[]{:S(2)}) copy-start(s32[32]{0:T(128)} %param.15) | copy-start | bytes 388
  2.5 33.5 %all-to-all-start = ((bf16[16,192,128]{2,1,0:T(8,128)(2,1)}), bf16[16,192,128]{2,1,0:T(8,128)(2,1)S(1)}, u32[]{:S(2)}, u32[]{:S(2)}) async-start(bf16[16,192,128]{2,1,0:T(8,128)(2,1)} %join_keys_values.1), calls=%async_computation | async-start | bytes 1572864 | tf_op jit(solution)/shard_map/all_to_all | solution.py:623
  16.9 30.6 %collective-permute-start.1 = (bf16[2,128,1024]{2,1,0:T(8,128)(2,1)}, bf16[2,128,1024]{2,1,0:T(8,128)(2,1)}, u32[]{:S(2)}, u32[]{:S(2)}) collective-permute-start(bf16[2,128,1024]{2,1,0:T(8,128)(2,1)} %get-tuple-element.28), channel_id=1, source_target_pairs={{0,32},{32,0},{64,96},{96,64},{1,33},{33,1},{65,97},{97,65},{2,34}... | collective-permute-start | bytes 1572872 | tf_op jit(solution)/shard_map/ppermute | solution.py:628
  18.5 29.0 %collective-permute-start.2 = (bf16[2,128,1024]{2,1,0:T(8,128)(2,1)}, bf16[2,128,1024]{2,1,0:T(8,128)(2,1)}, u32[]{:S(2)}, u32[]{:S(2)}) collective-permute-start(bf16[2,128,1024]{2,1,0:T(8,128)(2,1)} %get-tuple-element.29), channel_id=1, source_target_pairs={{0,64},{32,96},{64,0},{96,32},{1,65},{33,97},{65,1},{97,33},{2,66}... | collective-permute-start | bytes 1572872 | tf_op jit(solution)/shard_map/ppermute | solution.py:628
  21.2 26.3 %collective-permute-start.3 = (bf16[2,128,1024]{2,1,0:T(8,128)(2,1)}, bf16[2,128,1024]{2,1,0:T(8,128)(2,1)}, u32[]{:S(2)}, u32[]{:S(2)}) collective-permute-start(bf16[2,128,1024]{2,1,0:T(8,128)(2,1)} %get-tuple-element.30), channel_id=1, source_target_pairs={{0,96},{32,64},{64,32},{96,0},{1,97},{33,65},{65,33},{97,1},{2,98}... | collective-permute-start | bytes 1572872 | tf_op jit(solution)/shard_map/ppermute | solution.py:628
  40.8 8.2 %collective-permute-start = (bf16[16,64,128]{2,1,0:T(8,128)(2,1)}, bf16[16,64,128]{2,1,0:T(8,128)(2,1)S(1)}, u32[]{:S(2)}, u32[]{:S(2)}) collective-permute-start(bf16[16,64,128]{2,1,0:T(8,128)(2,1)} %get-tuple-element.25), channel_id=1, source_target_pairs={{0,8},{8,0},{1,9},{9,1},{2,10},{10,2},{3,11},{11,3},{4,12},{12,4},... | collective-permute-start | bytes 786440 | tf_op jit(solution)/shard_map/ppermute | solution.py:628
  42.2 23.6 %all-to-all-start.1 = ((bf16[16,128,128]{2,1,0:T(8,128)(2,1)}), bf16[16,128,128]{2,1,0:T(8,128)(2,1)}, u32[]{:S(2)}, u32[]{:S(2)}) async-start(bf16[16,128,128]{2,1,0:T(8,128)(2,1)} %bitcast.18), calls=%async_computation.1 | async-start | bytes 1048576 | tf_op jit(solution)/shard_map/all_to_all | solution.py:623
  53.3 19.8 %collective-permute-start.5 = (bf16[4,128,1024]{2,1,0:T(8,128)(2,1)}, bf16[4,128,1024]{2,1,0:T(8,128)(2,1)}, u32[]{:S(2)}, u32[]{:S(2)}) collective-permute-start(bf16[4,128,1024]{2,1,0:T(8,128)(2,1)} %get-tuple-element.37), channel_id=1, source_target_pairs={{0,16},{16,0},{1,17},{17,1},{2,18},{18,2},{3,19},{19,3},{4,20},{20... | collective-permute-start | bytes 3145736 | tf_op jit(solution)/shard_map/ppermute | solution.py:628
  53.4 12.4 %collective-permute-start.4 = (bf16[8,128,128]{2,1,0:T(8,128)(2,1)S(1)}, bf16[8,128,128]{2,1,0:T(8,128)(2,1)S(1)}, u32[]{:S(2)}, u32[]{:S(2)}) collective-permute-start(bf16[8,128,128]{2,1,0:T(8,128)(2,1)S(1)} %get-tuple-element.35), channel_id=1, source_target_pairs={{0,8},{8,0},{1,9},{9,1},{2,10},{10,2},{3,11},{11,3},{4,12},{12,4},... | collective-permute-start | bytes 786440 | tf_op jit(solution)/shard_map/ppermute | solution.py:628
  68.2 11.9 %all-to-all-start.2 = ((bf16[8,128,128]{2,1,0:T(8,128)(2,1)}), bf16[8,128,128]{2,1,0:T(8,128)(2,1)S(1)}, u32[]{:S(2)}, u32[]{:S(2)}) async-start(bf16[8,128,128]{2,1,0:T(8,128)(2,1)} %get-tuple-element.36), calls=%async_computation.2 | async-start | bytes 524288 | tf_op jit(solution)/shard_map/all_to_all | solution.py:623
  72.5 5.9 %collective-permute-start.6 = (bf16[4,128,128]{2,1,0:T(8,128)(2,1)S(1)}, bf16[4,128,128]{2,1,0:T(8,128)(2,1)S(1)}, u32[]{:S(2)}, u32[]{:S(2)}) collective-permute-start(bf16[4,128,128]{2,1,0:T(8,128)(2,1)S(1)} %get-tuple-element.39), channel_id=1, source_target_pairs={{0,1},{1,0},{2,3},{3,2},{4,5},{5,4},{6,7},{7,6},{8,9},{9,8},{10,11... | collective-permute-start | bytes 393224 | tf_op jit(solution)/shard_map/ppermute | solution.py:628
  81.9 22.9 %all-to-all-start.3 = ((bf16[32,32,128]{2,1,0:T(8,128)(2,1)}), bf16[32,32,128]{2,1,0:T(8,128)(2,1)S(1)}, u32[]{:S(2)}, u32[]{:S(2)}) async-start(bf16[32,32,128]{2,1,0:T(8,128)(2,1)} %bitcast.11), calls=%async_computation.3 | async-start | bytes 524288 | tf_op jit(solution)/shard_map/all_to_all | solution.py:623
  89.2 8.6 %collective-permute-start.7 = (bf16[2,128,128]{2,1,0:T(8,128)(2,1)S(1)}, bf16[2,128,128]{2,1,0:T(8,128)(2,1)S(1)}, u32[]{:S(2)}, u32[]{:S(2)}) collective-permute-start(bf16[2,128,128]{2,1,0:T(8,128)(2,1)S(1)} %get-tuple-element.42), channel_id=1, source_target_pairs={{0,2},{1,3},{2,0},{3,1},{4,6},{5,7},{6,4},{7,5},{8,10},{9,11},{10,... | collective-permute-start | bytes 196616 | tf_op jit(solution)/shard_map/ppermute | solution.py:628
  97.8 7.0 %collective-permute-start.8 = (bf16[1,128,128]{2,1,0:T(8,128)(2,1)S(1)}, bf16[1,128,128]{2,1,0:T(8,128)(2,1)S(1)}, u32[]{:S(2)}, u32[]{:S(2)}) collective-permute-start(bf16[1,128,128]{2,1,0:T(8,128)(2,1)S(1)} %slice.7), channel_id=1, source_target_pairs={{0,7},{1,6},{2,5},{3,4},{4,3},{5,2},{6,1},{7,0},{8,15},{9,14},{10,... | collective-permute-start | bytes 98312 | tf_op jit(solution)/shard_map/ppermute | solution.py:628
